TPU v7x, 512 devices: a whole 4x8x8 slice. The times are simulated.
512 devices in a mesh: leaf: 128 (over y, z, core), panel: 4 (over x).
Axes of the slice: x: 4, y: 8, z: 8, core: 2. Of those that a mesh axis runs over, the one named last changes fastest.
Arguments:
- leaf_rhs: bfloat16 [4, 128, 2, 128, 128], P('panel', 'leaf'), may hold values from -6 to 6
- leaf_inverse: bfloat16 [4, 128, 2, 128, 128], P('panel', 'leaf'), may hold values from -4 to 4, as said below
- leaf_panel: bfloat16 [4, 128, 2, 6, 128, 128], P('panel', 'leaf'), may hold values from -0.25 to 0.25
- panel_rows: int32 [4, 128, 2, 6], P('panel', 'leaf'), may hold values from 0 to 23, all different within a row
- live_count: int32 [4, 128], P('panel', 'leaf'), may hold values from 1 to 2, 192 in all within a row
- sep1_rhs: bfloat16 [4, 128, 128, 128], P('panel', 'leaf'), may hold values from -6 to 6
- sep1_inverse: bfloat16 [4, 128, 1024, 128], P('panel', 'leaf'), may hold values from -4 to 4, as said below
- sep1_panel: bfloat16 [4, 128, 2048, 128], P('panel', 'leaf'), may hold values from -0.125 to 0.125
- sep2_rhs: bfloat16 [4, 128, 128, 128], P('panel', 'leaf'), may hold values from -6 to 6
- sep2_inverse: bfloat16 [4, 128, 2048, 128], P('panel', 'leaf'), may hold values from -4 to 4, as said below
Outputs:
- leaf_sample: bfloat16 [4, 128, 2, 128, 128], P('panel', 'leaf')
- sep1_sample: bfloat16 [4, 128, 128, 128], P('panel', 'leaf')
- sep2_sample: bfloat16 [4, 128, 128, 128], P('panel', 'leaf')
Inputs may be any that keep to these rules, and one draw needn't show every extreme that they name: `panel_rows`: the 6 row block indices of one slot differ. `live_count`: slots at or beyond the count hold no supernode. `leaf_inverse`: zero above the diagonal of each 128 by 128 block. `sep1_inverse`: zero above the diagonal of the assembled separator block. `sep2_inverse`: zero above the diagonal of the assembled separator block.
All inputs are finite; a program needn't handle non-finite values. No bound on the sum of `live_count` on one device may be relied on, other than what follows from the above.
Results may differ from a plain program's by a relative error of at most 0.024.
Values may be sent and summed in bfloat16 or wider, within the bound.
No kernel may reach another device: no remote copies, remote signals or barrier semaphores. Data moves between devices by JAX's collectives and lax.ppermute only.
A program may use at most 64 MiB of HBM per device.

v0:
```python
import jax
import jax.numpy as jnp
from jax import lax
from jax.sharding import PartitionSpec as P


def partner(x, axis, apart):
    return lax.ppermute(x, axis, [(i, i ^ 1 << apart) for i in range(lax.axis_size(axis))])


def halve_sum(stacked, levels, leaf_place):
    for bit_index in reversed(range(levels)):
        paired = stacked.reshape((2, stacked.shape[0] // 2) + stacked.shape[1:])
        my_bit = leaf_place >> bit_index & 1
        kept_half = lax.dynamic_index_in_dim(paired, my_bit, 0, keepdims=False)
        other_half = lax.dynamic_index_in_dim(paired, 1 - my_bit, 0, keepdims=False)
        stacked = kept_half + partner(other_half.astype(jnp.bfloat16), "leaf", bit_index).astype(
            other_half.dtype
        )
    return stacked


def double_cat(stacked, levels, leaf_place):
    for bit_index in range(levels):
        received = partner(stacked, "leaf", bit_index)
        upper_side = leaf_place >> bit_index & 1 == 1
        lower_half = jnp.where(upper_side, received, stacked)
        upper_half = jnp.where(upper_side, stacked, received)
        stacked = jnp.concatenate([lower_half, upper_half], 0)
    return stacked


def full_vector(vector_piece, levels, leaf_place):
    stacked = vector_piece[None, None]
    stacked = lax.all_gather(stacked, "panel", axis=1, tiled=True)
    stacked = double_cat(stacked, levels, leaf_place)
    return stacked.reshape(-1, vector_piece.shape[-1])


def contract_rows(matrix, vectors):
    return lax.dot_general(
        matrix, vectors, (((0,), (0,)), ((), ())), preferred_element_type=jnp.float32
    )


def body(
    leaf_rhs,
    leaf_inverse,
    leaf_panel,
    panel_rows,
    live_count,
    sep1_rhs,
    sep1_inverse,
    sep1_panel,
    sep2_rhs,
    sep2_inverse,
):
    right_side = leaf_rhs[0, 0]
    inverse = leaf_inverse[0, 0]
    panels = leaf_panel[0, 0]
    row_blocks = panel_rows[0, 0]
    live_total = live_count[0, 0]
    slot_total, block_width = (inverse.shape[0], inverse.shape[1])
    samples = right_side.shape[-1]
    panel_total = lax.axis_size("panel")
    blocks = 6 * panel_total
    leaf_place = lax.axis_index("leaf")
    live_mask = (jnp.arange(slot_total, dtype=jnp.int32) < live_total).astype(jnp.float32)
    leaf_solved = jnp.einsum(
        "sab,sbn->san", inverse, right_side, preferred_element_type=jnp.float32
    )
    leaf_solved = (leaf_solved * live_mask[:, None, None]).astype(jnp.bfloat16)
    products = jnp.einsum("skab,sbn->skan", panels, leaf_solved, preferred_element_type=jnp.float32)
    leaf_terms = (
        jnp.zeros((blocks, block_width, samples), jnp.float32)
        .at[row_blocks.reshape(-1)]
        .add(products.reshape(-1, block_width, samples))
    )
    summed = lax.psum_scatter(
        leaf_terms.reshape(6, panel_total, block_width, samples).astype(jnp.bfloat16),
        "panel",
        scatter_dimension=1,
        tiled=True,
    ).astype(jnp.float32)
    own_first = halve_sum(summed[:2], 1, leaf_place)[0, 0]
    first_side = (sep1_rhs[0, 0].astype(jnp.float32) - own_first).astype(jnp.bfloat16)
    partial_value = jnp.dot(sep1_inverse[0, 0], first_side, preferred_element_type=jnp.float32)
    reduced = lax.psum_scatter(
        partial_value.reshape(2, panel_total, block_width, samples).astype(jnp.bfloat16),
        "panel",
        scatter_dimension=1,
        tiled=True,
    ).astype(jnp.float32)
    solved1 = halve_sum(reduced, 1, leaf_place)[0, 0].astype(jnp.bfloat16)
    upper_part = jnp.dot(sep1_panel[0, 0], solved1, preferred_element_type=jnp.float32)
    raised = lax.psum_scatter(
        upper_part.reshape(4, panel_total, block_width, samples).astype(jnp.bfloat16),
        "panel",
        scatter_dimension=1,
        tiled=True,
    ).astype(jnp.float32)
    own_second = halve_sum(summed[2:] + raised, 2, leaf_place)[0, 0]
    second_side = (sep2_rhs[0, 0].astype(jnp.float32) - own_second).astype(jnp.bfloat16)
    partial_value = jnp.dot(sep2_inverse[0, 0], second_side, preferred_element_type=jnp.float32)
    reduced = lax.psum_scatter(
        partial_value.reshape(4, panel_total, block_width, samples).astype(jnp.bfloat16),
        "panel",
        scatter_dimension=1,
        tiled=True,
    ).astype(jnp.float32)
    solved2 = halve_sum(reduced, 2, leaf_place)[0, 0].astype(jnp.bfloat16)
    whole_solved = full_vector(solved2, 2, leaf_place)
    sample2 = contract_rows(sep2_inverse[0, 0], whole_solved).astype(jnp.bfloat16)
    whole_second = full_vector(sample2, 2, leaf_place)
    correction = contract_rows(sep1_panel[0, 0], whole_second)
    shifted1 = (solved1.astype(jnp.float32) - correction).astype(jnp.bfloat16)
    whole_shifted = full_vector(shifted1, 1, leaf_place)
    sample1 = contract_rows(sep1_inverse[0, 0], whole_shifted).astype(jnp.bfloat16)
    whole_first = full_vector(sample1, 1, leaf_place)
    ancestors = jnp.concatenate([whole_first, whole_second], 0).reshape(
        blocks, block_width, samples
    )
    picked = ancestors[row_blocks]
    correction_all = jnp.einsum(
        "skab,skan->sbn", panels, picked, preferred_element_type=jnp.float32
    )
    leaf_shifted = (leaf_solved.astype(jnp.float32) - correction_all).astype(jnp.bfloat16)
    leaf_sample = jnp.einsum(
        "sab,san->sbn", inverse, leaf_shifted, preferred_element_type=jnp.float32
    )
    leaf_sample = (leaf_sample * live_mask[:, None, None]).astype(jnp.bfloat16)
    return (leaf_sample[None, None], sample1[None, None], sample2[None, None])


def solution(mesh):
    return jax.shard_map(
        body,
        mesh=mesh,
        in_specs=(
            P("panel", "leaf", None, None, None),
            P("panel", "leaf", None, None, None),
            P("panel", "leaf", None, None, None, None),
            P("panel", "leaf", None, None),
            P("panel", "leaf"),
            P("panel", "leaf", None, None),
            P("panel", "leaf", None, None),
            P("panel", "leaf", None, None),
            P("panel", "leaf", None, None),
            P("panel", "leaf", None, None),
        ),
        out_specs=(
            P("panel", "leaf", None, None, None),
            P("panel", "leaf", None, None),
            P("panel", "leaf", None, None),
        ),
        check_vma=False,
    )
```

profile of v0, /device:TPU:1, one launch (start us, length us, event | category | flops | bytes accessed | tf_op | source)
XLA Modules:
  0.0 334.5 jit_solution(9237844854299450858)
XLA Ops:
  9.7 1.3 fusion.14
  11.5 1.4 scatter_fusion
  12.9 1.1 convert_element_type.185
  14.0 1.3 dynamic-slice.20
  15.3 57.6 %all-reduce.7.cloned.1.call-done = bf16[6,4,128,128]{3,2,1,0:T(8,128)(2,1)} async-done(((bf16[6,4,128,128]{3,2,1,0:T(8,128)(2,1)}), bf16[6,4,128,128]{3,2,1,0:T(8,128)(2,1)}) %all-reduce.7.cloned.1.call-update) | async-done | bytes 786448
  72.9 1.7 dynamic-slice_convert_fusion
  74.6 4.4 %collective-permute-start = (bf16[1,1,128,128]{3,2,1,0:T(8,128)(2,1)S(1)}, bf16[1,1,128,128]{3,2,1,0:T(8,128)(2,1)S(1)}, u32[]{:S(2)}, u32[]{:S(2)}) collective-permute-start(bf16[1,1,128,128]{3,2,1,0:T(8,128)(2,1)S(1)} %dynamic-slice_convert_fusion.7), channel_id=1, source_target_pairs={{0,4},{4,0},{8,12},{12,8},{16,20},{20,16},{24,28},{28,24},{32,36},... | collective-permute-start | bytes 98312 | tf_op jit(solution)/shard_map/ppermute | solution.py:8
  81.1 50.9 %all-reduce.9.cloned.1.call-done = bf16[2,4,128,128]{2,3,1,0:T(8,128)(2,1)} async-done(((bf16[2,4,128,128]{2,3,1,0:T(8,128)(2,1)}), bf16[2,4,128,128]{2,3,1,0:T(8,128)(2,1)}) %all-reduce.9.cloned.1.call-update) | async-done | bytes 262160
  132.0 1.5 dynamic-slice_convert_fusion.3
  133.5 4.7 %collective-permute-start.1 = (bf16[1,1,128,128]{2,3,1,0:T(8,128)(2,1)S(1)}, bf16[1,1,128,128]{2,3,1,0:T(8,128)(2,1)S(1)}, u32[]{:S(2)}, u32[]{:S(2)}) collective-permute-start(bf16[1,1,128,128]{2,3,1,0:T(8,128)(2,1)S(1)} %dynamic-slice_convert_fusion.6), channel_id=1, source_target_pairs={{0,4},{4,0},{8,12},{12,8},{16,20},{20,16},{24,28},{28,24},{32,36},... | collective-permute-start | bytes 98312 | tf_op jit(solution)/shard_map/ppermute | solution.py:8
  140.5 51.8 %all-reduce.11.cloned.1.call-done = bf16[4,4,128,128]{3,2,1,0:T(8,128)(2,1)} async-done(((bf16[4,4,128,128]{3,2,1,0:T(8,128)(2,1)}), bf16[4,4,128,128]{3,2,1,0:T(8,128)(2,1)}) %all-reduce.11.cloned.1.call-update) | async-done | bytes 524304
  192.3 1.6 slice_add_fusion
  193.9 3.4 %collective-permute-start.2 = (bf16[2,1,128,128]{3,2,1,0:T(8,128)(2,1)S(1)}, bf16[2,1,128,128]{3,2,1,0:T(8,128)(2,1)S(1)}, u32[]{:S(2)}, u32[]{:S(2)}) collective-permute-start(bf16[2,1,128,128]{3,2,1,0:T(8,128)(2,1)S(1)} %fusion.19), channel_id=1, source_target_pairs={{0,8},{4,12},{8,0},{12,4},{16,24},{20,28},{24,16},{28,20},{32,40},... | collective-permute-start | bytes 196616 | tf_op jit(solution)/shard_map/ppermute | solution.py:8
  197.3 1.6 collective-permute-done.2
  199.0 5.8 %collective-permute-start.3 = (bf16[1,1,128,128]{3,2,1,0:T(8,128)(2,1)S(1)}, bf16[1,1,128,128]{3,2,1,0:T(8,128)(2,1)S(1)}, u32[]{:S(2)}, u32[]{:S(2)}) collective-permute-start(bf16[1,1,128,128]{3,2,1,0:T(8,128)(2,1)S(1)} %dynamic-slice_convert_fusion.5), channel_id=1, source_target_pairs={{0,4},{4,0},{8,12},{12,8},{16,20},{20,16},{24,28},{28,24},{32,36},... | collective-permute-start | bytes 98312 | tf_op jit(solution)/shard_map/ppermute | solution.py:8
  206.4 1.2 copy.49
  207.7 25.6 %reduce-scatter.11.cloned.1.call-done = bf16[4,1,128,128]{3,2,0,1:T(8,128)(2,1)} async-done(((bf16[4,4,128,128]{3,2,0,1:T(8,128)(2,1)}), bf16[4,1,128,128]{3,2,0,1:T(8,128)(2,1)}) %reduce-scatter.11.cloned.1.call-update) | async-done | bytes 131088 | tf_op jit(solution)/shard_map/reduce_scatter | solution.py:105
  234.2 3.3 collective-permute-start.4
  237.5 1.7 collective-permute-done.4
  239.3 5.4 %collective-permute-start.5 = (bf16[1,1,128,128]{3,2,0,1:T(8,128)(2,1)S(1)}, bf16[1,1,128,128]{3,2,0,1:T(8,128)(2,1)S(1)}, u32[]{:S(2)}, u32[]{:S(2)}) collective-permute-start(bf16[1,1,128,128]{3,2,0,1:T(8,128)(2,1)S(1)} %dynamic-slice_convert_fusion.4), channel_id=1, source_target_pairs={{0,4},{4,0},{8,12},{12,8},{16,20},{20,16},{24,28},{28,24},{32,36},... | collective-permute-start | bytes 98312 | tf_op jit(solution)/shard_map/ppermute | solution.py:8
  245.5 9.1 %all_gather.12 = bf16[1,4,128,128]{3,2,0,1:T(8,128)(2,1)S(1)} all-gather(bf16[1,1,128,128]{3,2,0,1:T(8,128)(2,1)S(1)} %add_convert_fusion), channel_id=1, replica_groups=mesh['leaf'=128,'panel'=4] {'panel'}, dimensions={1}, use_global_device_ids=true | all-gather | bytes 163840 | tf_op jit(solution)/shard_map/all_gather | solution.py:35
  254.6 5.1 %collective-permute-start.6 = (bf16[1,4,128,128]{3,2,1,0:T(8,128)(2,1)S(1)}, bf16[1,4,128,128]{3,2,1,0:T(8,128)(2,1)S(1)}, u32[]{:S(2)}, u32[]{:S(2)}) collective-permute-start(bf16[1,4,128,128]{3,2,1,0:T(8,128)(2,1)S(1)} %bitcast.155), channel_id=1, source_target_pairs={{0,4},{4,0},{8,12},{12,8},{16,20},{20,16},{24,28},{28,24},{32,36},... | collective-permute-start | bytes 393224 | tf_op jit(solution)/shard_map/ppermute | solution.py:8
  260.8 3.3 collective-permute-start.7
  264.1 6.1 %collective-permute-done.7 = bf16[2,4,128,128]{3,2,1,0:T(8,128)(2,1)S(1)} collective-permute-done((bf16[2,4,128,128]{3,2,1,0:T(8,128)(2,1)S(1)}, bf16[2,4,128,128]{3,2,1,0:T(8,128)(2,1)S(1)}, u32[]{:S(2)}, u32[]{:S(2)}) %collective-permute-start.7) | collective-permute-done | bytes 262176 | tf_op jit(solution)/shard_map/ppermute | solution.py:8
  270.7 8.4 %all-gather = bf16[512,128]{0,1:T(8,128)(2,1)S(1)} all-gather(bf16[128,128]{0,1:T(8,128)(2,1)S(1)} %bitcast.162), channel_id=2, replica_groups=mesh['leaf'=128,'panel'=4] {'panel'}, dimensions={0}, use_global_device_ids=true | all-gather | bytes 163840 | tf_op jit(solution)/shard_map/all_gather | solution.py:35
  279.2 5.4 %collective-permute-start.8 = (bf16[1,4,128,128]{3,2,1,0:T(8,128)(2,1)S(1)}, bf16[1,4,128,128]{3,2,1,0:T(8,128)(2,1)S(1)}, u32[]{:S(2)}, u32[]{:S(2)}) collective-permute-start(bf16[1,4,128,128]{3,2,1,0:T(8,128)(2,1)S(1)} %bitcast.158), channel_id=1, source_target_pairs={{0,4},{4,0},{8,12},{12,8},{16,20},{20,16},{24,28},{28,24},{32,36},... | collective-permute-start | bytes 393224 | tf_op jit(solution)/shard_map/ppermute | solution.py:8
  285.6 3.3 collective-permute-start.9
  288.9 6.1 %collective-permute-done.9 = bf16[2,4,128,128]{3,2,1,0:T(8,128)(2,1)S(1)} collective-permute-done((bf16[2,4,128,128]{3,2,1,0:T(8,128)(2,1)S(1)}, bf16[2,4,128,128]{3,2,1,0:T(8,128)(2,1)S(1)}, u32[]{:S(2)}, u32[]{:S(2)}) %collective-permute-start.9) | collective-permute-done | bytes 262176 | tf_op jit(solution)/shard_map/ppermute | solution.py:8
  295.5 8.4 %all-gather.1 = bf16[512,128]{0,1:T(8,128)(2,1)S(1)} all-gather(bf16[128,128]{0,1:T(8,128)(2,1)S(1)} %subtract_convert_fusion), channel_id=3, replica_groups=mesh['leaf'=128,'panel'=4] {'panel'}, dimensions={0}, use_global_device_ids=true | all-gather | bytes 163840 | tf_op jit(solution)/shard_map/all_gather | solution.py:35
  304.0 5.7 %collective-permute-start.10 = (bf16[1,4,128,128]{3,2,1,0:T(8,128)(2,1)S(1)}, bf16[1,4,128,128]{3,2,1,0:T(8,128)(2,1)S(1)}, u32[]{:S(2)}, u32[]{:S(2)}) collective-permute-start(bf16[1,4,128,128]{3,2,1,0:T(8,128)(2,1)S(1)} %bitcast.160), channel_id=1, source_target_pairs={{0,4},{4,0},{8,12},{12,8},{16,20},{20,16},{24,28},{28,24},{32,36},... | collective-permute-start | bytes 393224 | tf_op jit(solution)/shard_map/ppermute | solution.py:8
  311.0 8.4 %all-gather.2 = bf16[512,128]{0,1:T(8,128)(2,1)S(1)} all-gather(bf16[128,128]{0,1:T(8,128)(2,1)S(1)} %bitcast.164), channel_id=4, replica_groups=mesh['leaf'=128,'panel'=4] {'panel'}, dimensions={0}, use_global_device_ids=true | all-gather | bytes 163840 | tf_op jit(solution)/shard_map/all_gather | solution.py:35
  319.5 4.6 %collective-permute-start.11 = (bf16[1,4,128,128]{3,2,1,0:T(8,128)(2,1)S(1)}, bf16[1,4,128,128]{3,2,1,0:T(8,128)(2,1)S(1)}, u32[]{:S(2)}, u32[]{:S(2)}) collective-permute-start(bf16[1,4,128,128]{3,2,1,0:T(8,128)(2,1)S(1)} %bitcast.156), channel_id=1, source_target_pairs={{0,4},{4,0},{8,12},{12,8},{16,20},{20,16},{24,28},{28,24},{32,36},... | collective-permute-start | bytes 393224 | tf_op jit(solution)/shard_map/ppermute | solution.py:8
  (84 shorter events, 18.4 us)
Async XLA Ops:
  7.2 198.5 %copy-start = (bf16[1,1,2048,128]{3,2,1,0:T(8,128)(2,1)S(1)}, bf16[1,1,2048,128]{3,2,1,0:T(8,128)(2,1)}, u32[]{:S(2)}) copy-start(bf16[1,1,2048,128]{3,2,1,0:T(8,128)(2,1)} %param.19) | copy-start | bytes 1572868
  7.2 65.7 %all-reduce.7.cloned.1.call-start = ((), (), s32[]{:S(2)}) async-start(), calls=%async_computation.2 | async-start | bytes 1572864
  12.9 66.9 %copy-start.3 = (bf16[1,1,1024,128]{3,2,1,0:T(8,128)(2,1)S(1)}, bf16[1,1,1024,128]{3,2,1,0:T(8,128)(2,1)}, u32[]{:S(2)}) copy-start(bf16[1,1,1024,128]{3,2,1,0:T(8,128)(2,1)} %param.16) | copy-start | bytes 786436
  12.9 66.9 %copy-start.5 = (bf16[1,1,128,128]{3,2,1,0:T(8,128)(2,1)S(1)}, bf16[1,1,128,128]{3,2,1,0:T(8,128)(2,1)}, u32[]{:S(2)}) copy-start(bf16[1,1,128,128]{3,2,1,0:T(8,128)(2,1)} %param.15) | copy-start | bytes 98308
  14.0 118.0 %all-reduce.9.cloned.1.call-start = ((), (), s32[]{:S(2)}) async-start(), calls=%async_computation.3 | async-start | bytes 524288
  72.9 66.2 %copy-start.1 = (bf16[1,1,2048,128]{3,2,1,0:T(8,128)(2,1)S(1)}, bf16[1,1,2048,128]{3,2,1,0:T(8,128)(2,1)}, u32[]{:S(2)}) copy-start(bf16[1,1,2048,128]{3,2,1,0:T(8,128)(2,1)} %param.17) | copy-start | bytes 1572868
  74.6 5.2 %collective-permute-start = (bf16[1,1,128,128]{3,2,1,0:T(8,128)(2,1)S(1)}, bf16[1,1,128,128]{3,2,1,0:T(8,128)(2,1)S(1)}, u32[]{:S(2)}, u32[]{:S(2)}) collective-permute-start(bf16[1,1,128,128]{3,2,1,0:T(8,128)(2,1)S(1)} %dynamic-slice_convert_fusion.7), channel_id=1, source_target_pairs={{0,4},{4,0},{8,12},{12,8},{16,20},{20,16},{24,28},{28,24},{32,36},... | collective-permute-start | bytes 98312 | tf_op jit(solution)/shard_map/ppermute | solution.py:8
  81.0 111.3 %all-reduce.11.cloned.1.call-start = ((), (), s32[]{:S(2)}) async-start(), calls=%async_computation.4 | async-start | bytes 1048576
  133.5 5.6 %collective-permute-start.1 = (bf16[1,1,128,128]{2,3,1,0:T(8,128)(2,1)S(1)}, bf16[1,1,128,128]{2,3,1,0:T(8,128)(2,1)S(1)}, u32[]{:S(2)}, u32[]{:S(2)}) collective-permute-start(bf16[1,1,128,128]{2,3,1,0:T(8,128)(2,1)S(1)} %dynamic-slice_convert_fusion.6), channel_id=1, source_target_pairs={{0,4},{4,0},{8,12},{12,8},{16,20},{20,16},{24,28},{28,24},{32,36},... | collective-permute-start | bytes 98312 | tf_op jit(solution)/shard_map/ppermute | solution.py:8
  139.4 66.3 %copy-start.6 = (bf16[1,1,128,128]{3,2,1,0:T(8,128)(2,1)S(1)}, bf16[1,1,128,128]{3,2,1,0:T(8,128)(2,1)}, u32[]{:S(2)}) copy-start(bf16[1,1,128,128]{3,2,1,0:T(8,128)(2,1)} %param.18) | copy-start | bytes 98308
  140.4 92.8 %reduce-scatter.11.cloned.1.call-start = ((), (), s32[]{:S(2)}) async-start(), calls=%async_computation.1 | async-start | bytes 655360 | tf_op jit(solution)/shard_map/reduce_scatter | solution.py:105
  193.9 5.1 %collective-permute-start.2 = (bf16[2,1,128,128]{3,2,1,0:T(8,128)(2,1)S(1)}, bf16[2,1,128,128]{3,2,1,0:T(8,128)(2,1)S(1)}, u32[]{:S(2)}, u32[]{:S(2)}) collective-permute-start(bf16[2,1,128,128]{3,2,1,0:T(8,128)(2,1)S(1)} %fusion.19), channel_id=1, source_target_pairs={{0,8},{4,12},{8,0},{12,4},{16,24},{20,28},{24,16},{28,20},{32,40},... | collective-permute-start | bytes 196616 | tf_op jit(solution)/shard_map/ppermute | solution.py:8
  199.0 6.7 %collective-permute-start.3 = (bf16[1,1,128,128]{3,2,1,0:T(8,128)(2,1)S(1)}, bf16[1,1,128,128]{3,2,1,0:T(8,128)(2,1)S(1)}, u32[]{:S(2)}, u32[]{:S(2)}) collective-permute-start(bf16[1,1,128,128]{3,2,1,0:T(8,128)(2,1)S(1)} %dynamic-slice_convert_fusion.5), channel_id=1, source_target_pairs={{0,4},{4,0},{8,12},{12,8},{16,20},{20,16},{24,28},{28,24},{32,36},... | collective-permute-start | bytes 98312 | tf_op jit(solution)/shard_map/ppermute | solution.py:8
  234.2 5.0 %collective-permute-start.4 = (bf16[2,1,128,128]{3,2,0,1:T(8,128)(2,1)S(1)}, bf16[2,1,128,128]{3,2,0,1:T(8,128)(2,1)S(1)}, u32[]{:S(2)}, u32[]{:S(2)}) collective-permute-start(bf16[2,1,128,128]{3,2,0,1:T(8,128)(2,1)S(1)} %fusion.20), channel_id=1, source_target_pairs={{0,8},{4,12},{8,0},{12,4},{16,24},{20,28},{24,16},{28,20},{32,40},... | collective-permute-start | bytes 196616 | tf_op jit(solution)/shard_map/ppermute | solution.py:8
  239.3 6.2 %collective-permute-start.5 = (bf16[1,1,128,128]{3,2,0,1:T(8,128)(2,1)S(1)}, bf16[1,1,128,128]{3,2,0,1:T(8,128)(2,1)S(1)}, u32[]{:S(2)}, u32[]{:S(2)}) collective-permute-start(bf16[1,1,128,128]{3,2,0,1:T(8,128)(2,1)S(1)} %dynamic-slice_convert_fusion.4), channel_id=1, source_target_pairs={{0,4},{4,0},{8,12},{12,8},{16,20},{20,16},{24,28},{28,24},{32,36},... | collective-permute-start | bytes 98312 | tf_op jit(solution)/shard_map/ppermute | solution.py:8
  254.6 6.1 %collective-permute-start.6 = (bf16[1,4,128,128]{3,2,1,0:T(8,128)(2,1)S(1)}, bf16[1,4,128,128]{3,2,1,0:T(8,128)(2,1)S(1)}, u32[]{:S(2)}, u32[]{:S(2)}) collective-permute-start(bf16[1,4,128,128]{3,2,1,0:T(8,128)(2,1)S(1)} %bitcast.155), channel_id=1, source_target_pairs={{0,4},{4,0},{8,12},{12,8},{16,20},{20,16},{24,28},{28,24},{32,36},... | collective-permute-start | bytes 393224 | tf_op jit(solution)/shard_map/ppermute | solution.py:8
  260.8 9.4 %collective-permute-start.7 = (bf16[2,4,128,128]{3,2,1,0:T(8,128)(2,1)S(1)}, bf16[2,4,128,128]{3,2,1,0:T(8,128)(2,1)S(1)}, u32[]{:S(2)}, u32[]{:S(2)}) collective-permute-start(bf16[2,4,128,128]{3,2,1,0:T(8,128)(2,1)S(1)} %pad_maximum_fusion.3), channel_id=1, source_target_pairs={{0,8},{4,12},{8,0},{12,4},{16,24},{20,28},{24,16},{28,20},{32,40},... | collective-permute-start | bytes 786440 | tf_op jit(solution)/shard_map/ppermute | solution.py:8
  279.2 6.4 %collective-permute-start.8 = (bf16[1,4,128,128]{3,2,1,0:T(8,128)(2,1)S(1)}, bf16[1,4,128,128]{3,2,1,0:T(8,128)(2,1)S(1)}, u32[]{:S(2)}, u32[]{:S(2)}) collective-permute-start(bf16[1,4,128,128]{3,2,1,0:T(8,128)(2,1)S(1)} %bitcast.158), channel_id=1, source_target_pairs={{0,4},{4,0},{8,12},{12,8},{16,20},{20,16},{24,28},{28,24},{32,36},... | collective-permute-start | bytes 393224 | tf_op jit(solution)/shard_map/ppermute | solution.py:8
  285.6 9.4 %collective-permute-start.9 = (bf16[2,4,128,128]{3,2,1,0:T(8,128)(2,1)S(1)}, bf16[2,4,128,128]{3,2,1,0:T(8,128)(2,1)S(1)}, u32[]{:S(2)}, u32[]{:S(2)}) collective-permute-start(bf16[2,4,128,128]{3,2,1,0:T(8,128)(2,1)S(1)} %pad_maximum_fusion.4), channel_id=1, source_target_pairs={{0,8},{4,12},{8,0},{12,4},{16,24},{20,28},{24,16},{28,20},{32,40},... | collective-permute-start | bytes 786440 | tf_op jit(solution)/shard_map/ppermute | solution.py:8
  295.1 29.0 %copy-start.7 = (s32[1,1,2,6]{3,2,1,0:T(2,128)S(1)}, s32[1,1,2,6]{3,2,1,0:T(2,128)}, u32[]{:S(2)}) copy-start(s32[1,1,2,6]{3,2,1,0:T(2,128)} %param.13) | copy-start | bytes 148
  304.0 6.7 %collective-permute-start.10 = (bf16[1,4,128,128]{3,2,1,0:T(8,128)(2,1)S(1)}, bf16[1,4,128,128]{3,2,1,0:T(8,128)(2,1)S(1)}, u32[]{:S(2)}, u32[]{:S(2)}) collective-permute-start(bf16[1,4,128,128]{3,2,1,0:T(8,128)(2,1)S(1)} %bitcast.160), channel_id=1, source_target_pairs={{0,4},{4,0},{8,12},{12,8},{16,20},{20,16},{24,28},{28,24},{32,36},... | collective-permute-start | bytes 393224 | tf_op jit(solution)/shard_map/ppermute | solution.py:8
  319.5 6.2 %collective-permute-start.11 = (bf16[1,4,128,128]{3,2,1,0:T(8,128)(2,1)S(1)}, bf16[1,4,128,128]{3,2,1,0:T(8,128)(2,1)S(1)}, u32[]{:S(2)}, u32[]{:S(2)}) collective-permute-start(bf16[1,4,128,128]{3,2,1,0:T(8,128)(2,1)S(1)} %bitcast.156), channel_id=1, source_target_pairs={{0,4},{4,0},{8,12},{12,8},{16,20},{20,16},{24,28},{28,24},{32,36},... | collective-permute-start | bytes 393224 | tf_op jit(solution)/shard_map/ppermute | solution.py:8
  325.7 1.0 copy-start.2
  325.7 1.0 copy-start.4
Sparse Core Ops, SparseCore 0:
  14.1 58.7 all-reduce.6
  81.1 50.8 all-reduce.8
  140.6 51.7 all-reduce.10
  207.8 25.4 reduce-scatter.10
where the time goes:
time: 335 us; the launch traced here: 334 us
  waiting for transfers between devices  208 us (62%)
  starting transfers between devices  54.5 us (16%)
  blocking collectives  34.2 us (10%)
  between operations  14.9 us (4%)
  local copies, waits for them, and re-layouts  9.66 us (3%)
  other arithmetic  8.61 us (3%)
  matrix products  4.66 us (1%)
    unnamed x7, waiting for transfers between devices  160 us
    ppermute x12, starting transfers between devices, partner(): lax.ppermute(x, axis, [(i, i ^ 1 << apart) for i in range(lax.axis_size(a...  54.4 us
    all_gather x4, blocking collectives, full_vector(): stacked = lax.all_gather(stacked, 'panel', axis=1, tiled=True)  34.2 us
    reduce_scatter x1, waiting for transfers between devices, body(): lax.psum_scatter(partial_value.reshape(4, panel_total, block_width, sampl...  25.6 us
    ppermute x12, waiting for transfers between devices, partner(): lax.ppermute(x, axis, [(i, i ^ 1 << apart) for i in range(lax.axis_size(a...  21.9 us
  transfers between devices with their start and end apart: 16, of which 15 were waited for; matrix products, arithmetic and copies ran while one was open for 1% of the time, Pallas kernels for 0%

commit v1 on v0

v1 whole, which is shorter than its diff:
```python
import jax
import jax.numpy as jnp
from jax import lax
from jax.sharding import Mesh, PartitionSpec as P

FIRST = ("core", "panel")
SECOND = ("pair", "core", "panel")


def owned_sum(partials, axes):
    received = lax.all_to_all(partials, axes, 0, 0, tiled=True)
    return received.astype(jnp.float32).sum(axis=0)


def spread(piece, axes):
    size = 1
    for name in axes:
        size = size * lax.axis_size(name)
    copies = jnp.broadcast_to(piece[None], (size,) + piece.shape)
    return lax.all_to_all(copies, axes, 0, 0, tiled=True)


def gather(piece, axes):
    return lax.all_gather(piece[None], axes, axis=0, tiled=True)


def apply_columns(columns, piece, width):
    product = jnp.dot(columns, piece, preferred_element_type=jnp.float32)
    return product.reshape(-1, width, piece.shape[-1])


def contract_rows(matrix, vectors):
    vectors = vectors.reshape(-1, vectors.shape[-1])
    return lax.dot_general(
        matrix, vectors, (((0,), (0,)), ((), ())), preferred_element_type=jnp.float32
    )


def body(
    leaf_rhs,
    leaf_inverse,
    leaf_panel,
    panel_rows,
    live_count,
    sep1_rhs,
    sep1_inverse,
    sep1_panel,
    sep2_rhs,
    sep2_inverse,
):
    right_side = leaf_rhs[0, 0]
    inverse = leaf_inverse[0, 0]
    panels = leaf_panel[0, 0]
    row_blocks = panel_rows[0, 0]
    slots, width = inverse.shape[0], inverse.shape[1]
    samples = right_side.shape[-1]
    first_blocks = sep1_inverse.shape[2] // width
    second_blocks = sep2_inverse.shape[2] // width
    live = (jnp.arange(slots, dtype=jnp.int32) < live_count[0, 0]).astype(jnp.float32)

    leaf_solved = jnp.einsum(
        "sab,sbn->san", inverse, right_side, preferred_element_type=jnp.float32
    )
    leaf_solved = (leaf_solved * live[:, None, None]).astype(jnp.bfloat16)
    products = jnp.einsum("skab,sbn->skan", panels, leaf_solved, preferred_element_type=jnp.float32)
    leaf_terms = (
        jnp.zeros((first_blocks + second_blocks, width, samples), jnp.float32)
        .at[row_blocks.reshape(-1)]
        .add(products.reshape(-1, width, samples))
    )

    own_first = owned_sum(leaf_terms[:first_blocks].astype(jnp.bfloat16), FIRST)
    first_side = (sep1_rhs[0, 0].astype(jnp.float32) - own_first).astype(jnp.bfloat16)
    partial1 = apply_columns(sep1_inverse[0, 0], first_side, width)
    solved1 = owned_sum(partial1.astype(jnp.bfloat16), FIRST).astype(jnp.bfloat16)

    raised = apply_columns(sep1_panel[0, 0], solved1, width)
    own_second = owned_sum((leaf_terms[first_blocks:] + raised).astype(jnp.bfloat16), SECOND)
    second_side = (sep2_rhs[0, 0].astype(jnp.float32) - own_second).astype(jnp.bfloat16)
    partial2 = apply_columns(sep2_inverse[0, 0], second_side, width)
    solved2 = owned_sum(partial2.astype(jnp.bfloat16), SECOND).astype(jnp.bfloat16)

    whole_solved = gather(solved2, SECOND)
    sample2 = contract_rows(sep2_inverse[0, 0], whole_solved).astype(jnp.bfloat16)
    whole_second = spread(sample2, SECOND)
    correction = contract_rows(sep1_panel[0, 0], whole_second)
    shifted1 = (solved1.astype(jnp.float32) - correction).astype(jnp.bfloat16)
    whole_shifted = gather(shifted1, FIRST)
    sample1 = contract_rows(sep1_inverse[0, 0], whole_shifted).astype(jnp.bfloat16)
    whole_first = spread(sample1, FIRST)

    ancestors = jnp.concatenate([whole_first, whole_second], 0)
    picked = ancestors[row_blocks]
    correction_all = jnp.einsum("skab,skan->sbn", panels, picked, preferred_element_type=jnp.float32)
    leaf_shifted = (leaf_solved.astype(jnp.float32) - correction_all).astype(jnp.bfloat16)
    leaf_sample = jnp.einsum(
        "sab,san->sbn", inverse, leaf_shifted, preferred_element_type=jnp.float32
    )
    leaf_sample = (leaf_sample * live[:, None, None]).astype(jnp.bfloat16)
    return (leaf_sample[None, None], sample1[None, None], sample2[None, None])


def solution(mesh):
    places = mesh.devices.reshape(-1, 2, 2, mesh.shape["panel"])
    fine = Mesh(places, ("group", "pair", "core", "panel"))
    leaf = ("group", "pair", "core")

    def spec(rank):
        return P("panel", leaf, *(None,) * (rank - 2))

    return jax.shard_map(
        body,
        mesh=fine,
        in_specs=tuple(spec(rank) for rank in (5, 5, 6, 4, 2, 4, 4, 4, 4, 4)),
        out_specs=tuple(spec(rank) for rank in (5, 4, 4)),
        check_vma=False,
    )
```

time: 335 us -> 141 us (0.42)
  waiting for transfers between devices: 208 us -> 4.26 us
  blocking collectives: 34.2 us -> 117 us
  starting transfers between devices: 54.5 us -> 3.49 us
  between operations: 14.9 us -> 1.64 us
  other arithmetic: 8.61 us -> 1.83 us
  local copies, waits for them, and re-layouts: 9.66 us -> 6.27 us
    unnamed x7 -> x0, waiting for transfers between devices: 160 us -> none
    all_to_all x0 -> x5, blocking collectives: none -> 68.4 us  [the longest x4 52.7 us: owned_sum(): received = lax.all_to_all(partials, axes, 0, 0, tiled=True)]
    ppermute x12 -> x0, starting transfers between devices: 54.4 us -> none  [partner(): lax.ppermute(x, axis, [(i, i ^ 1 << apart) for i in range(lax.axis_size(a...]
    reduce_scatter x1 -> x0, waiting for transfers between devices: 25.6 us -> none  [body(): lax.psum_scatter(partial_value.reshape(4, panel_total, block_width, sampl...]
    ppermute x12 -> x0, waiting for transfers between devices: 21.9 us -> none  [partner(): lax.ppermute(x, axis, [(i, i ^ 1 << apart) for i in range(lax.axis_size(a...]
    all_gather x4 -> x2, blocking collectives: 34.2 us -> 48.8 us  [gather(): return lax.all_gather(piece[None], axes, axis=0, tiled=True)]
    all_to_all x0 -> x1, waiting for transfers between devices: none -> 4.26 us  [spread(): return lax.all_to_all(copies, axes, 0, 0, tiled=True)]
    convert_element_type x6 -> x2, other arithmetic: 4.24 us -> 0.13 us  [the longest x1 0.12 us: body(): (leaf_terms[first_blocks:] + raised).astype(jnp.bfloat16)]
  transfers between devices with their start and end apart: 16 -> 1, of which waited for: 15 -> 1; matrix products, arithmetic and copies ran while one was open for 1% -> 1% of each run, Pallas kernels for 0% -> 0%
where the time goes in v1:
time: 141 us; the launch traced here: 140 us
  blocking collectives  117 us (83%)
  local copies, waits for them, and re-layouts  6.27 us (4%)
  matrix products  5.55 us (4%)
  waiting for transfers between devices  4.26 us (3%)
  starting transfers between devices  3.49 us (2%)
  other arithmetic  1.83 us (1%)
  between operations  1.64 us (1%)
    all_to_all x4, blocking collectives, owned_sum(): received = lax.all_to_all(partials, axes, 0, 0, tiled=True)  52.7 us
    all_gather x2, blocking collectives, gather(): return lax.all_gather(piece[None], axes, axis=0, tiled=True)  48.8 us
    all_to_all x1, blocking collectives, spread(): return lax.all_to_all(copies, axes, 0, 0, tiled=True)  15.7 us
    all_to_all x1, waiting for transfers between devices, spread(): return lax.all_to_all(copies, axes, 0, 0, tiled=True)  4.26 us
    all_to_all x1, starting transfers between devices, spread(): return lax.all_to_all(copies, axes, 0, 0, tiled=True)  3.49 us
  transfers between devices with their start and end apart: 1, of which 1 were waited for; matrix products, arithmetic and copies ran while one was open for 1% of the time, Pallas kernels for 0%

profile of v1, /device:TPU:1, one launch (start us, length us, event | category | flops | bytes accessed | tf_op | source)
XLA Modules:
  0.0 140.2 jit_solution(8754897437891004119)
XLA Ops:
  1.4 1.0 fusion.4
  2.4 1.3 fusion.16
  3.7 0.3 copy.44
  4.1 0.2 broadcast_in_dim.16
  4.3 1.4 scatter_fusion
  5.7 16.0 %all_to_all.30 = bf16[8,128,128]{2,1,0:T(8,128)(2,1)S(1)} all-to-all(bf16[8,128,128]{2,1,0:T(8,128)(2,1)S(1)} %slice.17), channel_id=1, replica_groups=mesh['group'=32,'pair'=2,'core'=2,'panel'=4] {'core','panel'}, dimensions={0} | all-to-all | bytes 524288 | tf_op jit(solution)/shard_map/all_to_all | solution.py:11
  21.8 0.2 fusion.1
  22.1 9.8 %all_to_all.31 = bf16[8,128,128]{1,2,0:T(8,128)(2,1)S(1)} all-to-all(bf16[8,128,128]{1,2,0:T(8,128)(2,1)S(1)} %bitcast.118), channel_id=1, replica_groups=mesh['group'=32,'pair'=2,'core'=2,'panel'=4] {'core','panel'}, dimensions={0} | all-to-all | bytes 524288 | tf_op jit(solution)/shard_map/all_to_all | solution.py:11
  31.9 1.3 convolution_bitcast_fusion
  33.2 1.5 %copy.64 = f32[2048,128]{1,0:T(8,128)S(1)} copy(f32[2048,128]{0,1:T(8,128)} %convolution_bitcast_fusion) | data formatting | bytes 2097152 | tf_op jit(solution)/shard_map/reshape | solution.py:29
  34.8 0.1 fusion.9
  34.9 13.4 %all_to_all.32 = bf16[16,128,128]{2,1,0:T(8,128)(2,1)S(1)} all-to-all(bf16[16,128,128]{2,1,0:T(8,128)(2,1)S(1)} %fusion.9), channel_id=1, replica_groups=mesh['group'=32,'pair'=2,'core'=2,'panel'=4] {'pair','core','panel'}, dimensions={0} | all-to-all | bytes 1048576 | tf_op jit(solution)/shard_map/all_to_all | solution.py:11
  48.4 0.3 fusion
  48.8 0.1 copy.72
  48.9 13.5 %all_to_all.33 = bf16[16,128,128]{1,2,0:T(8,128)(2,1)S(1)} all-to-all(bf16[16,128,128]{1,2,0:T(8,128)(2,1)S(1)} %bitcast.116), channel_id=1, replica_groups=mesh['group'=32,'pair'=2,'core'=2,'panel'=4] {'pair','core','panel'}, dimensions={0} | all-to-all | bytes 1048576 | tf_op jit(solution)/shard_map/all_to_all | solution.py:11
  62.5 27.6 %all-gather = bf16[2048,128]{0,1:T(8,128)(2,1)S(1)} all-gather(bf16[128,128]{0,1:T(8,128)(2,1)S(1)} %reduce_sum.51), channel_id=2, replica_groups=mesh['group'=32,'pair'=2,'core'=2,'panel'=4] {'pair','core','panel'}, dimensions={0}, use_global_device_ids=true | all-gather | bytes 557056 | tf_op jit(solution)/shard_map/all_gather | solution.py:24
  90.1 0.3 convolution_convert_fusion.2
  90.4 0.1 copy.50
  90.5 0.1 broadcast_in_dim.36
  90.6 15.7 %all_to_all.34 = bf16[16,128,128]{2,1,0:T(8,128)(2,1)S(1)} all-to-all(bf16[16,128,128]{2,1,0:T(8,128)(2,1)S(1)} %broadcast_in_dim.36), channel_id=1, replica_groups=mesh['group'=32,'pair'=2,'core'=2,'panel'=4] {'pair','core','panel'}, dimensions={0} | all-to-all | bytes 1048576 | tf_op jit(solution)/shard_map/all_to_all | solution.py:20
  106.3 0.3 fusion.8
  106.6 21.2 %all-gather.1 = bf16[1024,128]{0,1:T(8,128)(2,1)S(1)} all-gather(bf16[128,128]{0,1:T(8,128)(2,1)S(1)} %fusion.8), channel_id=3, replica_groups=mesh['group'=32,'pair'=2,'core'=2,'panel'=4] {'core','panel'}, dimensions={0}, use_global_device_ids=true | all-gather | bytes 294912 | tf_op jit(solution)/shard_map/all_gather | solution.py:24
  127.9 0.2 convolution_convert_fusion.3
  128.1 0.1 copy.51
  128.2 0.7 broadcast_in_dim.38
  128.9 3.5 %all-to-all-start.5 = ((bf16[8,128,128]{2,1,0:T(8,128)(2,1)}), bf16[8,128,128]{2,1,0:T(8,128)(2,1)S(1)}, u32[]{:S(2)}, u32[]{:S(2)}) async-start(bf16[8,128,128]{2,1,0:T(8,128)(2,1)} %broadcast_in_dim.38), calls=%async_computation.5 | async-start | bytes 524288 | tf_op jit(solution)/shard_map/all_to_all | solution.py:20
  132.5 0.7 copy.57
  133.3 0.7 copy.56
  134.0 4.3 %all-to-all-done.5 = bf16[8,128,128]{2,1,0:T(8,128)(2,1)S(1)} async-done(((bf16[8,128,128]{2,1,0:T(8,128)(2,1)}), bf16[8,128,128]{2,1,0:T(8,128)(2,1)S(1)}, u32[]{:S(2)}, u32[]{:S(2)}) %all-to-all-start.5) | async-done | bytes 262176 | tf_op jit(solution)/shard_map/all_to_all | solution.py:20
  138.3 0.6 gather_fusion
  139.0 0.5 fusion.6
  139.5 0.7 copy.55
  (31 shorter events, 0.6 us)
Async XLA Ops:
  0.6 47.8 %copy-start = (bf16[1,1,2048,128]{3,2,1,0:T(8,128)(2,1)S(1)}, bf16[1,1,2048,128]{3,2,1,0:T(8,128)(2,1)}, u32[]{:S(2)}) copy-start(bf16[1,1,2048,128]{3,2,1,0:T(8,128)(2,1)} %param.19) | copy-start | bytes 1572868
  0.6 3.4 %copy-start.8 = (s32[1,1,2,6]{3,2,1,0:T(2,128)S(1)}, s32[1,1,2,6]{3,2,1,0:T(2,128)}, u32[]{:S(2)}) copy-start(s32[1,1,2,6]{3,2,1,0:T(2,128)} %param.13) | copy-start | bytes 148
  4.3 17.5 %copy-start.4 = (bf16[1,1,1024,128]{3,2,1,0:T(8,128)(2,1)S(1)}, bf16[1,1,1024,128]{3,2,1,0:T(8,128)(2,1)}, u32[]{:S(2)}) copy-start(bf16[1,1,1024,128]{3,2,1,0:T(8,128)(2,1)} %param.16) | copy-start | bytes 786436
  4.3 17.5 %copy-start.6 = (bf16[1,1,128,128]{3,2,1,0:T(8,128)(2,1)S(1)}, bf16[1,1,128,128]{3,2,1,0:T(8,128)(2,1)}, u32[]{:S(2)}) copy-start(bf16[1,1,128,128]{3,2,1,0:T(8,128)(2,1)} %param.15) | copy-start | bytes 98308
  5.7 26.2 %copy-start.1 = (bf16[1,1,2048,128]{3,2,1,0:T(8,128)(2,1)S(1)}, bf16[1,1,2048,128]{3,2,1,0:T(8,128)(2,1)}, u32[]{:S(2)}) copy-start(bf16[1,1,2048,128]{3,2,1,0:T(8,128)(2,1)} %param.17) | copy-start | bytes 1572868
  34.8 13.7 %copy-start.7 = (bf16[1,1,128,128]{3,2,1,0:T(8,128)(2,1)S(1)}, bf16[1,1,128,128]{3,2,1,0:T(8,128)(2,1)}, u32[]{:S(2)}) copy-start(bf16[1,1,128,128]{3,2,1,0:T(8,128)(2,1)} %param.18) | copy-start | bytes 98308
  62.5 43.8 %copy-start.2 = (bf16[1,1,2048,128]{3,2,1,0:T(8,128)(2,1)S(1)}, bf16[1,1,2048,128]{3,2,1,0:T(8,128)(2,1)}, u32[]{:S(2)}) copy-start(bf16[1,1,2048,128]{3,2,1,0:T(8,128)(2,1)} %param.17) | copy-start | bytes 1572868
  128.9 10.0 %copy-start.3 = (bf16[1,1,2,6,128,128]{5,4,3,2,1,0:T(8,128)(2,1)S(1)}, bf16[1,1,2,6,128,128]{5,4,3,2,1,0:T(8,128)(2,1)}, u32[]{:S(2)}) copy-start(bf16[1,1,2,6,128,128]{5,4,3,2,1,0:T(8,128)(2,1)} %param.12) | copy-start | bytes 1179652
  128.9 10.0 %copy-start.5 = (bf16[1,1,2,128,128]{4,3,2,1,0:T(8,128)(2,1)S(1)}, bf16[1,1,2,128,128]{4,3,2,1,0:T(8,128)(2,1)}, u32[]{:S(2)}) copy-start(bf16[1,1,2,128,128]{4,3,2,1,0:T(8,128)(2,1)} %param.11) | copy-start | bytes 196612
  128.9 9.3 %all-to-all-start.5 = ((bf16[8,128,128]{2,1,0:T(8,128)(2,1)}), bf16[8,128,128]{2,1,0:T(8,128)(2,1)S(1)}, u32[]{:S(2)}, u32[]{:S(2)}) async-start(bf16[8,128,128]{2,1,0:T(8,128)(2,1)} %broadcast_in_dim.38), calls=%async_computation.5 | async-start | bytes 524288 | tf_op jit(solution)/shard_map/all_to_all | solution.py:20

commit v2 on v1

v2 whole, which is shorter than its diff:
```python
import jax
import jax.numpy as jnp
from jax import lax
from jax.experimental import pallas as pl
from jax.experimental.pallas import tpu as pltpu
from jax.sharding import Mesh, PartitionSpec as P

FIRST = ("core", "panel")
SECOND = ("pair", "core", "panel")
CHIPS = ("pair", "panel")


def block_dot(left, right):
    return lax.dot_general(
        left, right, (((left.ndim - 1,), (0,)), ((), ())), preferred_element_type=jnp.float32
    )


def leaf_forward_kernel(rows, count, rhs, inverse, panels, solved, first, second, total):
    slots, touched, width, samples = panels.shape[0], panels.shape[1], rhs.shape[1], rhs.shape[2]
    total[...] = jnp.zeros_like(total)
    for s in range(slots):
        live = jnp.where(s < count[0, 0], 1.0, 0.0)
        piece = (block_dot(inverse[s], rhs[s]) * live).astype(jnp.bfloat16)
        solved[s] = piece
        products = block_dot(panels[s].reshape(touched * width, width), piece)
        products = products.reshape(touched, width, samples)
        for k in range(touched):
            total[rows[s, k]] += products[k]
    split = first.shape[0]
    first[...] = total[:split].astype(jnp.bfloat16)
    second[...] = total[split:]


def leaf_forward(rows, count, rhs, inverse, panels, first_blocks, second_blocks):
    width, samples = rhs.shape[1:]
    smem = pl.BlockSpec(memory_space=pltpu.SMEM)
    vmem = pl.BlockSpec(memory_space=pltpu.VMEM)
    return pl.pallas_call(
        leaf_forward_kernel,
        out_shape=(
            jax.ShapeDtypeStruct(rhs.shape, jnp.bfloat16),
            jax.ShapeDtypeStruct((first_blocks, width, samples), jnp.bfloat16),
            jax.ShapeDtypeStruct((second_blocks, width, samples), jnp.float32),
        ),
        in_specs=[smem, smem, vmem, vmem, vmem],
        out_specs=(vmem, vmem, vmem),
        scratch_shapes=[pltpu.VMEM((first_blocks + second_blocks, width, samples), jnp.float32)],
        compiler_params=pltpu.CompilerParams(vmem_limit_bytes=16 << 20),
        name="leaf_forward",
    )(rows, count, rhs, inverse, panels)


def side_kernel(received, rhs, columns, partials):
    side = rhs[...].astype(jnp.float32) - received[...].astype(jnp.float32).sum(axis=0)
    product = block_dot(columns[...], side.astype(jnp.bfloat16))
    partials[...] = product.reshape(partials.shape).astype(jnp.bfloat16)


def side_partials(received, rhs, columns):
    vmem = pl.BlockSpec(memory_space=pltpu.VMEM)
    return pl.pallas_call(
        side_kernel,
        out_shape=jax.ShapeDtypeStruct(received.shape, jnp.bfloat16),
        in_specs=[vmem] * 3,
        out_specs=vmem,
        compiler_params=pltpu.CompilerParams(vmem_limit_bytes=16 << 20),
        name="side_partials",
    )(received, rhs, columns)


def raise_kernel(received, terms, columns, solved, raised):
    piece = received[...].astype(jnp.float32).sum(axis=0).astype(jnp.bfloat16)
    solved[...] = piece
    product = block_dot(columns[...], piece).reshape(raised.shape)
    raised[...] = (product + terms[...]).astype(jnp.bfloat16)


def raise_terms(received, terms, columns):
    vmem = pl.BlockSpec(memory_space=pltpu.VMEM)
    return pl.pallas_call(
        raise_kernel,
        out_shape=(
            jax.ShapeDtypeStruct(received.shape[1:], jnp.bfloat16),
            jax.ShapeDtypeStruct(terms.shape, jnp.bfloat16),
        ),
        in_specs=[vmem] * 3,
        out_specs=(vmem, vmem),
        compiler_params=pltpu.CompilerParams(vmem_limit_bytes=16 << 20),
        name="raise_terms",
    )(received, terms, columns)


def leaf_backward_kernel(rows, count, first, second, panels, inverse, solved, sample, above):
    slots, touched, width = panels.shape[0], panels.shape[1], panels.shape[2]
    split = first.shape[0]
    above[:split] = first[...]
    above[split:] = second[...]
    contract = (((0,), (0,)), ((), ()))
    for s in range(slots):
        picked = jnp.concatenate([above[rows[s, k]] for k in range(touched)], axis=0)
        correction = lax.dot_general(
            panels[s].reshape(touched * width, width),
            picked,
            contract,
            preferred_element_type=jnp.float32,
        )
        shifted = (solved[s].astype(jnp.float32) - correction).astype(jnp.bfloat16)
        result = lax.dot_general(inverse[s], shifted, contract, preferred_element_type=jnp.float32)
        live = jnp.where(s < count[0, 0], 1.0, 0.0)
        sample[s] = (result * live).astype(jnp.bfloat16)


def leaf_backward(rows, count, first, second, panels, inverse, solved):
    smem = pl.BlockSpec(memory_space=pltpu.SMEM)
    vmem = pl.BlockSpec(memory_space=pltpu.VMEM)
    blocks = first.shape[0] + second.shape[0]
    return pl.pallas_call(
        leaf_backward_kernel,
        out_shape=jax.ShapeDtypeStruct(solved.shape, jnp.bfloat16),
        in_specs=[smem, smem] + [vmem] * 5,
        out_specs=vmem,
        scratch_shapes=[pltpu.VMEM((blocks,) + first.shape[1:], jnp.bfloat16)],
        compiler_params=pltpu.CompilerParams(vmem_limit_bytes=16 << 20),
        name="leaf_backward",
    )(rows, count, first, second, panels, inverse, solved)


def exchange(blocks, axes):
    return lax.all_to_all(blocks, axes, 0, 0, tiled=True)


def by_core(blocks, axis):
    other = lax.ppermute(blocks, "core", [(0, 1), (1, 0)])
    upper = lax.axis_index("core") == 1
    lower_part = jnp.where(upper, other, blocks)
    upper_part = jnp.where(upper, blocks, other)
    return jnp.stack([lower_part, upper_part], axis)


def copies(blocks, axes):
    size = 1
    for name in axes:
        size = size * lax.axis_size(name)
    return jnp.broadcast_to(blocks[None], (size,) + blocks.shape)


def spread_pairs(piece, axes):
    both = by_core(piece, 0)
    received = exchange(copies(both, axes), axes)
    panels = lax.axis_size("panel")
    received = received.reshape((-1, panels) + both.shape)
    return jnp.swapaxes(received, 1, 2).reshape((-1,) + piece.shape)


def spread_then_pair(piece, axes):
    received = exchange(copies(piece, axes), axes)
    panels = lax.axis_size("panel")
    received = received.reshape((-1, panels) + piece.shape)
    return by_core(received, 1).reshape((-1,) + piece.shape)


def contract_rows(matrix, vectors):
    vectors = vectors.reshape(-1, vectors.shape[-1])
    return lax.dot_general(
        matrix, vectors, (((0,), (0,)), ((), ())), preferred_element_type=jnp.float32
    )


def body(
    leaf_rhs,
    leaf_inverse,
    leaf_panel,
    panel_rows,
    live_count,
    sep1_rhs,
    sep1_inverse,
    sep1_panel,
    sep2_rhs,
    sep2_inverse,
):
    inverse, panels, row_blocks = leaf_inverse[0, 0], leaf_panel[0, 0], panel_rows[0, 0]
    width = inverse.shape[1]
    first_blocks = sep1_inverse.shape[2] // width
    second_blocks = sep2_inverse.shape[2] // width
    columns1, columns2, raising = sep1_inverse[0, 0], sep2_inverse[0, 0], sep1_panel[0, 0]

    leaf_solved, first_terms, second_terms = leaf_forward(
        row_blocks, live_count, leaf_rhs[0, 0], inverse, panels, first_blocks, second_blocks
    )
    partial1 = side_partials(exchange(first_terms, FIRST), sep1_rhs[0, 0], columns1)
    solved1, raised = raise_terms(exchange(partial1, FIRST), second_terms, raising)
    partial2 = side_partials(exchange(raised, SECOND), sep2_rhs[0, 0], columns2)
    received = exchange(partial2, SECOND)
    solved2 = received.astype(jnp.float32).sum(axis=0).astype(jnp.bfloat16)

    whole_solved = spread_pairs(solved2, CHIPS)
    sample2 = contract_rows(columns2, whole_solved).astype(jnp.bfloat16)
    whole_second = spread_then_pair(sample2, CHIPS)
    correction = contract_rows(raising, whole_second)
    shifted1 = (solved1.astype(jnp.float32) - correction).astype(jnp.bfloat16)
    whole_shifted = spread_pairs(shifted1, ("panel",))
    sample1 = contract_rows(columns1, whole_shifted).astype(jnp.bfloat16)
    whole_first = spread_then_pair(sample1, ("panel",))

    leaf_sample = leaf_backward(
        row_blocks, live_count, whole_first, whole_second, panels, inverse, leaf_solved
    )
    return (leaf_sample[None, None], sample1[None, None], sample2[None, None])


def solution(mesh):
    places = mesh.devices.reshape(-1, 2, 2, mesh.shape["panel"])
    fine = Mesh(places, ("group", "pair", "core", "panel"))
    leaf = ("group", "pair", "core")

    def spec(rank):
        return P("panel", leaf, *(None,) * (rank - 2))

    return jax.shard_map(
        body,
        mesh=fine,
        in_specs=tuple(spec(rank) for rank in (5, 5, 6, 4, 2, 4, 4, 4, 4, 4)),
        out_specs=tuple(spec(rank) for rank in (5, 4, 4)),
        check_vma=False,
    )
```

time: 141 us -> 119 us (0.84)
  blocking collectives: 117 us -> 89.6 us
  starting transfers between devices: 3.49 us -> 13.3 us
  matrix products: 5.55 us -> 0.95 us
  Pallas kernels: 0 us -> 3.75 us
  other arithmetic: 1.83 us -> 0.25 us
  waiting for transfers between devices: 4.26 us -> 2.81 us
    all_gather x2 -> x0, blocking collectives: 48.8 us -> none  [gather(): return lax.all_gather(piece[None], axes, axis=0, tiled=True)]
    all_to_all x5 -> x8, blocking collectives: 68.4 us -> 89.6 us  [exchange(): return lax.all_to_all(blocks, axes, 0, 0, tiled=True)]
    ppermute x0 -> x4, starting transfers between devices: none -> 13.3 us  [by_core(): other = lax.ppermute(blocks, 'core', [(0, 1), (1, 0)])]
    dot_general x6 -> x0, matrix products: 4.7 us -> none  [the longest x3 1.86 us: apply_columns(): product = jnp.dot(columns, piece, preferred_element_type=jnp.float32)]
    all_to_all x1 -> x0, waiting for transfers between devices: 4.26 us -> none  [spread(): return lax.all_to_all(copies, axes, 0, 0, tiled=True)]
    pallas_call x0 -> x5, Pallas kernels: none -> 3.75 us  [the longest x1 1.79 us: leaf_backward(): pl.pallas_call(leaf_backward_kernel, out_shape=jax.ShapeDtypeStruct(solve...]
    unnamed x21 -> x24, local copies, waits for them, and re-layouts: 2.24 us -> 5.77 us
    all_to_all x1 -> x0, starting transfers between devices: 3.49 us -> none  [spread(): return lax.all_to_all(copies, axes, 0, 0, tiled=True)]
  transfers between devices with their start and end apart: 1 -> 4, of which waited for: 1 -> 3; matrix products, arithmetic and copies ran while one was open for 1% -> 1% of each run, Pallas kernels for 0% -> 0%
where the time goes in v2:
time: 119 us
  blocking collectives  89.6 us (75%)
  starting transfers between devices  13.3 us (11%)
  local copies, waits for them, and re-layouts  6.25 us (5%)
  Pallas kernels  3.75 us (3%)
  waiting for transfers between devices  2.81 us (2%)
  between operations  1.53 us (1%)
    all_to_all x8, blocking collectives, exchange(): return lax.all_to_all(blocks, axes, 0, 0, tiled=True)  89.6 us
    ppermute x4, starting transfers between devices, by_core(): other = lax.ppermute(blocks, 'core', [(0, 1), (1, 0)])  13.3 us
    unnamed x24, local copies, waits for them, and re-layouts  5.77 us
    ppermute x4, waiting for transfers between devices, by_core(): other = lax.ppermute(blocks, 'core', [(0, 1), (1, 0)])  2.81 us
  transfers between devices with their start and end apart: 4, of which 3 were waited for; matrix products, arithmetic and copies ran while one was open for 1% of the time, Pallas kernels for 0%

profile of v2, /device:TPU:1, one launch (start us, length us, event | category | flops | bytes accessed | tf_op | source)
XLA Modules:
  0.0 118.5 jit_solution(5040805813611766169)
XLA Ops:
  1.3 0.7 copy-done.10
  2.0 1.0 copy-done.2
  3.0 0.8 copy-done.5
  3.8 0.8 copy-done.7
  4.6 1.1 leaf_forward.1
  5.8 16.0 %all_to_all.40.received = bf16[8,128,128]{2,1,0:T(8,128)(2,1)S(1)} all-to-all(bf16[8,128,128]{2,1,0:T(8,128)(2,1)S(1)} %get-tuple-element.8), channel_id=1, replica_groups=mesh['group'=32,'pair'=2,'core'=2,'panel'=4] {'core','panel'}, dimensions={0} | all-to-all | bytes 524288 | tf_op jit(solution)/shard_map/all_to_all | solution.py:130
  21.7 0.2 side_partials.2
  22.0 9.8 %all_to_all.41.received = bf16[8,128,128]{2,1,0:T(8,128)(2,1)S(1)} all-to-all(bf16[8,128,128]{2,1,0:T(8,128)(2,1)S(1)} %side_partials.2), channel_id=1, replica_groups=mesh['group'=32,'pair'=2,'core'=2,'panel'=4] {'core','panel'}, dimensions={0} | all-to-all | bytes 524288 | tf_op jit(solution)/shard_map/all_to_all | solution.py:130
  31.7 0.3 raise_terms.1
  32.1 13.6 %all_to_all.42.received = bf16[16,128,128]{2,1,0:T(8,128)(2,1)S(1)} all-to-all(bf16[16,128,128]{2,1,0:T(8,128)(2,1)S(1)} %get-tuple-element.11), channel_id=1, replica_groups=mesh['group'=32,'pair'=2,'core'=2,'panel'=4] {'pair','core','panel'}, dimensions={0} | all-to-all | bytes 1048576 | tf_op jit(solution)/shard_map/all_to_all | solution.py:130
  45.7 0.3 side_partials.3
  46.0 13.5 %all_to_all.43 = bf16[16,128,128]{2,1,0:T(8,128)(2,1)S(1)} all-to-all(bf16[16,128,128]{2,1,0:T(8,128)(2,1)S(1)} %side_partials.3), channel_id=1, replica_groups=mesh['group'=32,'pair'=2,'core'=2,'panel'=4] {'pair','core','panel'}, dimensions={0} | all-to-all | bytes 1048576 | tf_op jit(solution)/shard_map/all_to_all | solution.py:130
  59.6 2.5 %collective-permute-start = (bf16[128,128]{1,0:T(8,128)(2,1)S(1)}, bf16[128,128]{1,0:T(8,128)(2,1)S(1)}, u32[]{:S(2)}, u32[]{:S(2)}) collective-permute-start(bf16[128,128]{1,0:T(8,128)(2,1)S(1)} %reduce_sum.12), channel_id=1, source_target_pairs={{0,4},{4,0},{1,5},{5,1},{2,6},{6,2},{3,7},{7,3},{8,12},{12,8},{9,1... | collective-permute-start | bytes 98312 | tf_op jit(solution)/shard_map/ppermute | solution.py:134
  62.1 0.8 collective-permute-done
  63.0 11.3 %all_to_all.44 = bf16[8,2,128,128]{3,2,1,0:T(8,128)(2,1)S(1)} all-to-all(bf16[8,2,128,128]{3,2,1,0:T(8,128)(2,1)S(1)} %broadcast_in_dim.14), channel_id=1, replica_groups=mesh['group'=32,'pair'=2,'core'=2,'panel'=4] {'pair','panel'}, dimensions={0} | all-to-all | bytes 1048576 | tf_op jit(solution)/shard_map/all_to_all | solution.py:130
  74.3 0.3 convolution_convert_fusion
  74.7 0.1 copy.33
  74.9 9.5 %all_to_all.45 = bf16[8,128,128]{2,1,0:T(8,128)(2,1)S(1)} all-to-all(bf16[8,128,128]{2,1,0:T(8,128)(2,1)S(1)} %broadcast_in_dim.15), channel_id=1, replica_groups=mesh['group'=32,'pair'=2,'core'=2,'panel'=4] {'pair','panel'}, dimensions={0} | all-to-all | bytes 524288 | tf_op jit(solution)/shard_map/all_to_all | solution.py:130
  84.4 4.4 %collective-permute-start.1 = (bf16[2,4,128,128]{3,2,1,0:T(8,128)(2,1)S(1)}, bf16[2,4,128,128]{3,2,1,0:T(8,128)(2,1)S(1)}, u32[]{:S(2)}, u32[]{:S(2)}) collective-permute-start(bf16[2,4,128,128]{3,2,1,0:T(8,128)(2,1)S(1)} %bitcast.83), channel_id=1, source_target_pairs={{0,4},{4,0},{1,5},{5,1},{2,6},{6,2},{3,7},{7,3},{8,12},{12,8},{9,1... | collective-permute-start | bytes 786440 | tf_op jit(solution)/shard_map/ppermute | solution.py:134
  88.7 1.1 collective-permute-done.1
  90.0 0.3 fusion.1
  90.3 2.3 %collective-permute-start.2 = (bf16[128,128]{1,0:T(8,128)(2,1)S(1)}, bf16[128,128]{1,0:T(8,128)(2,1)S(1)}, u32[]{:S(2)}, u32[]{:S(2)}) collective-permute-start(bf16[128,128]{1,0:T(8,128)(2,1)S(1)} %fusion.1), channel_id=1, source_target_pairs={{0,4},{4,0},{1,5},{5,1},{2,6},{6,2},{3,7},{7,3},{8,12},{12,8},{9,1... | collective-permute-start | bytes 98312 | tf_op jit(solution)/shard_map/ppermute | solution.py:134
  92.6 0.8 collective-permute-done.2
  93.5 8.8 %all_to_all.46 = bf16[4,2,128,128]{3,2,1,0:T(8,128)(2,1)S(1)} all-to-all(bf16[4,2,128,128]{3,2,1,0:T(8,128)(2,1)S(1)} %broadcast_in_dim.16), channel_id=1, replica_groups=mesh['group'=32,'pair'=2,'core'=2,'panel'=4] {'panel'}, dimensions={0} | all-to-all | bytes 524288 | tf_op jit(solution)/shard_map/all_to_all | solution.py:130
  102.4 0.3 convolution_convert_fusion.1
  102.7 0.1 copy.37
  102.8 7.2 %all_to_all.47 = bf16[4,128,128]{2,1,0:T(8,128)(2,1)S(1)} all-to-all(bf16[4,128,128]{2,1,0:T(8,128)(2,1)S(1)} %broadcast_in_dim.17), channel_id=1, replica_groups=mesh['group'=32,'pair'=2,'core'=2,'panel'=4] {'panel'}, dimensions={0} | all-to-all | bytes 262144 | tf_op jit(solution)/shard_map/all_to_all | solution.py:130
  110.0 4.2 %collective-permute-start.3 = (bf16[1,4,128,128]{3,2,1,0:T(8,128)(2,1)S(1)}, bf16[1,4,128,128]{3,2,1,0:T(8,128)(2,1)S(1)}, u32[]{:S(2)}, u32[]{:S(2)}) collective-permute-start(bf16[1,4,128,128]{3,2,1,0:T(8,128)(2,1)S(1)} %bitcast.85), channel_id=1, source_target_pairs={{0,4},{4,0},{1,5},{5,1},{2,6},{6,2},{3,7},{7,3},{8,12},{12,8},{9,1... | collective-permute-start | bytes 393224 | tf_op jit(solution)/shard_map/ppermute | solution.py:134
  114.2 0.7 copy.39
  115.0 0.7 copy.38
  115.8 0.9 copy-done.3
  116.7 1.8 %leaf_backward.1 = bf16[2,128,128]{2,1,0:T(8,128)(2,1)} custom-call(s32[2,6]{1,0:T(2,128)S(1)} %bitcast.79, s32[1,1]{1,0:T(1,128)S(6)} %copy.41.count, bf16[8,128,128]{2,1,0:T(8,128)(2,1)S(1)} %bitcast.72, bf16[16,128,128]{2,1,0:T(8,128)(2,1)S(1)} %bitcast.66, bf16[2,6,128,128]{3,2,1,0:T(8,128)(2,1)S(1)} %bitcast.70, bf16[2,128,128]{2,1,0:T(8,128)(2,1)S(1)} %bitcast.74, ...), custom_call_target="tpu_custom_call" | custom-call | tf_op jit(solution)/shard_map/leaf_backward/pallas_call | solution.py:118
  (33 shorter events, 0.6 us)
Async XLA Ops:
  1.3 0.7 copy-start.10
  2.0 1.0 copy-start.2
  3.0 0.8 copy-start.5
  3.8 0.8 copy-start.7
  5.7 16.0 %copy-start.4 = (bf16[1,1,1024,128]{3,2,1,0:T(8,128)(2,1)S(1)}, bf16[1,1,1024,128]{3,2,1,0:T(8,128)(2,1)}, u32[]{:S(2)}) copy-start(bf16[1,1,1024,128]{3,2,1,0:T(8,128)(2,1)} %param.16) | copy-start | bytes 786436
  5.7 16.0 %copy-start.8 = (bf16[1,1,128,128]{3,2,1,0:T(8,128)(2,1)S(1)}, bf16[1,1,128,128]{3,2,1,0:T(8,128)(2,1)}, u32[]{:S(2)}) copy-start(bf16[1,1,128,128]{3,2,1,0:T(8,128)(2,1)} %param.15) | copy-start | bytes 98308
  21.7 10.0 %copy-start.1 = (bf16[1,1,2048,128]{3,2,1,0:T(8,128)(2,1)S(1)}, bf16[1,1,2048,128]{3,2,1,0:T(8,128)(2,1)}, u32[]{:S(2)}) copy-start(bf16[1,1,2048,128]{3,2,1,0:T(8,128)(2,1)} %param.17) | copy-start | bytes 1572868
  32.0 13.6 %copy-start = (bf16[1,1,2048,128]{3,2,1,0:T(8,128)(2,1)S(1)}, bf16[1,1,2048,128]{3,2,1,0:T(8,128)(2,1)}, u32[]{:S(2)}) copy-start(bf16[1,1,2048,128]{3,2,1,0:T(8,128)(2,1)} %param.19) | copy-start | bytes 1572868
  32.1 13.6 %copy-start.9 = (bf16[1,1,128,128]{3,2,1,0:T(8,128)(2,1)S(1)}, bf16[1,1,128,128]{3,2,1,0:T(8,128)(2,1)}, u32[]{:S(2)}) copy-start(bf16[1,1,128,128]{3,2,1,0:T(8,128)(2,1)} %param.18) | copy-start | bytes 98308
  59.6 3.3 %collective-permute-start = (bf16[128,128]{1,0:T(8,128)(2,1)S(1)}, bf16[128,128]{1,0:T(8,128)(2,1)S(1)}, u32[]{:S(2)}, u32[]{:S(2)}) collective-permute-start(bf16[128,128]{1,0:T(8,128)(2,1)S(1)} %reduce_sum.12), channel_id=1, source_target_pairs={{0,4},{4,0},{1,5},{5,1},{2,6},{6,2},{3,7},{7,3},{8,12},{12,8},{9,1... | collective-permute-start | bytes 98312 | tf_op jit(solution)/shard_map/ppermute | solution.py:134
  84.4 5.5 %collective-permute-start.1 = (bf16[2,4,128,128]{3,2,1,0:T(8,128)(2,1)S(1)}, bf16[2,4,128,128]{3,2,1,0:T(8,128)(2,1)S(1)}, u32[]{:S(2)}, u32[]{:S(2)}) collective-permute-start(bf16[2,4,128,128]{3,2,1,0:T(8,128)(2,1)S(1)} %bitcast.83), channel_id=1, source_target_pairs={{0,4},{4,0},{1,5},{5,1},{2,6},{6,2},{3,7},{7,3},{8,12},{12,8},{9,1... | collective-permute-start | bytes 786440 | tf_op jit(solution)/shard_map/ppermute | solution.py:134
  90.3 3.1 %collective-permute-start.2 = (bf16[128,128]{1,0:T(8,128)(2,1)S(1)}, bf16[128,128]{1,0:T(8,128)(2,1)S(1)}, u32[]{:S(2)}, u32[]{:S(2)}) collective-permute-start(bf16[128,128]{1,0:T(8,128)(2,1)S(1)} %fusion.1), channel_id=1, source_target_pairs={{0,4},{4,0},{1,5},{5,1},{2,6},{6,2},{3,7},{7,3},{8,12},{12,8},{9,1... | collective-permute-start | bytes 98312 | tf_op jit(solution)/shard_map/ppermute | solution.py:134
  110.0 5.7 %collective-permute-start.3 = (bf16[1,4,128,128]{3,2,1,0:T(8,128)(2,1)S(1)}, bf16[1,4,128,128]{3,2,1,0:T(8,128)(2,1)S(1)}, u32[]{:S(2)}, u32[]{:S(2)}) collective-permute-start(bf16[1,4,128,128]{3,2,1,0:T(8,128)(2,1)S(1)} %bitcast.85), channel_id=1, source_target_pairs={{0,4},{4,0},{1,5},{5,1},{2,6},{6,2},{3,7},{7,3},{8,12},{12,8},{9,1... | collective-permute-start | bytes 393224 | tf_op jit(solution)/shard_map/ppermute | solution.py:134
  115.7 1.0 copy-start.3
  115.7 1.0 copy-start.6

commit v3 on v1

v3 whole, which is shorter than its diff:
```python
import jax
import jax.numpy as jnp
from jax import lax
from jax.experimental import pallas as pl
from jax.experimental.pallas import tpu as pltpu
from jax.sharding import Mesh, PartitionSpec as P

FIRST = ("core", "panel")
CHIPS = ("pair", "panel")
LINE = ("panel",)
F32, BF16 = jnp.float32, jnp.bfloat16
VMEM = pl.BlockSpec(memory_space=pltpu.VMEM)
SMEM = pl.BlockSpec(memory_space=pltpu.SMEM)
HBM = pl.BlockSpec(memory_space=pltpu.HBM)
PARAMS = pltpu.CompilerParams(vmem_limit_bytes=24 << 20)


def in_hbm(*arrays):
    return [pltpu.with_memory_space_constraint(array, pltpu.HBM) for array in arrays]


def dot(left, right):
    return lax.dot_general(left, right, (((1,), (0,)), ((), ())), preferred_element_type=F32)


def half_lanes(block):
    return lax.broadcasted_iota(jnp.int32, block.shape, 1) < block.shape[1] // 2


def turned(block):
    return pltpu.roll(block, block.shape[1] // 2, 1)


def packed(lower, upper):
    low = half_lanes(lower)
    return jnp.where(low, lower, turned(upper)), jnp.where(low, turned(lower), upper)


def start_loads(sems, *pairs):
    loads = [pltpu.make_async_copy(*pair, sems.at[i]) for i, pair in enumerate(pairs)]
    for load in loads:
        load.start()
    return loads


def leaf_forward_kernel(
    rows_h, count, rhs, inverse, panels, side1, solved, send, above, total, *scratch
):
    rows, rhs_v, inverse_v, panels_v, side1_v, sems = scratch
    loads = start_loads(
        sems,
        (inverse, inverse_v),
        (rhs, rhs_v),
        (panels, panels_v),
        (side1, side1_v),
        (rows_h, rows),
    )
    slots, touched, width = panels_v.shape[:3]
    first_blocks = send.shape[0]
    half = first_blocks // 2
    total[...] = jnp.zeros_like(total)
    loads[0].wait()
    loads[1].wait()
    for s in range(slots):
        live = jnp.where(s < count[0, 0], 1.0, 0.0)
        solved[s] = (dot(inverse_v[s], rhs_v[s]) * live).astype(BF16)
    loads[2].wait()
    loads[4].wait()
    for s in range(slots):
        products = dot(panels_v[s].reshape(touched * width, width), solved[s])
        for k in range(touched):
            total[rows[s, k]] += products[k * width : (k + 1) * width]
    loads[3].wait()
    own = lax.axis_index("core") * half + lax.axis_index("panel")
    total[own] -= side1_v[...].astype(F32)
    for p in range(half):
        zero, one = packed(total[p], total[half + p])
        send[p] = zero.astype(BF16)
        send[half + p] = one.astype(BF16)
    above[...] = total[first_blocks:]


def leaf_forward(rows, count, rhs, inverse, panels, side1, first_blocks, second_blocks):
    block = rhs.shape[1:]
    return pl.pallas_call(
        leaf_forward_kernel,
        out_shape=(
            jax.ShapeDtypeStruct(rhs.shape, BF16),
            jax.ShapeDtypeStruct((first_blocks,) + block, BF16),
            jax.ShapeDtypeStruct((second_blocks,) + block, F32),
        ),
        in_specs=[HBM, SMEM] + [HBM] * 4,
        out_specs=(VMEM,) * 3,
        scratch_shapes=[
            pltpu.VMEM((first_blocks + second_blocks,) + block, F32),
            pltpu.SMEM(rows.shape, rows.dtype),
            pltpu.VMEM(rhs.shape, BF16),
            pltpu.VMEM(inverse.shape, BF16),
            pltpu.VMEM(panels.shape, BF16),
            pltpu.VMEM(side1.shape, BF16),
            pltpu.SemaphoreType.DMA((5,)),
        ],
        compiler_params=PARAMS,
        name="leaf_forward",
    )(*in_hbm(rows), count, *in_hbm(rhs, inverse, panels, side1))


def leaf_second_kernel(
    above, solved, side2, inverse1, panel1, inverse2, panels, inverse, *outputs_and_scratch
):
    store, keep, solved_t, panels_v, inverse_v, side2_v, sems = outputs_and_scratch
    rows1, rows2 = inverse1.shape[0], inverse2.shape[0]
    loads = start_loads(
        sems,
        (inverse1, store.at[0:rows1]),
        (panel1, store.at[rows1 : rows1 + rows2]),
        (inverse2, store.at[rows1 + rows2 : rows1 + 2 * rows2]),
        (panels, panels_v),
        (inverse, inverse_v),
        (side2, side2_v),
    )
    send = rows1 + 2 * rows2
    width = above.shape[1]
    line = above.shape[0] // 4
    core = lax.axis_index("core")
    own = (lax.axis_index("pair") * 2 + core) * line + lax.axis_index("panel")
    loads[5].wait()
    side = side2_v[...].astype(F32)
    for z in range(2):
        for p in range(line):
            at = z * 2 * line + p
            lower = above[at] - jnp.where(own == at, 1.0, 0.0) * side
            upper = above[at + line] - jnp.where(own == at + line, 1.0, 0.0) * side
            zero, one = packed(lower, upper)
            at = z * line + p
            keep[at] = jnp.where(core == 0, zero, one)
            away = jnp.where(core == 0, one, zero)
            store[send + at * width : send + (at + 1) * width] = away.astype(BF16)
    for s in range(solved.shape[0]):
        solved_t[s] = solved[s].astype(F32).T.astype(BF16)
    for load in loads[:5]:
        load.wait()


def leaf_second(above, solved, side2, inverse1, panel1, inverse2, panels, inverse):
    halves = above.shape[0] // 2
    rows = inverse1.shape[0] + panel1.shape[0] + inverse2.shape[0] + halves * above.shape[1]
    return pl.pallas_call(
        leaf_second_kernel,
        out_shape=(
            jax.ShapeDtypeStruct((rows, inverse1.shape[1]), BF16),
            jax.ShapeDtypeStruct((halves,) + above.shape[1:], F32),
            jax.ShapeDtypeStruct(solved.shape, BF16),
            jax.ShapeDtypeStruct(panels.shape, BF16),
            jax.ShapeDtypeStruct(inverse.shape, BF16),
        ),
        in_specs=[VMEM] * 2 + [HBM] * 6,
        out_specs=(VMEM,) * 5,
        scratch_shapes=[pltpu.VMEM(side2.shape, BF16), pltpu.SemaphoreType.DMA((6,))],
        compiler_params=PARAMS,
        name="leaf_second",
    )(above, solved, *in_hbm(side2, inverse1, panel1, inverse2, panels, inverse))


def column_products(piece, mine, other, first_row, row_count):
    low = half_lanes(piece)
    across = turned(piece)
    zero = jnp.zeros_like(piece)
    lower = (jnp.where(low, piece, zero), jnp.where(low, across, zero))
    upper = (jnp.where(low, zero, across), jnp.where(low, zero, piece))
    swap = lax.axis_index("core") == 1

    def ordered(two):
        return [jnp.where(swap, two[1], two[0]), jnp.where(swap, two[0], two[1])]

    weights = jnp.concatenate(ordered(lower) + ordered(upper), 0).astype(BF16)
    half = mine.shape[1] * 4
    parts = []
    for start in range(first_row, first_row + row_count, 2 * half):
        middle = start + half
        wide = jnp.concatenate(
            [
                mine[start:middle],
                other[start:middle],
                mine[middle : middle + half],
                other[middle : middle + half],
            ],
            1,
        )
        parts.append(dot(wide, weights))
    return parts


def side_partials(received, mine, other, first_row, row_count):
    width = mine.shape[1]

    def kernel(received, mine, other, partials):
        side = -received[...].astype(F32).sum(axis=0)
        side = side.astype(BF16).astype(F32)
        for z, part in enumerate(column_products(side, mine, other, first_row, row_count)):
            for p in range(4):
                partials[z * 4 + p] = part[p * width : (p + 1) * width].astype(BF16)

    return pl.pallas_call(
        kernel,
        out_shape=jax.ShapeDtypeStruct((row_count // width // 2,) + received.shape[1:], BF16),
        in_specs=[VMEM] * 3,
        out_specs=VMEM,
        compiler_params=PARAMS,
        name="side_partials",
    )(received, mine, other)


def raise_terms(received, keep, mine, other, first_row, row_count, terms_row):
    width = mine.shape[1]

    def kernel(received, keep, mine, other, raised, solved_t):
        piece = received[...].astype(F32).sum(axis=0)
        piece = piece.astype(BF16).astype(F32)
        for z, part in enumerate(column_products(piece, mine, other, first_row, row_count)):
            for p in range(4):
                at = z * 4 + p
                came = other[terms_row + at * width : terms_row + (at + 1) * width]
                terms = keep[at] + came.astype(F32)
                raised[at] = (part[p * width : (p + 1) * width] + terms).astype(BF16)
        solved_t[...] = piece.T.astype(BF16)

    return pl.pallas_call(
        kernel,
        out_shape=(
            jax.ShapeDtypeStruct(keep.shape, BF16),
            jax.ShapeDtypeStruct(received.shape[1:], BF16),
        ),
        in_specs=[VMEM] * 4,
        out_specs=(VMEM,) * 2,
        compiler_params=PARAMS,
        name="raise_terms",
    )(received, keep, mine, other)


def turn_kernel(received, copies):
    piece = received[...].astype(F32).sum(axis=0).T.astype(BF16)
    for i in range(copies.shape[0]):
        copies[i] = piece


def turned_sum(received):
    return pl.pallas_call(
        turn_kernel,
        out_shape=jax.ShapeDtypeStruct(received.shape, BF16),
        in_specs=[VMEM],
        out_specs=VMEM,
        compiler_params=PARAMS,
        name="turned_sum",
    )(received)


def back_step(whole, mine, other, first_row, targets, base=None):
    panels = 4
    half = whole.shape[1] // 2
    rows = pl.ds(first_row, 2 * whole.shape[0] * mine.shape[1])

    def kernel(whole, mine, other, *rest):
        pieces = []
        for z in range(whole.shape[0] // panels):
            for c in range(2):
                for p in range(panels):
                    pieces.append(whole[z * panels + p, c * half : (c + 1) * half])
        vectors = jnp.concatenate(pieces, 1)
        mine_t = dot(vectors, mine[rows])
        other_t = dot(vectors, other[rows])
        swap = lax.axis_index("core") == 1
        result = jnp.concatenate(
            [jnp.where(swap, other_t, mine_t), jnp.where(swap, mine_t, other_t)], 0
        )
        if base is not None:
            result = rest[0][...].astype(F32) - result
        copies = rest[-1]
        result = result.astype(BF16)
        for i in range(targets):
            copies[i] = result

    operands = (whole, mine, other) + (() if base is None else (base,))
    return pl.pallas_call(
        kernel,
        out_shape=jax.ShapeDtypeStruct((targets,) + whole.shape[1:], BF16),
        in_specs=[VMEM] * len(operands),
        out_specs=VMEM,
        compiler_params=PARAMS,
        name="back_step",
    )(*operands)


def join_kernel(mine, other, above, sample):
    core = lax.axis_index("core")
    half = mine.shape[1] // 2
    panels = 4
    here = pl.ds(pl.multiple_of(core * half, half), half)
    there = pl.ds(pl.multiple_of((1 - core) * half, half), half)
    for z in range(mine.shape[0] // panels):
        for c in range(2):
            for p in range(panels):
                at = z * 2 * panels + c * panels + p
                above[at, here] = mine[z * panels + p, c * half : (c + 1) * half]
                above[at, there] = other[z * panels + p, c * half : (c + 1) * half]
    own = lax.axis_index("pair") * 2 * panels + core * panels + lax.axis_index("panel")
    sample[...] = above[own].astype(F32).T.astype(BF16)


def join_halves(mine, other):
    return pl.pallas_call(
        join_kernel,
        out_shape=(
            jax.ShapeDtypeStruct((2 * mine.shape[0],) + mine.shape[1:], BF16),
            jax.ShapeDtypeStruct(mine.shape[1:], BF16),
        ),
        in_specs=[VMEM] * 2,
        out_specs=(VMEM,) * 2,
        compiler_params=PARAMS,
        name="join_halves",
    )(mine, other)


def leaf_backward_kernel(
    rows, count, whole, second, panels, inverse, solved_t, sample, sample1, first
):
    slots, touched, width = panels.shape[:3]
    half = width // 2
    split = whole.shape[0]
    line = split // 2
    for c in range(2):
        for p in range(line):
            for h in range(2):
                first[c * line + p, h * half : (h + 1) * half] = whole[
                    h * line + p, c * half : (c + 1) * half
                ]
    for s in range(slots):
        picked = []
        for k in range(touched):
            row = rows[s, k]
            low = first[jnp.minimum(row, split - 1)]
            high = second[jnp.maximum(row - split, 0)]
            picked.append(jnp.where(row < split, low, high))
        correction = dot(
            jnp.concatenate(picked, 1), panels[s].reshape(touched * width, width)
        )
        shifted = (solved_t[s].astype(F32) - correction).astype(BF16)
        live = jnp.where(s < count[0, 0], 1.0, 0.0)
        result = dot(shifted, inverse[s]) * live
        sample[s] = result.T.astype(BF16)
    own = lax.axis_index("core") * line + lax.axis_index("panel")
    sample1[...] = first[own].astype(F32).T.astype(BF16)


def leaf_backward(rows, count, whole, second, panels, inverse, solved_t):
    return pl.pallas_call(
        leaf_backward_kernel,
        out_shape=(
            jax.ShapeDtypeStruct(solved_t.shape, BF16),
            jax.ShapeDtypeStruct(whole.shape[1:], BF16),
        ),
        in_specs=[SMEM, SMEM] + [VMEM] * 5,
        out_specs=(VMEM,) * 2,
        scratch_shapes=[pltpu.VMEM(whole.shape, BF16)],
        compiler_params=PARAMS,
        name="leaf_backward",
    )(rows, count, whole, second, panels, inverse, solved_t)


def exchange(blocks, axes):
    return lax.all_to_all(blocks, axes, 0, 0, tiled=True)


def swapped(array):
    return lax.ppermute(array, "core", [(0, 1), (1, 0)])


def body(
    leaf_rhs,
    leaf_inverse,
    leaf_panel,
    panel_rows,
    live_count,
    sep1_rhs,
    sep1_inverse,
    sep1_panel,
    sep2_rhs,
    sep2_inverse,
):
    inverse, panels, rows = leaf_inverse[0, 0], leaf_panel[0, 0], panel_rows[0, 0]
    inverse1, inverse2, panel1 = sep1_inverse[0, 0], sep2_inverse[0, 0], sep1_panel[0, 0]
    width = inverse.shape[1]
    first_blocks = inverse1.shape[0] // width
    second_blocks = inverse2.shape[0] // width
    line = first_blocks // 2

    solved, send1, above = leaf_forward(
        rows,
        live_count,
        leaf_rhs[0, 0],
        inverse,
        panels,
        sep1_rhs[0, 0],
        first_blocks,
        second_blocks,
    )
    received1 = exchange(send1, FIRST)
    store, keep, solved_t, panels, inverse = leaf_second(
        above, solved, sep2_rhs[0, 0], inverse1, panel1, inverse2, panels, inverse
    )
    other = swapped(store)
    rows1, rows2 = inverse1.shape[0], inverse2.shape[0]
    panel1_at, inverse2_at, terms_at = rows1, rows1 + rows2, rows1 + 2 * rows2

    partial1 = side_partials(received1, store, other, 0, rows1)
    raised, solved1_t = raise_terms(
        exchange(partial1, LINE), keep, store, other, panel1_at, rows2, terms_at
    )
    partial2 = side_partials(exchange(raised, CHIPS), store, other, inverse2_at, rows2)
    whole_solved = exchange(turned_sum(exchange(partial2, CHIPS)), CHIPS)

    whole_second = exchange(
        back_step(whole_solved, store, other, inverse2_at, second_blocks // 2), CHIPS
    )
    shifted = back_step(whole_second, store, other, panel1_at, line, solved1_t)
    whole_shifted = exchange(shifted, LINE)
    other_second = swapped(lax.optimization_barrier((whole_second, shifted))[0])
    second, sample2 = join_halves(whole_second, other_second)
    whole_first = exchange(back_step(whole_shifted, store, other, 0, first_blocks), FIRST)
    leaf_sample, sample1 = leaf_backward(
        rows, live_count, whole_first, second, panels, inverse, solved_t
    )
    return (leaf_sample[None, None], sample1[None, None], sample2[None, None])


def solution(mesh):
    places = mesh.devices.reshape(-1, 2, 2, mesh.shape["panel"])
    fine = Mesh(places, ("group", "pair", "core", "panel"))
    leaf = ("group", "pair", "core")

    def spec(rank):
        return P("panel", leaf, *(None,) * (rank - 2))

    return jax.shard_map(
        body,
        mesh=fine,
        in_specs=tuple(spec(rank) for rank in (5, 5, 6, 4, 2, 4, 4, 4, 4, 4)),
        out_specs=tuple(spec(rank) for rank in (5, 4, 4)),
        check_vma=False,
    )
```

time: 141 us -> 99 us (0.70)
  blocking collectives: 117 us -> 50.3 us
  starting transfers between devices: 3.49 us -> 28.2 us
  Pallas kernels: 0 us -> 9.3 us
  matrix products: 5.55 us -> 0 us
  local copies, waits for them, and re-layouts: 6.27 us -> 4.04 us
  other arithmetic: 1.83 us -> 0 us
    all_gather x2 -> x0, blocking collectives: 48.8 us -> none  [gather(): return lax.all_gather(piece[None], axes, axis=0, tiled=True)]
    all_to_all x5 -> x6, blocking collectives: 68.4 us -> 50.3 us  [exchange(): return lax.all_to_all(blocks, axes, 0, 0, tiled=True)]
    ppermute x0 -> x2, starting transfers between devices: none -> 17.6 us  [swapped(): return lax.ppermute(array, 'core', [(0, 1), (1, 0)])]
    pallas_call x0 -> x11, Pallas kernels: none -> 9.3 us  [the longest x1 1.79 us: leaf_backward(): pl.pallas_call(leaf_backward_kernel, out_shape=(jax.ShapeDtypeStruct(solv...]
    all_to_all x1 -> x2, starting transfers between devices: 3.49 us -> 10.7 us  [exchange(): return lax.all_to_all(blocks, axes, 0, 0, tiled=True)]
    dot_general x9 -> x0, matrix products: 5.55 us -> none  [the longest x3 1.86 us: apply_columns(): product = jnp.dot(columns, piece, preferred_element_type=jnp.float32)]
    reshape x2 -> x0, local copies, waits for them, and re-layouts: 1.81 us -> none  [the longest x1 1.55 us: apply_columns(): return product.reshape(-1, width, piece.shape[-1])]
    unnamed x21 -> x18, local copies, waits for them, and re-layouts: 2.24 us -> 4.04 us
  transfers between devices with their start and end apart: 1 -> 4, of which waited for: 1 -> 1; matrix products, arithmetic and copies ran while one was open for 1% -> 0% of each run, Pallas kernels for 0% -> 2%
where the time goes in v3:
time: 99 us; the launch traced here: 98.2 us
  blocking collectives  50.3 us (51%)
  starting transfers between devices  28.2 us (28%)
  Pallas kernels  9.3 us (9%)
  waiting for transfers between devices  4.85 us (5%)
  local copies, waits for them, and re-layouts  4.04 us (4%)
  between operations  1.45 us (1%)
    all_to_all x6, blocking collectives, exchange(): return lax.all_to_all(blocks, axes, 0, 0, tiled=True)  50.3 us
    ppermute x2, starting transfers between devices, swapped(): return lax.ppermute(array, 'core', [(0, 1), (1, 0)])  17.6 us
    all_to_all x2, starting transfers between devices, exchange(): return lax.all_to_all(blocks, axes, 0, 0, tiled=True)  10.7 us
    all_to_all x2, waiting for transfers between devices, exchange(): return lax.all_to_all(blocks, axes, 0, 0, tiled=True)  4.85 us
    unnamed x18, local copies, waits for them, and re-layouts  4.04 us
  transfers between devices with their start and end apart: 4, of which 1 were waited for; matrix products, arithmetic and copies ran while one was open for 0% of the time, Pallas kernels for 2%

profile of v3, /device:TPU:1, one launch (start us, length us, event | category | flops | bytes accessed | tf_op | source)
XLA Modules:
  0.0 98.2 jit_solution(13091320029843201715)
XLA Ops:
  1.3 1.6 %leaf_forward.1 = (bf16[2,128,128]{2,1,0:T(8,128)(2,1)S(1)}, bf16[8,128,128]{2,1,0:T(8,128)(2,1)S(1)}, f32[16,128,128]{2,1,0:T(8,128)S(1)}) custom-call(s32[2,6]{1,0:T(2,128)} %bitcast.12, s32[1,1]{1,0:T(1,128)S(6)} %copy.13.count, bf16[2,128,128]{2,1,0:T(8,128)(2,1)} %bitcast.21, bf16[2,128,128]{2,1,0:T(8,128)(2,1)} %bitcast.19, ...), custom_call_target="tpu_custom_call" | custom-call | tf_op jit(solution)/shard_map/leaf_forward/pallas_call | solution.py:85
  2.9 1.8 %leaf_second.1 = (bf16[6144,128]{1,0:T(8,128)(2,1)S(1)}, f32[8,128,128]{2,1,0:T(8,128)S(1)}, bf16[2,128,128]{2,1,0:T(8,128)(2,1)S(1)}, bf16[2,6,128,128]{3,2,1,0:T(8,128)(2,1)S(1)}, bf16[2,128,128]{2,1,0:T(8,128)(2,1)S(1)}) custom-call(f32[16,128,128]{2,1,0:T(8,128)S(1)} %get-tuple-element.19.above, bf16[2,128,128]{2,1,0:T(8,128)(2,1)S(1)} %get-tuple-element.20.solved, ...), custom_call_target="tpu_custom_call" | custom-call | tf_op jit(solution)/shard_map/leaf_second/pallas_call | solution.py:148
  4.7 0.0 copy-start.6
  4.7 8.8 %collective-permute-start = (bf16[6144,128]{1,0:T(8,128)(2,1)S(1)}, bf16[6144,128]{1,0:T(8,128)(2,1)S(1)}, u32[]{:S(2)}, u32[]{:S(2)}) collective-permute-start(bf16[6144,128]{1,0:T(8,128)(2,1)S(1)} %get-tuple-element.21.mine), channel_id=1, source_target_pairs={{0,4},{4,0},{1,5},{5,1},{2,6},{6,2},{3,7},{7,3},{8,12},{12,8},{9,1... | collective-permute-start | bytes 4718600 | tf_op jit(solution)/shard_map/ppermute | solution.py:375
  13.5 9.0 %all_to_all.40.received = bf16[8,128,128]{2,1,0:T(8,128)(2,1)S(1)} all-to-all(bf16[8,128,128]{2,1,0:T(8,128)(2,1)S(1)} %get-tuple-element.18), channel_id=1, replica_groups=mesh['group'=32,'pair'=2,'core'=2,'panel'=4] {'core','panel'}, dimensions={0} | all-to-all | bytes 524288 | tf_op jit(solution)/shard_map/all_to_all | solution.py:371
  22.5 0.0 collective-permute-done.other
  22.5 0.4 side_partials.2
  22.9 7.2 %all_to_all.41.received = bf16[4,128,128]{2,1,0:T(8,128)(2,1)S(1)} all-to-all(bf16[4,128,128]{2,1,0:T(8,128)(2,1)S(1)} %side_partials.2), channel_id=1, replica_groups=mesh['group'=32,'pair'=2,'core'=2,'panel'=4] {'panel'}, dimensions={0} | all-to-all | bytes 262144 | tf_op jit(solution)/shard_map/all_to_all | solution.py:371
  30.1 0.5 raise_terms.1
  30.7 8.5 %all_to_all.42.received = bf16[8,128,128]{2,1,0:T(8,128)(2,1)S(1)} all-to-all(bf16[8,128,128]{2,1,0:T(8,128)(2,1)S(1)} %get-tuple-element.23), channel_id=1, replica_groups=mesh['group'=32,'pair'=2,'core'=2,'panel'=4] {'pair','panel'}, dimensions={0} | all-to-all | bytes 524288 | tf_op jit(solution)/shard_map/all_to_all | solution.py:371
  39.1 0.5 side_partials.3
  39.7 8.7 %all_to_all.43.received = bf16[8,128,128]{2,1,0:T(8,128)(2,1)S(1)} all-to-all(bf16[8,128,128]{2,1,0:T(8,128)(2,1)S(1)} %side_partials.3), channel_id=1, replica_groups=mesh['group'=32,'pair'=2,'core'=2,'panel'=4] {'pair','panel'}, dimensions={0} | all-to-all | bytes 524288 | tf_op jit(solution)/shard_map/all_to_all | solution.py:371
  48.4 0.1 turned_sum.1
  48.5 8.5 %all_to_all.44.whole = bf16[8,128,128]{2,1,0:T(8,128)(2,1)S(1)} all-to-all(bf16[8,128,128]{2,1,0:T(8,128)(2,1)S(1)} %turned_sum.1), channel_id=1, replica_groups=mesh['group'=32,'pair'=2,'core'=2,'panel'=4] {'pair','panel'}, dimensions={0} | all-to-all | bytes 524288 | tf_op jit(solution)/shard_map/all_to_all | solution.py:371
  57.0 0.3 back_step.3
  57.3 8.5 %all_to_all.45.whole.mine = bf16[8,128,128]{2,1,0:T(8,128)(2,1)S(1)} all-to-all(bf16[8,128,128]{2,1,0:T(8,128)(2,1)S(1)} %back_step.3), channel_id=1, replica_groups=mesh['group'=32,'pair'=2,'core'=2,'panel'=4] {'pair','panel'}, dimensions={0} | all-to-all | bytes 524288 | tf_op jit(solution)/shard_map/all_to_all | solution.py:371
  65.8 0.3 back_step.4
  66.1 0.6 copy-done.1
  66.8 3.3 %all-to-all-start.6 = ((bf16[4,128,128]{2,1,0:T(8,128)(2,1)}), bf16[4,128,128]{2,1,0:T(8,128)(2,1)S(1)}, u32[]{:S(2)}, u32[]{:S(2)}) async-start(bf16[4,128,128]{2,1,0:T(8,128)(2,1)} %copy-done.1), calls=%async_computation.6 | async-start | bytes 262144 | tf_op jit(solution)/shard_map/all_to_all | solution.py:371
  70.1 0.0 copy-start.8
  70.1 8.8 %collective-permute-start.1 = (bf16[8,128,128]{2,1,0:T(8,128)(2,1)S(1)}, bf16[8,128,128]{2,1,0:T(8,128)(2,1)}, u32[]{:S(2)}, u32[]{:S(2)}) collective-permute-start(bf16[8,128,128]{2,1,0:T(8,128)(2,1)S(1)} %all_to_all.45.whole.mine), channel_id=1, source_target_pairs={{0,4},{4,0},{1,5},{5,1},{2,6},{6,2},{3,7},{7,3},{8,12},{12,8},{9,1... | collective-permute-start | bytes 786440 | tf_op jit(solution)/shard_map/ppermute | solution.py:375
  78.9 0.0 all-to-all-done.6.whole
  78.9 0.2 back_step.5
  79.2 0.7 copy-done
  79.9 7.3 %all-to-all-start.7 = ((bf16[8,128,128]{2,1,0:T(8,128)(2,1)}), bf16[8,128,128]{2,1,0:T(8,128)(2,1)S(1)}, u32[]{:S(2)}, u32[]{:S(2)}) async-start(bf16[8,128,128]{2,1,0:T(8,128)(2,1)} %copy-done), calls=%async_computation.7 | async-start | bytes 524288 | tf_op jit(solution)/shard_map/all_to_all | solution.py:371
  87.2 0.0 collective-permute-done.1.other
  87.2 1.7 %join_halves.1 = (bf16[16,128,128]{2,1,0:T(8,128)(2,1)S(1)}, bf16[128,128]{1,0:T(8,128)(2,1)}) custom-call(bf16[8,128,128]{2,1,0:T(8,128)(2,1)S(1)} %all_to_all.45.whole.mine, bf16[8,128,128]{2,1,0:T(8,128)(2,1)} %collective-permute-done.1.other), custom_call_target="tpu_custom_call" | custom-call | tf_op jit(solution)/shard_map/join_halves/pallas_call | solution.py:311
  88.9 4.8 %all-to-all-done.7.whole = bf16[8,128,128]{2,1,0:T(8,128)(2,1)S(1)} async-done(((bf16[8,128,128]{2,1,0:T(8,128)(2,1)}), bf16[8,128,128]{2,1,0:T(8,128)(2,1)S(1)}, u32[]{:S(2)}, u32[]{:S(2)}) %all-to-all-start.7) | async-done | bytes 262176 | tf_op jit(solution)/shard_map/all_to_all | solution.py:371
  93.8 1.0 %copy-done.3 = bf16[2,6,128,128]{3,2,1,0:T(8,128)(2,1)S(1)} copy-done((bf16[2,6,128,128]{3,2,1,0:T(8,128)(2,1)S(1)}, bf16[2,6,128,128]{3,2,1,0:T(8,128)(2,1)}, u32[]{:S(2)}) %copy-start.3) | copy-done | bytes 393240
  94.8 0.8 copy-done.5
  95.6 0.8 copy-done.7
  96.4 1.8 %leaf_backward.1 = (bf16[2,128,128]{2,1,0:T(8,128)(2,1)}, bf16[128,128]{1,0:T(8,128)(2,1)}) custom-call(s32[2,6]{1,0:T(2,128)S(1)} %bitcast.13, s32[1,1]{1,0:T(1,128)S(6)} %copy.13.count, bf16[8,128,128]{2,1,0:T(8,128)(2,1)S(1)} %all-to-all-done.7.whole, bf16[16,128,128]{2,1,0:T(8,128)(2,1)S(1)} %get-tuple-element.26.second, ...), custom_call_target="tpu_custom_call" | custom-call | tf_op jit(solution)/shard_map/leaf_backward/pallas_call | solution.py:356
  (11 shorter events, 0.0 us)
Async XLA Ops:
  4.7 18.2 %copy-start.2 = (bf16[2,6,128,128]{3,2,1,0:T(8,128)(2,1)}, bf16[2,6,128,128]{3,2,1,0:T(8,128)(2,1)S(1)}, u32[]{:S(2)}) copy-start(bf16[2,6,128,128]{3,2,1,0:T(8,128)(2,1)S(1)} %get-tuple-element.27.panels) | copy-start | bytes 1179652
  4.7 18.2 %copy-start.4 = (bf16[2,128,128]{2,1,0:T(8,128)(2,1)}, bf16[2,128,128]{2,1,0:T(8,128)(2,1)S(1)}, u32[]{:S(2)}) copy-start(bf16[2,128,128]{2,1,0:T(8,128)(2,1)S(1)} %get-tuple-element.29.solved_t) | copy-start | bytes 196612
  4.7 18.2 %copy-start.6 = (bf16[2,128,128]{2,1,0:T(8,128)(2,1)}, bf16[2,128,128]{2,1,0:T(8,128)(2,1)S(1)}, u32[]{:S(2)}) copy-start(bf16[2,128,128]{2,1,0:T(8,128)(2,1)S(1)} %get-tuple-element.28.inverse) | copy-start | bytes 196612
  4.7 17.8 %collective-permute-start = (bf16[6144,128]{1,0:T(8,128)(2,1)S(1)}, bf16[6144,128]{1,0:T(8,128)(2,1)S(1)}, u32[]{:S(2)}, u32[]{:S(2)}) collective-permute-start(bf16[6144,128]{1,0:T(8,128)(2,1)S(1)} %get-tuple-element.21.mine), channel_id=1, source_target_pairs={{0,4},{4,0},{1,5},{5,1},{2,6},{6,2},{3,7},{7,3},{8,12},{12,8},{9,1... | collective-permute-start | bytes 4718600 | tf_op jit(solution)/shard_map/ppermute | solution.py:375
  66.1 0.7 copy-start.1
  66.8 12.2 %all-to-all-start.6 = ((bf16[4,128,128]{2,1,0:T(8,128)(2,1)}), bf16[4,128,128]{2,1,0:T(8,128)(2,1)S(1)}, u32[]{:S(2)}, u32[]{:S(2)}) async-start(bf16[4,128,128]{2,1,0:T(8,128)(2,1)} %copy-done.1), calls=%async_computation.6 | async-start | bytes 262144 | tf_op jit(solution)/shard_map/all_to_all | solution.py:371
  70.1 23.7 %copy-start.8 = (s32[1,1,2,6]{3,2,1,0:T(2,128)S(1)}, s32[1,1,2,6]{3,2,1,0:T(2,128)}, u32[]{:S(2)}) copy-start(s32[1,1,2,6]{3,2,1,0:T(2,128)} %param.13) | copy-start | bytes 148
  70.1 17.1 %collective-permute-start.1 = (bf16[8,128,128]{2,1,0:T(8,128)(2,1)S(1)}, bf16[8,128,128]{2,1,0:T(8,128)(2,1)}, u32[]{:S(2)}, u32[]{:S(2)}) collective-permute-start(bf16[8,128,128]{2,1,0:T(8,128)(2,1)S(1)} %all_to_all.45.whole.mine), channel_id=1, source_target_pairs={{0,4},{4,0},{1,5},{5,1},{2,6},{6,2},{3,7},{7,3},{8,12},{12,8},{9,1... | collective-permute-start | bytes 786440 | tf_op jit(solution)/shard_map/ppermute | solution.py:375
  79.2 0.7 copy-start
  79.9 13.9 %all-to-all-start.7 = ((bf16[8,128,128]{2,1,0:T(8,128)(2,1)}), bf16[8,128,128]{2,1,0:T(8,128)(2,1)S(1)}, u32[]{:S(2)}, u32[]{:S(2)}) async-start(bf16[8,128,128]{2,1,0:T(8,128)(2,1)} %copy-done), calls=%async_computation.7 | async-start | bytes 524288 | tf_op jit(solution)/shard_map/all_to_all | solution.py:371
  93.8 1.0 %copy-start.3 = (bf16[2,6,128,128]{3,2,1,0:T(8,128)(2,1)S(1)}, bf16[2,6,128,128]{3,2,1,0:T(8,128)(2,1)}, u32[]{:S(2)}) copy-start(bf16[2,6,128,128]{3,2,1,0:T(8,128)(2,1)} %copy-done.2) | copy-start | bytes 1179652
  94.8 0.8 copy-start.5
  95.6 0.8 copy-start.7

commit v4 on v3

v4 whole, which is shorter than its diff:
```python
import jax
import jax.numpy as jnp
from jax import lax
from jax.experimental import pallas as pl
from jax.experimental.pallas import tpu as pltpu
from jax.sharding import Mesh, PartitionSpec as P

FIRST = ("core", "panel")
CHIPS = ("pair", "panel")
LINE = ("panel",)
F32, BF16 = jnp.float32, jnp.bfloat16
VMEM = pl.BlockSpec(memory_space=pltpu.VMEM)
SMEM = pl.BlockSpec(memory_space=pltpu.SMEM)
HBM = pl.BlockSpec(memory_space=pltpu.HBM)
PARAMS = pltpu.CompilerParams(vmem_limit_bytes=24 << 20)


def in_hbm(*arrays):
    return [pltpu.with_memory_space_constraint(array, pltpu.HBM) for array in arrays]


def dot(left, right):
    return lax.dot_general(left, right, (((1,), (0,)), ((), ())), preferred_element_type=F32)


def half_lanes(block):
    return lax.broadcasted_iota(jnp.int32, block.shape, 1) < block.shape[1] // 2


def turned(block):
    return pltpu.roll(block, block.shape[1] // 2, 1)


def packed(lower, upper):
    low = half_lanes(lower)
    return jnp.where(low, lower, turned(upper)), jnp.where(low, turned(lower), upper)


def start_loads(sems, *pairs):
    loads = [pltpu.make_async_copy(*pair, sems.at[i]) for i, pair in enumerate(pairs)]
    for load in loads:
        load.start()
    return loads


def leaf_solve(count, inverse, rhs, slot):
    live = jnp.where(slot < count[0, 0], 1.0, 0.0)
    return (dot(inverse[slot], rhs[slot]) * live).astype(BF16)


def leaf_forward_kernel(
    rows_h,
    count,
    rhs,
    inverse,
    panels,
    side1,
    side2,
    inverse1,
    panel1,
    inverse2,
    send,
    store,
    keep,
    total,
    rows,
    rhs_v,
    inverse_v,
    panels_v,
    side1_v,
    side2_v,
    sems,
):
    rows1, rows2 = inverse1.shape[0], inverse2.shape[0]
    loads = start_loads(
        sems,
        (inverse, inverse_v),
        (rhs, rhs_v),
        (panels, panels_v),
        (rows_h, rows),
        (side1, side1_v),
        (side2, side2_v),
        (inverse1, store.at[0:rows1]),
        (panel1, store.at[rows1 : rows1 + rows2]),
        (inverse2, store.at[rows1 + rows2 : rows1 + 2 * rows2]),
    )
    slots, touched, width = panels_v.shape[:3]
    split = send.shape[0]
    line = split // 2
    core = lax.axis_index("core")
    total[...] = jnp.zeros_like(total)
    loads[0].wait()
    loads[1].wait()
    solved = [leaf_solve(count, inverse_v, rhs_v, s) for s in range(slots)]
    loads[2].wait()
    loads[3].wait()
    for s in range(slots):
        products = dot(panels_v[s].reshape(touched * width, width), solved[s])
        for k in range(touched):
            total[rows[s, k]] += products[k * width : (k + 1) * width]
    loads[4].wait()
    loads[5].wait()
    own = core * line + lax.axis_index("panel")
    total[own] -= side1_v[...].astype(F32)
    total[split + lax.axis_index("pair") * split + own] -= side2_v[...].astype(F32)
    for p in range(line):
        zero, one = packed(total[p], total[line + p])
        send[p] = zero.astype(BF16)
        send[line + p] = one.astype(BF16)
    away_row = rows1 + 2 * rows2
    for z in range(2):
        for p in range(line):
            at = split + z * split + p
            zero, one = packed(total[at], total[at + line])
            at = z * line + p
            keep[at] = jnp.where(core == 0, zero, one)
            away = jnp.where(core == 0, one, zero)
            store[away_row + at * width : away_row + (at + 1) * width] = away.astype(BF16)
    for load in loads[6:]:
        load.wait()


def leaf_forward(count, rows, rhs, inverse, panels, side1, side2, inverse1, panel1, inverse2):
    block = rhs.shape[1:]
    first_blocks, second_blocks = (m.shape[0] // block[0] for m in (inverse1, inverse2))
    halves = second_blocks // 2
    store_rows = inverse1.shape[0] + 2 * inverse2.shape[0] + halves * block[0]
    arrays = in_hbm(rhs, inverse, panels, side1, side2, inverse1, panel1, inverse2)
    return pl.pallas_call(
        leaf_forward_kernel,
        out_shape=(
            jax.ShapeDtypeStruct((first_blocks,) + block, BF16),
            jax.ShapeDtypeStruct((store_rows, block[0]), BF16),
            jax.ShapeDtypeStruct((halves,) + block, F32),
        ),
        in_specs=[HBM, SMEM] + [HBM] * len(arrays),
        out_specs=(VMEM,) * 3,
        scratch_shapes=[
            pltpu.VMEM((first_blocks + second_blocks,) + block, F32),
            pltpu.SMEM(rows.shape, rows.dtype),
            pltpu.VMEM(rhs.shape, BF16),
            pltpu.VMEM(inverse.shape, BF16),
            pltpu.VMEM(panels.shape, BF16),
            pltpu.VMEM(side1.shape, BF16),
            pltpu.VMEM(side2.shape, BF16),
            pltpu.SemaphoreType.DMA((9,)),
        ],
        compiler_params=PARAMS,
        name="leaf_forward",
    )(*in_hbm(rows), count, *arrays)


def column_products(piece, mine, other, first_row, row_count):
    low = half_lanes(piece)
    across = turned(piece)
    zero = jnp.zeros_like(piece)
    lower = (jnp.where(low, piece, zero), jnp.where(low, across, zero))
    upper = (jnp.where(low, zero, across), jnp.where(low, zero, piece))
    swap = lax.axis_index("core") == 1

    def ordered(two):
        return [jnp.where(swap, two[1], two[0]), jnp.where(swap, two[0], two[1])]

    weights = jnp.concatenate(ordered(lower) + ordered(upper), 0).astype(BF16)
    half = mine.shape[1] * 4
    parts = []
    for start in range(first_row, first_row + row_count, 2 * half):
        middle = start + half
        wide = jnp.concatenate(
            [
                mine[start:middle],
                other[start:middle],
                mine[middle : middle + half],
                other[middle : middle + half],
            ],
            1,
        )
        parts.append(dot(wide, weights))
    return parts


def side_partials(received, mine, other, first_row, row_count):
    width = mine.shape[1]

    def kernel(received, mine, other, partials):
        side = -received[...].astype(F32).sum(axis=0)
        side = side.astype(BF16).astype(F32)
        for z, part in enumerate(column_products(side, mine, other, first_row, row_count)):
            for p in range(4):
                partials[z * 4 + p] = part[p * width : (p + 1) * width].astype(BF16)

    return pl.pallas_call(
        kernel,
        out_shape=jax.ShapeDtypeStruct((row_count // width // 2,) + received.shape[1:], BF16),
        in_specs=[VMEM] * 3,
        out_specs=VMEM,
        compiler_params=PARAMS,
        name="side_partials",
    )(received, mine, other)


def raise_terms(received, keep, mine, other, first_row, row_count, terms_row):
    width = mine.shape[1]

    def kernel(received, keep, mine, other, raised, solved_t):
        piece = received[...].astype(F32).sum(axis=0)
        piece = piece.astype(BF16).astype(F32)
        for z, part in enumerate(column_products(piece, mine, other, first_row, row_count)):
            for p in range(4):
                at = z * 4 + p
                came = other[terms_row + at * width : terms_row + (at + 1) * width]
                terms = keep[at] + came.astype(F32)
                raised[at] = (part[p * width : (p + 1) * width] + terms).astype(BF16)
        solved_t[...] = piece.T.astype(BF16)

    return pl.pallas_call(
        kernel,
        out_shape=(
            jax.ShapeDtypeStruct(keep.shape, BF16),
            jax.ShapeDtypeStruct(received.shape[1:], BF16),
        ),
        in_specs=[VMEM] * 4,
        out_specs=(VMEM,) * 2,
        compiler_params=PARAMS,
        name="raise_terms",
    )(received, keep, mine, other)


def turn_kernel(received, copies):
    piece = received[...].astype(F32).sum(axis=0).T.astype(BF16)
    for i in range(copies.shape[0]):
        copies[i] = piece


def turned_sum(received):
    return pl.pallas_call(
        turn_kernel,
        out_shape=jax.ShapeDtypeStruct(received.shape, BF16),
        in_specs=[VMEM],
        out_specs=VMEM,
        compiler_params=PARAMS,
        name="turned_sum",
    )(received)


def back_step(whole, mine, other, first_row, targets, base=None):
    panels = 4
    half = whole.shape[1] // 2
    rows = pl.ds(first_row, 2 * whole.shape[0] * mine.shape[1])

    def kernel(whole, mine, other, *rest):
        pieces = []
        for z in range(whole.shape[0] // panels):
            for c in range(2):
                for p in range(panels):
                    pieces.append(whole[z * panels + p, c * half : (c + 1) * half])
        vectors = jnp.concatenate(pieces, 1)
        mine_t = dot(vectors, mine[rows])
        other_t = dot(vectors, other[rows])
        swap = lax.axis_index("core") == 1
        result = jnp.concatenate(
            [jnp.where(swap, other_t, mine_t), jnp.where(swap, mine_t, other_t)], 0
        )
        if base is not None:
            result = rest[0][...].astype(F32) - result
        copies = rest[-1]
        result = result.astype(BF16)
        for i in range(targets):
            copies[i] = result

    operands = (whole, mine, other) + (() if base is None else (base,))
    return pl.pallas_call(
        kernel,
        out_shape=jax.ShapeDtypeStruct((targets,) + whole.shape[1:], BF16),
        in_specs=[VMEM] * len(operands),
        out_specs=VMEM,
        compiler_params=PARAMS,
        name="back_step",
    )(*operands)


def reload_kernel(count, rhs, inverse, panels, inverse_v, panels_v, solved_t, rhs_v, sems):
    loads = start_loads(sems, (inverse, inverse_v), (rhs, rhs_v), (panels, panels_v))
    loads[0].wait()
    loads[1].wait()
    for s in range(solved_t.shape[0]):
        solved_t[s] = leaf_solve(count, inverse_v, rhs_v, s).astype(F32).T.astype(BF16)
    loads[2].wait()


def leaf_reload(count, rhs, inverse, panels):
    return pl.pallas_call(
        reload_kernel,
        out_shape=tuple(jax.ShapeDtypeStruct(a.shape, BF16) for a in (inverse, panels, rhs)),
        in_specs=[SMEM] + [HBM] * 3,
        out_specs=(VMEM,) * 3,
        scratch_shapes=[pltpu.VMEM(rhs.shape, BF16), pltpu.SemaphoreType.DMA((3,))],
        compiler_params=PARAMS,
        name="leaf_reload",
    )(count, *in_hbm(rhs, inverse, panels))


def leaf_backward_kernel(
    rows, count, whole, mine, other, panels, inverse, solved_t, sample, sample1, sample2
):
    slots, touched, width = panels.shape[:3]
    half = width // 2
    line = 4
    split = 2 * line
    core = lax.axis_index("core")

    def first_block(block):
        at = pl.ds(pl.multiple_of(block // line * half, half), half)
        return [whole[h * line + block % line, at] for h in range(2)]

    def second_block(block):
        at = pl.ds(pl.multiple_of(block // line % 2 * half, half), half)
        place = block // split * line + block % line
        here, there = mine[place, at], other[place, at]
        return [jnp.where(core == 0, here, there), jnp.where(core == 0, there, here)]

    for s in range(slots):
        picked = []
        for k in range(touched):
            row = rows[s, k]
            low = first_block(jnp.minimum(row, split - 1))
            high = second_block(jnp.maximum(row - split, 0))
            chosen = [jnp.where(row < split, a, b) for a, b in zip(low, high)]
            picked.append(jnp.concatenate(chosen, 0))
        correction = dot(
            jnp.concatenate(picked, 1), panels[s].reshape(touched * width, width)
        )
        shifted = (solved_t[s].astype(F32) - correction).astype(BF16)
        live = jnp.where(s < count[0, 0], 1.0, 0.0)
        result = dot(shifted, inverse[s]) * live
        sample[s] = result.T.astype(BF16)
    own = core * line + lax.axis_index("panel")
    sample1[...] = jnp.concatenate(first_block(own), 0).astype(F32).T.astype(BF16)
    own = own + lax.axis_index("pair") * split
    sample2[...] = jnp.concatenate(second_block(own), 0).astype(F32).T.astype(BF16)


def leaf_backward(rows, count, whole, mine, other, panels, inverse, solved_t):
    return pl.pallas_call(
        leaf_backward_kernel,
        out_shape=(
            jax.ShapeDtypeStruct(solved_t.shape, BF16),
            jax.ShapeDtypeStruct(whole.shape[1:], BF16),
            jax.ShapeDtypeStruct(whole.shape[1:], BF16),
        ),
        in_specs=[SMEM, SMEM] + [VMEM] * 6,
        out_specs=(VMEM,) * 3,
        compiler_params=PARAMS,
        name="leaf_backward",
    )(rows, count, whole, mine, other, panels, inverse, solved_t)


def exchange(blocks, axes):
    return lax.all_to_all(blocks, axes, 0, 0, tiled=True)


def swapped(array):
    return lax.ppermute(array, "core", [(0, 1), (1, 0)])


def body(
    leaf_rhs,
    leaf_inverse,
    leaf_panel,
    panel_rows,
    live_count,
    sep1_rhs,
    sep1_inverse,
    sep1_panel,
    sep2_rhs,
    sep2_inverse,
):
    rhs, inverse, panels = leaf_rhs[0, 0], leaf_inverse[0, 0], leaf_panel[0, 0]
    rows = panel_rows[0, 0]
    inverse1, inverse2, panel1 = sep1_inverse[0, 0], sep2_inverse[0, 0], sep1_panel[0, 0]
    width = inverse.shape[1]
    first_blocks = inverse1.shape[0] // width
    second_blocks = inverse2.shape[0] // width
    rows1, rows2 = inverse1.shape[0], inverse2.shape[0]
    panel1_at, inverse2_at, terms_at = rows1, rows1 + rows2, rows1 + 2 * rows2

    send1, store, keep = leaf_forward(
        live_count,
        rows,
        rhs,
        inverse,
        panels,
        sep1_rhs[0, 0],
        sep2_rhs[0, 0],
        inverse1,
        panel1,
        inverse2,
    )
    other = swapped(store)
    partial1 = side_partials(exchange(send1, FIRST), store, other, 0, rows1)
    raised, solved1_t = raise_terms(
        exchange(partial1, LINE), keep, store, other, panel1_at, rows2, terms_at
    )
    partial2 = side_partials(exchange(raised, CHIPS), store, other, inverse2_at, rows2)
    whole_solved = exchange(turned_sum(exchange(partial2, CHIPS)), CHIPS)

    whole_second = exchange(
        back_step(whole_solved, store, other, inverse2_at, second_blocks // 2), CHIPS
    )
    shifted = back_step(whole_second, store, other, panel1_at, first_blocks // 2, solved1_t)
    whole_shifted = exchange(shifted, LINE)
    second_late, rhs, inverse, panels, _ = lax.optimization_barrier(
        (whole_second, rhs, inverse, panels, shifted)
    )
    other_second = swapped(second_late)
    inverse, panels, solved_t = leaf_reload(live_count, rhs, inverse, panels)
    whole_shifted, inverse, panels, solved_t = lax.optimization_barrier(
        (whole_shifted, inverse, panels, solved_t)
    )
    whole_first = exchange(back_step(whole_shifted, store, other, 0, first_blocks), FIRST)
    leaf_sample, sample1, sample2 = leaf_backward(
        rows, live_count, whole_first, whole_second, other_second, panels, inverse, solved_t
    )
    return (leaf_sample[None, None], sample1[None, None], sample2[None, None])


def solution(mesh):
    places = mesh.devices.reshape(-1, 2, 2, mesh.shape["panel"])
    fine = Mesh(places, ("group", "pair", "core", "panel"))
    leaf = ("group", "pair", "core")

    def spec(rank):
        return P("panel", leaf, *(None,) * (rank - 2))

    return jax.shard_map(
        body,
        mesh=fine,
        in_specs=tuple(spec(rank) for rank in (5, 5, 6, 4, 2, 4, 4, 4, 4, 4)),
        out_specs=tuple(spec(rank) for rank in (5, 4, 4)),
        check_vma=False,
    )
```

time: 99 us -> 98.6 us (level)
  starting transfers between devices: 28.2 us -> 25.8 us
  local copies, waits for them, and re-layouts: 4.04 us -> 6.03 us
  waiting for transfers between devices: 4.85 us -> 6.57 us
  Pallas kernels: 9.3 us -> 7.69 us
    all_to_all x2, starting transfers between devices: 10.7 us -> 8.19 us  [exchange(): return lax.all_to_all(blocks, axes, 0, 0, tiled=True)]
    pallas_call x3 -> x2, Pallas kernels: 5.12 us -> 3.03 us  [the longest x1 1.88 us: leaf_forward(): pl.pallas_call(leaf_forward_kernel, out_shape=(jax.ShapeDtypeStruct((firs...]
    unnamed x18, local copies, waits for them, and re-layouts: 4.04 us -> 6.03 us
    all_to_all x2, waiting for transfers between devices: 4.85 us -> 6.56 us  [exchange(): return lax.all_to_all(blocks, axes, 0, 0, tiled=True)]
  transfers between devices with their start and end apart: 4 -> 4, of which waited for: 1 -> 1; matrix products, arithmetic and copies ran while one was open for 0% -> 0% of each run, Pallas kernels for 2% -> 1%
where the time goes in v4:
time: 98.6 us; the launch traced here: 97.8 us
  blocking collectives  50.3 us (51%)
  starting transfers between devices  25.8 us (26%)
  Pallas kernels  7.69 us (8%)
  waiting for transfers between devices  6.57 us (7%)
  local copies, waits for them, and re-layouts  6.03 us (6%)
  between operations  1.4 us (1%)
    all_to_all x6, blocking collectives, exchange(): return lax.all_to_all(blocks, axes, 0, 0, tiled=True)  50.3 us
    ppermute x2, starting transfers between devices, swapped(): return lax.ppermute(array, 'core', [(0, 1), (1, 0)])  17.6 us
    all_to_all x2, starting transfers between devices, exchange(): return lax.all_to_all(blocks, axes, 0, 0, tiled=True)  8.19 us
    all_to_all x2, waiting for transfers between devices, exchange(): return lax.all_to_all(blocks, axes, 0, 0, tiled=True)  6.56 us
    unnamed x18, local copies, waits for them, and re-layouts  6.03 us
    pallas_call x1, Pallas kernels, leaf_backward(): pl.pallas_call(leaf_backward_kernel, out_shape=(jax.ShapeDtypeStruct(solv...  2.26 us
  transfers between devices with their start and end apart: 4, of which 1 were waited for; matrix products, arithmetic and copies ran while one was open for 0% of the time, Pallas kernels for 1%

profile of v4, /device:TPU:1, one launch (start us, length us, event | category | flops | bytes accessed | tf_op | source)
XLA Modules:
  0.0 97.8 jit_solution(17848816453567180803)
XLA Ops:
  1.3 1.9 %leaf_forward.1 = (bf16[8,128,128]{2,1,0:T(8,128)(2,1)S(1)}, bf16[6144,128]{1,0:T(8,128)(2,1)S(1)}, f32[8,128,128]{2,1,0:T(8,128)S(1)}) custom-call(s32[2,6]{1,0:T(2,128)} %bitcast.12, s32[1,1]{1,0:T(1,128)S(6)} %copy.13.count, bf16[2,128,128]{2,1,0:T(8,128)(2,1)} %bitcast.18, bf16[2,128,128]{2,1,0:T(8,128)(2,1)} %bitcast.20, ...), custom_call_target="tpu_custom_call" | custom-call | tf_op jit(solution)/shard_map/leaf_forward/pallas_call | solution.py:129
  3.2 8.8 %collective-permute-start = (bf16[6144,128]{1,0:T(8,128)(2,1)S(1)}, bf16[6144,128]{1,0:T(8,128)(2,1)S(1)}, u32[]{:S(2)}, u32[]{:S(2)}) collective-permute-start(bf16[6144,128]{1,0:T(8,128)(2,1)S(1)} %get-tuple-element.23.mine), channel_id=1, source_target_pairs={{0,4},{4,0},{1,5},{5,1},{2,6},{6,2},{3,7},{7,3},{8,12},{12,8},{9,1... | collective-permute-start | bytes 4718600 | tf_op jit(solution)/shard_map/ppermute | solution.py:363
  12.0 9.0 %all_to_all.40.received = bf16[8,128,128]{2,1,0:T(8,128)(2,1)S(1)} all-to-all(bf16[8,128,128]{2,1,0:T(8,128)(2,1)S(1)} %get-tuple-element.22), channel_id=1, replica_groups=mesh['group'=32,'pair'=2,'core'=2,'panel'=4] {'core','panel'}, dimensions={0} | all-to-all | bytes 524288 | tf_op jit(solution)/shard_map/all_to_all | solution.py:359
  20.9 0.0 collective-permute-done.other
  20.9 0.4 side_partials.2
  21.3 7.2 %all_to_all.41.received = bf16[4,128,128]{2,1,0:T(8,128)(2,1)S(1)} all-to-all(bf16[4,128,128]{2,1,0:T(8,128)(2,1)S(1)} %side_partials.2), channel_id=1, replica_groups=mesh['group'=32,'pair'=2,'core'=2,'panel'=4] {'panel'}, dimensions={0} | all-to-all | bytes 262144 | tf_op jit(solution)/shard_map/all_to_all | solution.py:359
  28.5 0.5 raise_terms.1
  29.1 8.5 %all_to_all.42.received = bf16[8,128,128]{2,1,0:T(8,128)(2,1)S(1)} all-to-all(bf16[8,128,128]{2,1,0:T(8,128)(2,1)S(1)} %get-tuple-element.25), channel_id=1, replica_groups=mesh['group'=32,'pair'=2,'core'=2,'panel'=4] {'pair','panel'}, dimensions={0} | all-to-all | bytes 524288 | tf_op jit(solution)/shard_map/all_to_all | solution.py:359
  37.6 0.5 side_partials.3
  38.1 8.7 %all_to_all.43.received = bf16[8,128,128]{2,1,0:T(8,128)(2,1)S(1)} all-to-all(bf16[8,128,128]{2,1,0:T(8,128)(2,1)S(1)} %side_partials.3), channel_id=1, replica_groups=mesh['group'=32,'pair'=2,'core'=2,'panel'=4] {'pair','panel'}, dimensions={0} | all-to-all | bytes 524288 | tf_op jit(solution)/shard_map/all_to_all | solution.py:359
  46.8 0.1 turned_sum.1
  46.9 8.5 %all_to_all.44.whole = bf16[8,128,128]{2,1,0:T(8,128)(2,1)S(1)} all-to-all(bf16[8,128,128]{2,1,0:T(8,128)(2,1)S(1)} %turned_sum.1), channel_id=1, replica_groups=mesh['group'=32,'pair'=2,'core'=2,'panel'=4] {'pair','panel'}, dimensions={0} | all-to-all | bytes 524288 | tf_op jit(solution)/shard_map/all_to_all | solution.py:359
  55.4 0.3 back_step.3
  55.7 8.5 %all_to_all.45.whole.mine = bf16[8,128,128]{2,1,0:T(8,128)(2,1)S(1)} all-to-all(bf16[8,128,128]{2,1,0:T(8,128)(2,1)S(1)} %back_step.3), channel_id=1, replica_groups=mesh['group'=32,'pair'=2,'core'=2,'panel'=4] {'pair','panel'}, dimensions={0} | all-to-all | bytes 524288 | tf_op jit(solution)/shard_map/all_to_all | solution.py:359
  64.2 0.3 back_step.4
  64.5 0.7 copy-done.1
  65.2 3.3 %all-to-all-start.6 = ((bf16[4,128,128]{2,1,0:T(8,128)(2,1)}), bf16[4,128,128]{2,1,0:T(8,128)(2,1)S(1)}, u32[]{:S(2)}, u32[]{:S(2)}) async-start(bf16[4,128,128]{2,1,0:T(8,128)(2,1)} %copy-done.1), calls=%async_computation.6 | async-start | bytes 262144 | tf_op jit(solution)/shard_map/all_to_all | solution.py:359
  68.5 8.8 %collective-permute-start.1 = (bf16[8,128,128]{2,1,0:T(8,128)(2,1)S(1)}, bf16[8,128,128]{2,1,0:T(8,128)(2,1)}, u32[]{:S(2)}, u32[]{:S(2)}) collective-permute-start(bf16[8,128,128]{2,1,0:T(8,128)(2,1)S(1)} %all_to_all.45.whole.mine), channel_id=1, source_target_pairs={{0,4},{4,0},{1,5},{5,1},{2,6},{6,2},{3,7},{7,3},{8,12},{12,8},{9,1... | collective-permute-start | bytes 786440 | tf_op jit(solution)/shard_map/ppermute | solution.py:363
  77.3 1.1 %leaf_reload.1 = (bf16[2,128,128]{2,1,0:T(8,128)(2,1)S(1)}, bf16[2,6,128,128]{3,2,1,0:T(8,128)(2,1)S(1)}, bf16[2,128,128]{2,1,0:T(8,128)(2,1)S(1)}) custom-call(s32[1,1]{1,0:T(1,128)S(6)} %copy.13.count, bf16[2,128,128]{2,1,0:T(8,128)(2,1)} %bitcast.19, bf16[2,128,128]{2,1,0:T(8,128)(2,1)} %bitcast.21, bf16[2,6,128,128]{3,2,1,0:T(8,128)(2,1)} %bitcast.15), custom_call_target="tpu_custom_call" | custom-call | tf_op jit(solution)/shard_map/leaf_reload/pallas_call | solution.py:292
  78.5 0.7 copy-done.2
  79.2 0.6 copy-done.4
  79.9 0.6 copy-done.6
  80.5 0.0 all-to-all-done.6.whole
  80.5 0.2 back_step.5
  80.7 0.7 copy-done
  81.4 4.9 %all-to-all-start.7 = ((bf16[8,128,128]{2,1,0:T(8,128)(2,1)}), bf16[8,128,128]{2,1,0:T(8,128)(2,1)S(1)}, u32[]{:S(2)}, u32[]{:S(2)}) async-start(bf16[8,128,128]{2,1,0:T(8,128)(2,1)} %copy-done), calls=%async_computation.7 | async-start | bytes 524288 | tf_op jit(solution)/shard_map/all_to_all | solution.py:359
  86.3 0.0 collective-permute-done.1.other
  86.3 6.6 %all-to-all-done.7.whole = bf16[8,128,128]{2,1,0:T(8,128)(2,1)S(1)} async-done(((bf16[8,128,128]{2,1,0:T(8,128)(2,1)}), bf16[8,128,128]{2,1,0:T(8,128)(2,1)S(1)}, u32[]{:S(2)}, u32[]{:S(2)}) %all-to-all-start.7) | async-done | bytes 262176 | tf_op jit(solution)/shard_map/all_to_all | solution.py:359
  92.9 1.0 %copy-done.3 = bf16[2,6,128,128]{3,2,1,0:T(8,128)(2,1)S(1)} copy-done((bf16[2,6,128,128]{3,2,1,0:T(8,128)(2,1)S(1)}, bf16[2,6,128,128]{3,2,1,0:T(8,128)(2,1)}, u32[]{:S(2)}) %copy-start.3) | copy-done | bytes 393240
  93.9 0.8 copy-done.5
  94.7 0.8 copy-done.7
  95.5 2.3 %leaf_backward.1 = (bf16[2,128,128]{2,1,0:T(8,128)(2,1)}, bf16[128,128]{1,0:T(8,128)(2,1)}, bf16[128,128]{1,0:T(8,128)(2,1)}) custom-call(s32[2,6]{1,0:T(2,128)S(1)} %bitcast.13, s32[1,1]{1,0:T(1,128)S(6)} %copy.13.count, bf16[8,128,128]{2,1,0:T(8,128)(2,1)S(1)} %all-to-all-done.7.whole, bf16[8,128,128]{2,1,0:T(8,128)(2,1)S(1)} %all_to_all.45.whole.mine, ...), custom_call_target="tpu_custom_call" | custom-call | tf_op jit(solution)/shard_map/leaf_backward/pallas_call | solution.py:344
  (10 shorter events, 0.0 us)
Async XLA Ops:
  3.2 17.8 %collective-permute-start = (bf16[6144,128]{1,0:T(8,128)(2,1)S(1)}, bf16[6144,128]{1,0:T(8,128)(2,1)S(1)}, u32[]{:S(2)}, u32[]{:S(2)}) collective-permute-start(bf16[6144,128]{1,0:T(8,128)(2,1)S(1)} %get-tuple-element.23.mine), channel_id=1, source_target_pairs={{0,4},{4,0},{1,5},{5,1},{2,6},{6,2},{3,7},{7,3},{8,12},{12,8},{9,1... | collective-permute-start | bytes 4718600 | tf_op jit(solution)/shard_map/ppermute | solution.py:363
  64.5 0.7 copy-start.1
  65.2 15.3 %all-to-all-start.6 = ((bf16[4,128,128]{2,1,0:T(8,128)(2,1)}), bf16[4,128,128]{2,1,0:T(8,128)(2,1)S(1)}, u32[]{:S(2)}, u32[]{:S(2)}) async-start(bf16[4,128,128]{2,1,0:T(8,128)(2,1)} %copy-done.1), calls=%async_computation.6 | async-start | bytes 262144 | tf_op jit(solution)/shard_map/all_to_all | solution.py:359
  68.5 17.8 %collective-permute-start.1 = (bf16[8,128,128]{2,1,0:T(8,128)(2,1)S(1)}, bf16[8,128,128]{2,1,0:T(8,128)(2,1)}, u32[]{:S(2)}, u32[]{:S(2)}) collective-permute-start(bf16[8,128,128]{2,1,0:T(8,128)(2,1)S(1)} %all_to_all.45.whole.mine), channel_id=1, source_target_pairs={{0,4},{4,0},{1,5},{5,1},{2,6},{6,2},{3,7},{7,3},{8,12},{12,8},{9,1... | collective-permute-start | bytes 786440 | tf_op jit(solution)/shard_map/ppermute | solution.py:363
  78.5 0.8 copy-start.2
  79.2 0.6 copy-start.4
  79.8 0.6 copy-start.6
  80.5 12.4 %copy-start.8 = (s32[1,1,2,6]{3,2,1,0:T(2,128)S(1)}, s32[1,1,2,6]{3,2,1,0:T(2,128)}, u32[]{:S(2)}) copy-start(s32[1,1,2,6]{3,2,1,0:T(2,128)} %param.13) | copy-start | bytes 148
  80.7 0.7 copy-start
  81.4 11.4 %all-to-all-start.7 = ((bf16[8,128,128]{2,1,0:T(8,128)(2,1)}), bf16[8,128,128]{2,1,0:T(8,128)(2,1)S(1)}, u32[]{:S(2)}, u32[]{:S(2)}) async-start(bf16[8,128,128]{2,1,0:T(8,128)(2,1)} %copy-done), calls=%async_computation.7 | async-start | bytes 524288 | tf_op jit(solution)/shard_map/all_to_all | solution.py:359
  92.9 1.0 %copy-start.3 = (bf16[2,6,128,128]{3,2,1,0:T(8,128)(2,1)S(1)}, bf16[2,6,128,128]{3,2,1,0:T(8,128)(2,1)}, u32[]{:S(2)}) copy-start(bf16[2,6,128,128]{3,2,1,0:T(8,128)(2,1)} %copy-done.2) | copy-start | bytes 1179652
  93.9 0.8 copy-start.5
  94.7 0.8 copy-start.7

commit v5 on v4

--- a/solution.py
+++ b/solution.py
@@ -279,31 +279,26 @@
     )(*operands)
 
 
-def reload_kernel(count, rhs, inverse, panels, inverse_v, panels_v, solved_t, rhs_v, sems):
+def leaf_backward_kernel(
+    rows,
+    count,
+    rhs,
+    inverse,
+    panels,
+    whole,
+    mine,
+    other,
+    sample,
+    sample1,
+    sample2,
+    rhs_v,
+    inverse_v,
+    panels_v,
+    picked,
+    sems,
+):
     loads = start_loads(sems, (inverse, inverse_v), (rhs, rhs_v), (panels, panels_v))
-    loads[0].wait()
-    loads[1].wait()
-    for s in range(solved_t.shape[0]):
-        solved_t[s] = leaf_solve(count, inverse_v, rhs_v, s).astype(F32).T.astype(BF16)
-    loads[2].wait()
-
-
-def leaf_reload(count, rhs, inverse, panels):
-    return pl.pallas_call(
-        reload_kernel,
-        out_shape=tuple(jax.ShapeDtypeStruct(a.shape, BF16) for a in (inverse, panels, rhs)),
-        in_specs=[SMEM] + [HBM] * 3,
-        out_specs=(VMEM,) * 3,
-        scratch_shapes=[pltpu.VMEM(rhs.shape, BF16), pltpu.SemaphoreType.DMA((3,))],
-        compiler_params=PARAMS,
-        name="leaf_reload",
-    )(count, *in_hbm(rhs, inverse, panels))
-
-
-def leaf_backward_kernel(
-    rows, count, whole, mine, other, panels, inverse, solved_t, sample, sample1, sample2
-):
-    slots, touched, width = panels.shape[:3]
+    slots, touched, width = panels_v.shape[:3]
     half = width // 2
     line = 4
     split = 2 * line
@@ -320,39 +315,50 @@
         return [jnp.where(core == 0, here, there), jnp.where(core == 0, there, here)]
 
     for s in range(slots):
-        picked = []
         for k in range(touched):
             row = rows[s, k]
             low = first_block(jnp.minimum(row, split - 1))
             high = second_block(jnp.maximum(row - split, 0))
-            chosen = [jnp.where(row < split, a, b) for a, b in zip(low, high)]
-            picked.append(jnp.concatenate(chosen, 0))
-        correction = dot(
-            jnp.concatenate(picked, 1), panels[s].reshape(touched * width, width)
-        )
-        shifted = (solved_t[s].astype(F32) - correction).astype(BF16)
-        live = jnp.where(s < count[0, 0], 1.0, 0.0)
-        result = dot(shifted, inverse[s]) * live
-        sample[s] = result.T.astype(BF16)
+            for h in range(2):
+                picked[s, h * half : (h + 1) * half, k * width : (k + 1) * width] = jnp.where(
+                    row < split, low[h], high[h]
+                )
     own = core * line + lax.axis_index("panel")
     sample1[...] = jnp.concatenate(first_block(own), 0).astype(F32).T.astype(BF16)
     own = own + lax.axis_index("pair") * split
     sample2[...] = jnp.concatenate(second_block(own), 0).astype(F32).T.astype(BF16)
-
-
-def leaf_backward(rows, count, whole, mine, other, panels, inverse, solved_t):
+    loads[0].wait()
+    loads[1].wait()
+    solved_t = [
+        leaf_solve(count, inverse_v, rhs_v, s).astype(F32).T for s in range(slots)
+    ]
+    loads[2].wait()
+    for s in range(slots):
+        correction = dot(picked[s], panels_v[s].reshape(touched * width, width))
+        shifted = (solved_t[s] - correction).astype(BF16)
+        live = jnp.where(s < count[0, 0], 1.0, 0.0)
+        result = dot(shifted, inverse_v[s]) * live
+        sample[s] = result.T.astype(BF16)
+
+
+def leaf_backward(rows, count, rhs, inverse, panels, whole, mine, other):
+    slots, touched, width = panels.shape[:3]
+    block = jax.ShapeDtypeStruct(whole.shape[1:], BF16)
     return pl.pallas_call(
         leaf_backward_kernel,
-        out_shape=(
-            jax.ShapeDtypeStruct(solved_t.shape, BF16),
-            jax.ShapeDtypeStruct(whole.shape[1:], BF16),
-            jax.ShapeDtypeStruct(whole.shape[1:], BF16),
-        ),
-        in_specs=[SMEM, SMEM] + [VMEM] * 6,
+        out_shape=(jax.ShapeDtypeStruct(rhs.shape, BF16), block, block),
+        in_specs=[SMEM, SMEM] + [HBM] * 3 + [VMEM] * 3,
         out_specs=(VMEM,) * 3,
+        scratch_shapes=[
+            pltpu.VMEM(rhs.shape, BF16),
+            pltpu.VMEM(inverse.shape, BF16),
+            pltpu.VMEM(panels.shape, BF16),
+            pltpu.VMEM((slots, whole.shape[1], touched * width), BF16),
+            pltpu.SemaphoreType.DMA((3,)),
+        ],
         compiler_params=PARAMS,
         name="leaf_backward",
-    )(rows, count, whole, mine, other, panels, inverse, solved_t)
+    )(rows, count, *in_hbm(rhs, inverse, panels), whole, mine, other)
 
 
 def exchange(blocks, axes):
@@ -409,17 +415,11 @@
     )
     shifted = back_step(whole_second, store, other, panel1_at, first_blocks // 2, solved1_t)
     whole_shifted = exchange(shifted, LINE)
-    second_late, rhs, inverse, panels, _ = lax.optimization_barrier(
-        (whole_second, rhs, inverse, panels, shifted)
-    )
-    other_second = swapped(second_late)
-    inverse, panels, solved_t = leaf_reload(live_count, rhs, inverse, panels)
-    whole_shifted, inverse, panels, solved_t = lax.optimization_barrier(
-        (whole_shifted, inverse, panels, solved_t)
-    )
+    other_second = swapped(lax.optimization_barrier((whole_second, shifted))[0])
+    whole_shifted, other_second = lax.optimization_barrier((whole_shifted, other_second))
     whole_first = exchange(back_step(whole_shifted, store, other, 0, first_blocks), FIRST)
     leaf_sample, sample1, sample2 = leaf_backward(
-        rows, live_count, whole_first, whole_second, other_second, panels, inverse, solved_t
+        rows, live_count, rhs, inverse, panels, whole_first, whole_second, other_second
     )
     return (leaf_sample[None, None], sample1[None, None], sample2[None, None])
 

time: 98.6 us -> 94.9 us (0.962)
  blocking collectives: 50.3 us -> 67.9 us
  starting transfers between devices: 25.8 us -> 17.6 us
  waiting for transfers between devices: 6.57 us -> 0.01 us
  local copies, waits for them, and re-layouts: 6.03 us -> 0.01 us
    all_to_all x6 -> x8, blocking collectives: 50.3 us -> 67.9 us  [exchange(): return lax.all_to_all(blocks, axes, 0, 0, tiled=True)]
    all_to_all x2 -> x0, starting transfers between devices: 8.19 us -> none  [exchange(): return lax.all_to_all(blocks, axes, 0, 0, tiled=True)]
    all_to_all x2 -> x0, waiting for transfers between devices: 6.56 us -> none  [exchange(): return lax.all_to_all(blocks, axes, 0, 0, tiled=True)]
    unnamed x18 -> x2, local copies, waits for them, and re-layouts: 6.03 us -> 0.01 us
    pallas_call x2 -> x1, Pallas kernels: 3.41 us -> 3.25 us  [leaf_backward(): pl.pallas_call(leaf_backward_kernel, out_shape=(jax.ShapeDtypeStruct(rhs....]
  transfers between devices with their start and end apart: 4 -> 2, of which waited for: 1 -> 0; matrix products, arithmetic and copies ran while one was open for 0% -> 0% of each run, Pallas kernels for 1% -> 0%
where the time goes in v5:
time: 94.9 us; the launch traced here: 94.4 us
  blocking collectives  67.9 us (72%)
  starting transfers between devices  17.6 us (19%)
  Pallas kernels  7.53 us (8%)
  between operations  1.35 us (1%)
    all_to_all x8, blocking collectives, exchange(): return lax.all_to_all(blocks, axes, 0, 0, tiled=True)  67.9 us
    ppermute x2, starting transfers between devices, swapped(): return lax.ppermute(array, 'core', [(0, 1), (1, 0)])  17.6 us
    pallas_call x1, Pallas kernels, leaf_backward(): pl.pallas_call(leaf_backward_kernel, out_shape=(jax.ShapeDtypeStruct(rhs....  3.25 us
  transfers between devices with their start and end apart: 2, of which 0 were waited for; matrix products, arithmetic and copies ran while one was open for 0% of the time, Pallas kernels for 0%

profile of v5, /device:TPU:1, one launch (start us, length us, event | category | flops | bytes accessed | tf_op | source)
XLA Modules:
  0.0 94.4 jit_solution(16908972828922417821)
XLA Ops:
  1.3 1.9 %leaf_forward.1 = (bf16[8,128,128]{2,1,0:T(8,128)(2,1)S(1)}, bf16[6144,128]{1,0:T(8,128)(2,1)S(1)}, f32[8,128,128]{2,1,0:T(8,128)S(1)}) custom-call(s32[2,6]{1,0:T(2,128)} %bitcast.12, s32[1,1]{1,0:T(1,128)S(6)} %copy.13.count, bf16[2,128,128]{2,1,0:T(8,128)(2,1)} %bitcast.18, bf16[2,128,128]{2,1,0:T(8,128)(2,1)} %bitcast.20, ...), custom_call_target="tpu_custom_call" | custom-call | tf_op jit(solution)/shard_map/leaf_forward/pallas_call | solution.py:129
  3.2 8.8 %collective-permute-start = (bf16[6144,128]{1,0:T(8,128)(2,1)S(1)}, bf16[6144,128]{1,0:T(8,128)(2,1)S(1)}, u32[]{:S(2)}, u32[]{:S(2)}) collective-permute-start(bf16[6144,128]{1,0:T(8,128)(2,1)S(1)} %get-tuple-element.15.mine), channel_id=1, source_target_pairs={{0,4},{4,0},{1,5},{5,1},{2,6},{6,2},{3,7},{7,3},{8,12},{12,8},{9,1... | collective-permute-start | bytes 4718600 | tf_op jit(solution)/shard_map/ppermute | solution.py:369
  12.0 9.0 %all_to_all.40.received = bf16[8,128,128]{2,1,0:T(8,128)(2,1)S(1)} all-to-all(bf16[8,128,128]{2,1,0:T(8,128)(2,1)S(1)} %get-tuple-element.14), channel_id=1, replica_groups=mesh['group'=32,'pair'=2,'core'=2,'panel'=4] {'core','panel'}, dimensions={0} | all-to-all | bytes 524288 | tf_op jit(solution)/shard_map/all_to_all | solution.py:365
  20.9 0.0 collective-permute-done.other
  20.9 0.4 side_partials.2
  21.3 7.2 %all_to_all.41.received = bf16[4,128,128]{2,1,0:T(8,128)(2,1)S(1)} all-to-all(bf16[4,128,128]{2,1,0:T(8,128)(2,1)S(1)} %side_partials.2), channel_id=1, replica_groups=mesh['group'=32,'pair'=2,'core'=2,'panel'=4] {'panel'}, dimensions={0} | all-to-all | bytes 262144 | tf_op jit(solution)/shard_map/all_to_all | solution.py:365
  28.5 0.5 raise_terms.1
  29.1 8.5 %all_to_all.42.received = bf16[8,128,128]{2,1,0:T(8,128)(2,1)S(1)} all-to-all(bf16[8,128,128]{2,1,0:T(8,128)(2,1)S(1)} %get-tuple-element.17), channel_id=1, replica_groups=mesh['group'=32,'pair'=2,'core'=2,'panel'=4] {'pair','panel'}, dimensions={0} | all-to-all | bytes 524288 | tf_op jit(solution)/shard_map/all_to_all | solution.py:365
  37.6 0.5 side_partials.3
  38.1 8.7 %all_to_all.43.received = bf16[8,128,128]{2,1,0:T(8,128)(2,1)S(1)} all-to-all(bf16[8,128,128]{2,1,0:T(8,128)(2,1)S(1)} %side_partials.3), channel_id=1, replica_groups=mesh['group'=32,'pair'=2,'core'=2,'panel'=4] {'pair','panel'}, dimensions={0} | all-to-all | bytes 524288 | tf_op jit(solution)/shard_map/all_to_all | solution.py:365
  46.8 0.1 turned_sum.1
  46.9 8.5 %all_to_all.44.whole = bf16[8,128,128]{2,1,0:T(8,128)(2,1)S(1)} all-to-all(bf16[8,128,128]{2,1,0:T(8,128)(2,1)S(1)} %turned_sum.1), channel_id=1, replica_groups=mesh['group'=32,'pair'=2,'core'=2,'panel'=4] {'pair','panel'}, dimensions={0} | all-to-all | bytes 524288 | tf_op jit(solution)/shard_map/all_to_all | solution.py:365
  55.4 0.3 back_step.3
  55.7 8.5 %all_to_all.45.whole.mine = bf16[8,128,128]{2,1,0:T(8,128)(2,1)S(1)} all-to-all(bf16[8,128,128]{2,1,0:T(8,128)(2,1)S(1)} %back_step.3), channel_id=1, replica_groups=mesh['group'=32,'pair'=2,'core'=2,'panel'=4] {'pair','panel'}, dimensions={0} | all-to-all | bytes 524288 | tf_op jit(solution)/shard_map/all_to_all | solution.py:365
  64.2 0.3 back_step.4
  64.5 8.8 %collective-permute-start.1 = (bf16[8,128,128]{2,1,0:T(8,128)(2,1)S(1)}, bf16[8,128,128]{2,1,0:T(8,128)(2,1)S(1)}, u32[]{:S(2)}, u32[]{:S(2)}) collective-permute-start(bf16[8,128,128]{2,1,0:T(8,128)(2,1)S(1)} %all_to_all.45.whole.mine), channel_id=1, source_target_pairs={{0,4},{4,0},{1,5},{5,1},{2,6},{6,2},{3,7},{7,3},{8,12},{12,8},{9,1... | collective-permute-start | bytes 786440 | tf_op jit(solution)/shard_map/ppermute | solution.py:369
  73.3 7.5 %all_to_all.46.whole = bf16[4,128,128]{2,1,0:T(8,128)(2,1)S(1)} all-to-all(bf16[4,128,128]{2,1,0:T(8,128)(2,1)S(1)} %back_step.4), channel_id=1, replica_groups=mesh['group'=32,'pair'=2,'core'=2,'panel'=4] {'panel'}, dimensions={0} | all-to-all | bytes 262144 | tf_op jit(solution)/shard_map/all_to_all | solution.py:365
  80.8 0.0 copy-start
  80.8 0.0 collective-permute-done.1.other
  80.8 0.2 back_step.5
  81.1 10.1 %all_to_all.47.whole = bf16[8,128,128]{2,1,0:T(8,128)(2,1)S(1)} all-to-all(bf16[8,128,128]{2,1,0:T(8,128)(2,1)S(1)} %back_step.5), channel_id=1, replica_groups=mesh['group'=32,'pair'=2,'core'=2,'panel'=4] {'core','panel'}, dimensions={0} | all-to-all | bytes 524288 | tf_op jit(solution)/shard_map/all_to_all | solution.py:365
  91.1 0.0 copy-done
  91.1 3.2 %leaf_backward.1 = (bf16[2,128,128]{2,1,0:T(8,128)(2,1)}, bf16[128,128]{1,0:T(8,128)(2,1)}, bf16[128,128]{1,0:T(8,128)(2,1)}) custom-call(s32[2,6]{1,0:T(2,128)S(1)} %bitcast.13, s32[1,1]{1,0:T(1,128)S(6)} %copy.13.count, bf16[2,128,128]{2,1,0:T(8,128)(2,1)} %bitcast.19, bf16[2,128,128]{2,1,0:T(8,128)(2,1)} %bitcast.21, bf16[2,6,128,128]{3,2,1,0:T(8,128)(2,1)} %bitcast.15, ...), custom_call_target="tpu_custom_call" | custom-call | tf_op jit(solution)/shard_map/leaf_backward/pallas_call | solution.py:347
Async XLA Ops:
  3.2 17.8 %collective-permute-start = (bf16[6144,128]{1,0:T(8,128)(2,1)S(1)}, bf16[6144,128]{1,0:T(8,128)(2,1)S(1)}, u32[]{:S(2)}, u32[]{:S(2)}) collective-permute-start(bf16[6144,128]{1,0:T(8,128)(2,1)S(1)} %get-tuple-element.15.mine), channel_id=1, source_target_pairs={{0,4},{4,0},{1,5},{5,1},{2,6},{6,2},{3,7},{7,3},{8,12},{12,8},{9,1... | collective-permute-start | bytes 4718600 | tf_op jit(solution)/shard_map/ppermute | solution.py:369
  64.5 16.3 %collective-permute-start.1 = (bf16[8,128,128]{2,1,0:T(8,128)(2,1)S(1)}, bf16[8,128,128]{2,1,0:T(8,128)(2,1)S(1)}, u32[]{:S(2)}, u32[]{:S(2)}) collective-permute-start(bf16[8,128,128]{2,1,0:T(8,128)(2,1)S(1)} %all_to_all.45.whole.mine), channel_id=1, source_target_pairs={{0,4},{4,0},{1,5},{5,1},{2,6},{6,2},{3,7},{7,3},{8,12},{12,8},{9,1... | collective-permute-start | bytes 786440 | tf_op jit(solution)/shard_map/ppermute | solution.py:369
  80.8 10.3 %copy-start = (s32[1,1,2,6]{3,2,1,0:T(2,128)S(1)}, s32[1,1,2,6]{3,2,1,0:T(2,128)}, u32[]{:S(2)}) copy-start(s32[1,1,2,6]{3,2,1,0:T(2,128)} %param.13) | copy-start | bytes 148

commit v6 on v5

--- a/solution.py
+++ b/solution.py
@@ -43,94 +43,128 @@
     return loads
 
 
-def leaf_solve(count, inverse, rhs, slot):
-    live = jnp.where(slot < count[0, 0], 1.0, 0.0)
-    return (dot(inverse[slot], rhs[slot]) * live).astype(BF16)
-
-
-def leaf_forward_kernel(
-    rows_h,
-    count,
-    rhs,
-    inverse,
-    panels,
-    side1,
-    side2,
-    inverse1,
-    panel1,
-    inverse2,
-    send,
-    store,
-    keep,
-    total,
-    rows,
-    rhs_v,
-    inverse_v,
-    panels_v,
-    side1_v,
-    side2_v,
-    sems,
+def store_rows(rows1, rows2, slots, touched, width):
+    sizes = {
+        "inverse1": rows1,
+        "panel1": rows2,
+        "inverse2": rows2,
+        "terms": rows2 // 2,
+        "panels": slots * touched * width,
+        "inverse": slots * width,
+        "solved": slots * width,
+    }
+    places, end = {}, 0
+    for name, size in sizes.items():
+        places[name] = end
+        end += size
+    return places, end
+
+
+def leaf_forward(
+    places, count, rows, rhs, inverse, panels, side1, side2, inverse1, panel1, inverse2
 ):
-    rows1, rows2 = inverse1.shape[0], inverse2.shape[0]
-    loads = start_loads(
+    block = rhs.shape[1:]
+    width = block[0]
+    slots, touched = rows.shape
+    first_blocks, second_blocks = inverse1.shape[0] // width, inverse2.shape[0] // width
+    halves, line = second_blocks // 2, first_blocks // 2
+    own_rows, all_rows = places
+
+    def kernel(
+        rows_h,
+        count,
+        rhs,
+        inverse,
+        panels,
+        side1,
+        side2,
+        inverse1,
+        panel1,
+        inverse2,
+        send,
+        store,
+        keep,
+        total,
+        rows,
+        rhs_v,
+        side1_v,
+        side2_v,
         sems,
-        (inverse, inverse_v),
-        (rhs, rhs_v),
-        (panels, panels_v),
-        (rows_h, rows),
-        (side1, side1_v),
-        (side2, side2_v),
-        (inverse1, store.at[0:rows1]),
-        (panel1, store.at[rows1 : rows1 + rows2]),
-        (inverse2, store.at[rows1 + rows2 : rows1 + 2 * rows2]),
-    )
-    slots, touched, width = panels_v.shape[:3]
-    split = send.shape[0]
-    line = split // 2
-    core = lax.axis_index("core")
-    total[...] = jnp.zeros_like(total)
-    loads[0].wait()
-    loads[1].wait()
-    solved = [leaf_solve(count, inverse_v, rhs_v, s) for s in range(slots)]
-    loads[2].wait()
-    loads[3].wait()
-    for s in range(slots):
-        products = dot(panels_v[s].reshape(touched * width, width), solved[s])
-        for k in range(touched):
-            total[rows[s, k]] += products[k * width : (k + 1) * width]
-    loads[4].wait()
-    loads[5].wait()
-    own = core * line + lax.axis_index("panel")
-    total[own] -= side1_v[...].astype(F32)
-    total[split + lax.axis_index("pair") * split + own] -= side2_v[...].astype(F32)
-    for p in range(line):
-        zero, one = packed(total[p], total[line + p])
-        send[p] = zero.astype(BF16)
-        send[line + p] = one.astype(BF16)
-    away_row = rows1 + 2 * rows2
-    for z in range(2):
+        more_sems,
+    ):
+        def part(name, start=0, size=None, of=None):
+            first = own_rows[name] + start
+            return slice(first, first + (of.shape[0] if size is None else size))
+
+        loads = start_loads(
+            sems,
+            (inverse, store.at[part("inverse", of=inverse)]),
+            (rhs, rhs_v),
+            (panels, store.at[part("panels", of=panels)]),
+            (rows_h, rows),
+            (side1, side1_v),
+            (side2, side2_v),
+        )
+        core = lax.axis_index("core")
+        total[...] = jnp.zeros_like(total)
+        loads[0].wait()
+        loads[1].wait()
+        matrices = start_loads(
+            more_sems,
+            (inverse1, store.at[part("inverse1", of=inverse1)]),
+            (panel1, store.at[part("panel1", of=panel1)]),
+            (inverse2, store.at[part("inverse2", of=inverse2)]),
+        )
+        solved = []
+        for s in range(slots):
+            live = jnp.where(s < count[0, 0], 1.0, 0.0)
+            piece = dot(store[part("inverse", s * width, width)], rhs_v[s]) * live
+            piece = piece.astype(BF16)
+            store[part("solved", s * width, width)] = piece.astype(F32).T.astype(BF16)
+            solved.append(piece)
+        loads[2].wait()
+        loads[3].wait()
+        for s in range(slots):
+            tall = touched * width
+            products = dot(store[part("panels", s * tall, tall)], solved[s])
+            for k in range(touched):
+                total[rows[s, k]] += products[k * width : (k + 1) * width]
+        loads[4].wait()
+        loads[5].wait()
+        own = core * line + lax.axis_index("panel")
+        total[own] -= side1_v[...].astype(F32)
+        own = own + (lax.axis_index("pair") + 1) * first_blocks
+        total[own] -= side2_v[...].astype(F32)
         for p in range(line):
-            at = split + z * split + p
-            zero, one = packed(total[at], total[at + line])
-            at = z * line + p
-            keep[at] = jnp.where(core == 0, zero, one)
-            away = jnp.where(core == 0, one, zero)
-            store[away_row + at * width : away_row + (at + 1) * width] = away.astype(BF16)
-    for load in loads[6:]:
-        load.wait()
-
-
-def leaf_forward(count, rows, rhs, inverse, panels, side1, side2, inverse1, panel1, inverse2):
-    block = rhs.shape[1:]
-    first_blocks, second_blocks = (m.shape[0] // block[0] for m in (inverse1, inverse2))
-    halves = second_blocks // 2
-    store_rows = inverse1.shape[0] + 2 * inverse2.shape[0] + halves * block[0]
-    arrays = in_hbm(rhs, inverse, panels, side1, side2, inverse1, panel1, inverse2)
-    return pl.pallas_call(
-        leaf_forward_kernel,
+            zero, one = packed(total[p], total[line + p])
+            send[p] = zero.astype(BF16)
+            send[line + p] = one.astype(BF16)
+        for z in range(2):
+            for p in range(line):
+                at = (z + 1) * first_blocks + p
+                zero, one = packed(total[at], total[at + line])
+                at = z * line + p
+                keep[at] = jnp.where(core == 0, zero, one)
+                away = jnp.where(core == 0, one, zero)
+                store[part("terms", at * width, width)] = away.astype(BF16)
+        for load in matrices:
+            load.wait()
+
+    arrays = in_hbm(
+        rhs,
+        inverse.reshape(-1, width),
+        panels.reshape(-1, width),
+        side1,
+        side2,
+        inverse1,
+        panel1,
+        inverse2,
+    )
+    return pl.pallas_call(
+        kernel,
         out_shape=(
             jax.ShapeDtypeStruct((first_blocks,) + block, BF16),
-            jax.ShapeDtypeStruct((store_rows, block[0]), BF16),
+            jax.ShapeDtypeStruct((all_rows, width), BF16),
             jax.ShapeDtypeStruct((halves,) + block, F32),
         ),
         in_specs=[HBM, SMEM] + [HBM] * len(arrays),
@@ -139,11 +173,10 @@
             pltpu.VMEM((first_blocks + second_blocks,) + block, F32),
             pltpu.SMEM(rows.shape, rows.dtype),
             pltpu.VMEM(rhs.shape, BF16),
-            pltpu.VMEM(inverse.shape, BF16),
-            pltpu.VMEM(panels.shape, BF16),
             pltpu.VMEM(side1.shape, BF16),
             pltpu.VMEM(side2.shape, BF16),
-            pltpu.SemaphoreType.DMA((9,)),
+            pltpu.SemaphoreType.DMA((6,)),
+            pltpu.SemaphoreType.DMA((3,)),
         ],
         compiler_params=PARAMS,
         name="leaf_forward",
@@ -279,86 +312,58 @@
     )(*operands)
 
 
-def leaf_backward_kernel(
-    rows,
-    count,
-    rhs,
-    inverse,
-    panels,
-    whole,
-    mine,
-    other,
-    sample,
-    sample1,
-    sample2,
-    rhs_v,
-    inverse_v,
-    panels_v,
-    picked,
-    sems,
-):
-    loads = start_loads(sems, (inverse, inverse_v), (rhs, rhs_v), (panels, panels_v))
-    slots, touched, width = panels_v.shape[:3]
+def leaf_backward(places, rows, count, whole, mine, other, store):
+    slots, touched = rows.shape
+    width = whole.shape[1]
     half = width // 2
-    line = 4
-    split = 2 * line
-    core = lax.axis_index("core")
-
-    def first_block(block):
-        at = pl.ds(pl.multiple_of(block // line * half, half), half)
-        return [whole[h * line + block % line, at] for h in range(2)]
-
-    def second_block(block):
-        at = pl.ds(pl.multiple_of(block // line % 2 * half, half), half)
-        place = block // split * line + block % line
-        here, there = mine[place, at], other[place, at]
-        return [jnp.where(core == 0, here, there), jnp.where(core == 0, there, here)]
-
-    for s in range(slots):
-        for k in range(touched):
-            row = rows[s, k]
-            low = first_block(jnp.minimum(row, split - 1))
-            high = second_block(jnp.maximum(row - split, 0))
-            for h in range(2):
-                picked[s, h * half : (h + 1) * half, k * width : (k + 1) * width] = jnp.where(
-                    row < split, low[h], high[h]
-                )
-    own = core * line + lax.axis_index("panel")
-    sample1[...] = jnp.concatenate(first_block(own), 0).astype(F32).T.astype(BF16)
-    own = own + lax.axis_index("pair") * split
-    sample2[...] = jnp.concatenate(second_block(own), 0).astype(F32).T.astype(BF16)
-    loads[0].wait()
-    loads[1].wait()
-    solved_t = [
-        leaf_solve(count, inverse_v, rhs_v, s).astype(F32).T for s in range(slots)
-    ]
-    loads[2].wait()
-    for s in range(slots):
-        correction = dot(picked[s], panels_v[s].reshape(touched * width, width))
-        shifted = (solved_t[s] - correction).astype(BF16)
-        live = jnp.where(s < count[0, 0], 1.0, 0.0)
-        result = dot(shifted, inverse_v[s]) * live
-        sample[s] = result.T.astype(BF16)
-
-
-def leaf_backward(rows, count, rhs, inverse, panels, whole, mine, other):
-    slots, touched, width = panels.shape[:3]
-    block = jax.ShapeDtypeStruct(whole.shape[1:], BF16)
-    return pl.pallas_call(
-        leaf_backward_kernel,
-        out_shape=(jax.ShapeDtypeStruct(rhs.shape, BF16), block, block),
-        in_specs=[SMEM, SMEM] + [HBM] * 3 + [VMEM] * 3,
+    split = whole.shape[0]
+    line = split // 2
+    own_rows, _ = places
+
+    def kernel(rows, count, whole, mine, other, store, sample, sample1, sample2, above):
+        core = lax.axis_index("core")
+        here = pl.ds(pl.multiple_of(core * half, half), half)
+        there = pl.ds(pl.multiple_of((1 - core) * half, half), half)
+        for c in range(2):
+            part = slice(c * half, (c + 1) * half)
+            for p in range(line):
+                for h in range(2):
+                    above[c * line + p, h * half : (h + 1) * half] = whole[h * line + p, part]
+                for z in range(2):
+                    at = (z + 1) * split + c * line + p
+                    above[at, here] = mine[z * line + p, part]
+                    above[at, there] = other[z * line + p, part]
+
+        def stored(name, slot, size):
+            first = own_rows[name] + slot * size
+            return store[first : first + size]
+
+        for s in range(slots):
+            vectors = jnp.concatenate([above[rows[s, k]] for k in range(touched)], 1)
+            correction = dot(vectors, stored("panels", s, touched * width))
+            shifted = stored("solved", s, width).astype(F32) - correction
+            live = jnp.where(s < count[0, 0], 1.0, 0.0)
+            result = dot(shifted.astype(BF16), stored("inverse", s, width)) * live
+            sample[s] = result.T.astype(BF16)
+        own = core * line + lax.axis_index("panel")
+        sample1[...] = above[own].astype(F32).T.astype(BF16)
+        own = own + (lax.axis_index("pair") + 1) * split
+        sample2[...] = above[own].astype(F32).T.astype(BF16)
+
+    block = whole.shape[1:]
+    return pl.pallas_call(
+        kernel,
+        out_shape=(
+            jax.ShapeDtypeStruct((slots,) + block, BF16),
+            jax.ShapeDtypeStruct(block, BF16),
+            jax.ShapeDtypeStruct(block, BF16),
+        ),
+        in_specs=[SMEM, SMEM] + [VMEM] * 4,
         out_specs=(VMEM,) * 3,
-        scratch_shapes=[
-            pltpu.VMEM(rhs.shape, BF16),
-            pltpu.VMEM(inverse.shape, BF16),
-            pltpu.VMEM(panels.shape, BF16),
-            pltpu.VMEM((slots, whole.shape[1], touched * width), BF16),
-            pltpu.SemaphoreType.DMA((3,)),
-        ],
+        scratch_shapes=[pltpu.VMEM((split + 2 * mine.shape[0],) + block, BF16)],
         compiler_params=PARAMS,
         name="leaf_backward",
-    )(rows, count, *in_hbm(rhs, inverse, panels), whole, mine, other)
+    )(rows, count, whole, mine, other, store)
 
 
 def exchange(blocks, axes):
@@ -388,9 +393,12 @@
     first_blocks = inverse1.shape[0] // width
     second_blocks = inverse2.shape[0] // width
     rows1, rows2 = inverse1.shape[0], inverse2.shape[0]
-    panel1_at, inverse2_at, terms_at = rows1, rows1 + rows2, rows1 + 2 * rows2
+    places = store_rows(rows1, rows2, rows.shape[0], rows.shape[1], width)
+    panel1_at, inverse2_at = places[0]["panel1"], places[0]["inverse2"]
+    terms_at = places[0]["terms"]
 
     send1, store, keep = leaf_forward(
+        places,
         live_count,
         rows,
         rhs,
@@ -419,7 +427,7 @@
     whole_shifted, other_second = lax.optimization_barrier((whole_shifted, other_second))
     whole_first = exchange(back_step(whole_shifted, store, other, 0, first_blocks), FIRST)
     leaf_sample, sample1, sample2 = leaf_backward(
-        rows, live_count, rhs, inverse, panels, whole_first, whole_second, other_second
+        places, rows, live_count, whole_first, whole_second, other_second, store
     )
     return (leaf_sample[None, None], sample1[None, None], sample2[None, None])
 

time: 94.9 us -> 93.8 us (0.988)
  Pallas kernels: 7.53 us -> 6.48 us
    pallas_call x2, Pallas kernels: 5.13 us -> 4.09 us  [the longest x1 2.26 us: leaf_forward(): pl.pallas_call(kernel, out_shape=(jax.ShapeDtypeStruct((first_blocks,) +...]
where the time goes in v6:
time: 93.8 us; the launch traced here: 93.3 us
  blocking collectives  67.9 us (72%)
  starting transfers between devices  17.6 us (19%)
  Pallas kernels  6.48 us (7%)
  between operations  1.36 us (1%)
    all_to_all x8, blocking collectives, exchange(): return lax.all_to_all(blocks, axes, 0, 0, tiled=True)  67.9 us
    ppermute x2, starting transfers between devices, swapped(): return lax.ppermute(array, 'core', [(0, 1), (1, 0)])  17.6 us
    pallas_call x1, Pallas kernels, leaf_forward(): pl.pallas_call(kernel, out_shape=(jax.ShapeDtypeStruct((first_blocks,) +...  2.26 us
  transfers between devices with their start and end apart: 2, of which 0 were waited for; matrix products, arithmetic and copies ran while one was open for 0% of the time, Pallas kernels for 0%

profile of v6, /device:TPU:1, one launch (start us, length us, event | category | flops | bytes accessed | tf_op | source)
XLA Modules:
  0.0 93.3 jit_solution(7625855808910710474)
XLA Ops:
  1.3 2.3 %leaf_forward.1 = (bf16[8,128,128]{2,1,0:T(8,128)(2,1)S(1)}, bf16[8192,128]{1,0:T(8,128)(2,1)S(1)}, f32[8,128,128]{2,1,0:T(8,128)S(1)}) custom-call(s32[2,6]{1,0:T(2,128)} %bitcast.12, s32[1,1]{1,0:T(1,128)S(6)} %copy.13.count, bf16[2,128,128]{2,1,0:T(8,128)(2,1)} %bitcast.18, bf16[256,128]{1,0:T(8,128)(2,1)} %bitcast.19, bf16[1536,128]{1,0:T(8,128)(2,1)} %bitcast.16, ...), custom_call_target="tpu_custom_call" | custom-call | tf_op jit(solution)/shard_map/leaf_forward/pallas_call | solution.py:163
  3.5 8.8 %collective-permute-start = (bf16[8192,128]{1,0:T(8,128)(2,1)S(1)}, bf16[8192,128]{1,0:T(8,128)(2,1)S(1)}, u32[]{:S(2)}, u32[]{:S(2)}) collective-permute-start(bf16[8192,128]{1,0:T(8,128)(2,1)S(1)} %get-tuple-element.15.mine.store), channel_id=1, source_target_pairs={{0,4},{4,0},{1,5},{5,1},{2,6},{6,2},{3,7},{7,3},{8,12},{12,8},{9,1... | collective-permute-start | bytes 6291464 | tf_op jit(solution)/shard_map/ppermute | solution.py:374
  12.3 9.0 %all_to_all.40.received = bf16[8,128,128]{2,1,0:T(8,128)(2,1)S(1)} all-to-all(bf16[8,128,128]{2,1,0:T(8,128)(2,1)S(1)} %get-tuple-element.14), channel_id=1, replica_groups=mesh['group'=32,'pair'=2,'core'=2,'panel'=4] {'core','panel'}, dimensions={0} | all-to-all | bytes 524288 | tf_op jit(solution)/shard_map/all_to_all | solution.py:370
  21.3 0.0 collective-permute-done.other
  21.3 0.4 side_partials.2
  21.7 7.2 %all_to_all.41.received = bf16[4,128,128]{2,1,0:T(8,128)(2,1)S(1)} all-to-all(bf16[4,128,128]{2,1,0:T(8,128)(2,1)S(1)} %side_partials.2), channel_id=1, replica_groups=mesh['group'=32,'pair'=2,'core'=2,'panel'=4] {'panel'}, dimensions={0} | all-to-all | bytes 262144 | tf_op jit(solution)/shard_map/all_to_all | solution.py:370
  28.9 0.5 raise_terms.1
  29.4 8.5 %all_to_all.42.received = bf16[8,128,128]{2,1,0:T(8,128)(2,1)S(1)} all-to-all(bf16[8,128,128]{2,1,0:T(8,128)(2,1)S(1)} %get-tuple-element.17), channel_id=1, replica_groups=mesh['group'=32,'pair'=2,'core'=2,'panel'=4] {'pair','panel'}, dimensions={0} | all-to-all | bytes 524288 | tf_op jit(solution)/shard_map/all_to_all | solution.py:370
  37.9 0.5 side_partials.3
  38.5 8.7 %all_to_all.43.received = bf16[8,128,128]{2,1,0:T(8,128)(2,1)S(1)} all-to-all(bf16[8,128,128]{2,1,0:T(8,128)(2,1)S(1)} %side_partials.3), channel_id=1, replica_groups=mesh['group'=32,'pair'=2,'core'=2,'panel'=4] {'pair','panel'}, dimensions={0} | all-to-all | bytes 524288 | tf_op jit(solution)/shard_map/all_to_all | solution.py:370
  47.2 0.1 turned_sum.1
  47.3 8.5 %all_to_all.44.whole = bf16[8,128,128]{2,1,0:T(8,128)(2,1)S(1)} all-to-all(bf16[8,128,128]{2,1,0:T(8,128)(2,1)S(1)} %turned_sum.1), channel_id=1, replica_groups=mesh['group'=32,'pair'=2,'core'=2,'panel'=4] {'pair','panel'}, dimensions={0} | all-to-all | bytes 524288 | tf_op jit(solution)/shard_map/all_to_all | solution.py:370
  55.8 0.3 back_step.3
  56.1 8.5 %all_to_all.45.whole.mine = bf16[8,128,128]{2,1,0:T(8,128)(2,1)S(1)} all-to-all(bf16[8,128,128]{2,1,0:T(8,128)(2,1)S(1)} %back_step.3), channel_id=1, replica_groups=mesh['group'=32,'pair'=2,'core'=2,'panel'=4] {'pair','panel'}, dimensions={0} | all-to-all | bytes 524288 | tf_op jit(solution)/shard_map/all_to_all | solution.py:370
  64.6 0.3 back_step.4
  64.9 8.8 %collective-permute-start.1 = (bf16[8,128,128]{2,1,0:T(8,128)(2,1)S(1)}, bf16[8,128,128]{2,1,0:T(8,128)(2,1)S(1)}, u32[]{:S(2)}, u32[]{:S(2)}) collective-permute-start(bf16[8,128,128]{2,1,0:T(8,128)(2,1)S(1)} %all_to_all.45.whole.mine), channel_id=1, source_target_pairs={{0,4},{4,0},{1,5},{5,1},{2,6},{6,2},{3,7},{7,3},{8,12},{12,8},{9,1... | collective-permute-start | bytes 786440 | tf_op jit(solution)/shard_map/ppermute | solution.py:374
  73.7 7.5 %all_to_all.46.whole = bf16[4,128,128]{2,1,0:T(8,128)(2,1)S(1)} all-to-all(bf16[4,128,128]{2,1,0:T(8,128)(2,1)S(1)} %back_step.4), channel_id=1, replica_groups=mesh['group'=32,'pair'=2,'core'=2,'panel'=4] {'panel'}, dimensions={0} | all-to-all | bytes 262144 | tf_op jit(solution)/shard_map/all_to_all | solution.py:370
  81.2 0.0 copy-start
  81.2 0.0 collective-permute-done.1.other
  81.2 0.2 back_step.5
  81.5 10.1 %all_to_all.47.whole = bf16[8,128,128]{2,1,0:T(8,128)(2,1)S(1)} all-to-all(bf16[8,128,128]{2,1,0:T(8,128)(2,1)S(1)} %back_step.5), channel_id=1, replica_groups=mesh['group'=32,'pair'=2,'core'=2,'panel'=4] {'core','panel'}, dimensions={0} | all-to-all | bytes 524288 | tf_op jit(solution)/shard_map/all_to_all | solution.py:370
  91.5 0.0 copy-done
  91.5 1.8 %leaf_backward.1 = (bf16[2,128,128]{2,1,0:T(8,128)(2,1)}, bf16[128,128]{1,0:T(8,128)(2,1)}, bf16[128,128]{1,0:T(8,128)(2,1)}) custom-call(s32[2,6]{1,0:T(2,128)S(1)} %bitcast.13, s32[1,1]{1,0:T(1,128)S(6)} %copy.13.count, bf16[8,128,128]{2,1,0:T(8,128)(2,1)S(1)} %all_to_all.47.whole, bf16[8,128,128]{2,1,0:T(8,128)(2,1)S(1)} %all_to_all.45.whole.mine, ...), custom_call_target="tpu_custom_call" | custom-call | tf_op jit(solution)/shard_map/leaf_backward/pallas_call | solution.py:354
Async XLA Ops:
  3.5 17.8 %collective-permute-start = (bf16[8192,128]{1,0:T(8,128)(2,1)S(1)}, bf16[8192,128]{1,0:T(8,128)(2,1)S(1)}, u32[]{:S(2)}, u32[]{:S(2)}) collective-permute-start(bf16[8192,128]{1,0:T(8,128)(2,1)S(1)} %get-tuple-element.15.mine.store), channel_id=1, source_target_pairs={{0,4},{4,0},{1,5},{5,1},{2,6},{6,2},{3,7},{7,3},{8,12},{12,8},{9,1... | collective-permute-start | bytes 6291464 | tf_op jit(solution)/shard_map/ppermute | solution.py:374
  64.9 16.3 %collective-permute-start.1 = (bf16[8,128,128]{2,1,0:T(8,128)(2,1)S(1)}, bf16[8,128,128]{2,1,0:T(8,128)(2,1)S(1)}, u32[]{:S(2)}, u32[]{:S(2)}) collective-permute-start(bf16[8,128,128]{2,1,0:T(8,128)(2,1)S(1)} %all_to_all.45.whole.mine), channel_id=1, source_target_pairs={{0,4},{4,0},{1,5},{5,1},{2,6},{6,2},{3,7},{7,3},{8,12},{12,8},{9,1... | collective-permute-start | bytes 786440 | tf_op jit(solution)/shard_map/ppermute | solution.py:374
  81.2 10.3 %copy-start = (s32[1,1,2,6]{3,2,1,0:T(2,128)S(1)}, s32[1,1,2,6]{3,2,1,0:T(2,128)}, u32[]{:S(2)}) copy-start(s32[1,1,2,6]{3,2,1,0:T(2,128)} %param.13) | copy-start | bytes 148

commit v7 on v6

--- a/solution.py
+++ b/solution.py
@@ -105,16 +105,16 @@
             (side1, side1_v),
             (side2, side2_v),
         )
-        core = lax.axis_index("core")
-        total[...] = jnp.zeros_like(total)
-        loads[0].wait()
-        loads[1].wait()
         matrices = start_loads(
             more_sems,
             (inverse1, store.at[part("inverse1", of=inverse1)]),
             (panel1, store.at[part("panel1", of=panel1)]),
             (inverse2, store.at[part("inverse2", of=inverse2)]),
         )
+        core = lax.axis_index("core")
+        total[...] = jnp.zeros_like(total)
+        loads[0].wait()
+        loads[1].wait()
         solved = []
         for s in range(slots):
             live = jnp.where(s < count[0, 0], 1.0, 0.0)
@@ -312,25 +312,55 @@
     )(*operands)
 
 
-def leaf_backward(places, rows, count, whole, mine, other, store):
+def full_step(whole, pieces, second):
+    line, width = whole.shape[:2]
+    half = width // 2
+    height = 2 * line * width
+
+    def piece_rows(piece):
+        return slice(piece * height, (piece + 1) * height)
+
+    def kernel(whole, pieces, second, joined, pieces_v, sems):
+        loads = start_loads(
+            sems, *((pieces.at[at], pieces_v.at[at]) for at in map(piece_rows, range(2 * line)))
+        )
+        vectors = jnp.concatenate(
+            [whole[p, c * half : (c + 1) * half] for c in range(2) for p in range(line)], 1
+        )
+        joined[line:] = second[...]
+        for c in range(2):
+            for p in range(line):
+                loads[c * line + p].wait()
+                result = dot(vectors, pieces_v[piece_rows(c * line + p)])
+                joined[p, c * half : (c + 1) * half] = result.astype(BF16)
+
+    return pl.pallas_call(
+        kernel,
+        out_shape=jax.ShapeDtypeStruct((line + second.shape[0],) + whole.shape[1:], BF16),
+        in_specs=[VMEM, HBM, VMEM],
+        out_specs=VMEM,
+        scratch_shapes=[pltpu.VMEM(pieces.shape, BF16), pltpu.SemaphoreType.DMA((2 * line,))],
+        compiler_params=PARAMS,
+        name="full_step",
+    )(whole, *in_hbm(pieces), second)
+
+
+def leaf_backward(places, rows, count, mine, other, store):
     slots, touched = rows.shape
-    width = whole.shape[1]
+    width = mine.shape[1]
     half = width // 2
-    split = whole.shape[0]
-    line = split // 2
+    line = mine.shape[0] // 3
     own_rows, _ = places
 
-    def kernel(rows, count, whole, mine, other, store, sample, sample1, sample2, above):
+    def kernel(rows, count, mine, other, store, sample, sample1, sample2, above):
         core = lax.axis_index("core")
         here = pl.ds(pl.multiple_of(core * half, half), half)
         there = pl.ds(pl.multiple_of((1 - core) * half, half), half)
-        for c in range(2):
-            part = slice(c * half, (c + 1) * half)
-            for p in range(line):
-                for h in range(2):
-                    above[c * line + p, h * half : (h + 1) * half] = whole[h * line + p, part]
-                for z in range(2):
-                    at = (z + 1) * split + c * line + p
+        for z in range(3):
+            for c in range(2):
+                part = slice(c * half, (c + 1) * half)
+                for p in range(line):
+                    at = (2 * z + c) * line + p
                     above[at, here] = mine[z * line + p, part]
                     above[at, there] = other[z * line + p, part]
 
@@ -347,10 +377,10 @@
             sample[s] = result.T.astype(BF16)
         own = core * line + lax.axis_index("panel")
         sample1[...] = above[own].astype(F32).T.astype(BF16)
-        own = own + (lax.axis_index("pair") + 1) * split
+        own = own + (lax.axis_index("pair") + 1) * 2 * line
         sample2[...] = above[own].astype(F32).T.astype(BF16)
 
-    block = whole.shape[1:]
+    block = mine.shape[1:]
     return pl.pallas_call(
         kernel,
         out_shape=(
@@ -358,12 +388,12 @@
             jax.ShapeDtypeStruct(block, BF16),
             jax.ShapeDtypeStruct(block, BF16),
         ),
-        in_specs=[SMEM, SMEM] + [VMEM] * 4,
+        in_specs=[SMEM, SMEM] + [VMEM] * 3,
         out_specs=(VMEM,) * 3,
-        scratch_shapes=[pltpu.VMEM((split + 2 * mine.shape[0],) + block, BF16)],
+        scratch_shapes=[pltpu.VMEM((2 * mine.shape[0],) + block, BF16)],
         compiler_params=PARAMS,
         name="leaf_backward",
-    )(rows, count, whole, mine, other, store)
+    )(rows, count, mine, other, store)
 
 
 def exchange(blocks, axes):
@@ -397,6 +427,7 @@
     panel1_at, inverse2_at = places[0]["panel1"], places[0]["inverse2"]
     terms_at = places[0]["terms"]
 
+    pieces = lax.all_gather(inverse1, FIRST, axis=0, tiled=True)
     send1, store, keep = leaf_forward(
         places,
         live_count,
@@ -423,11 +454,9 @@
     )
     shifted = back_step(whole_second, store, other, panel1_at, first_blocks // 2, solved1_t)
     whole_shifted = exchange(shifted, LINE)
-    other_second = swapped(lax.optimization_barrier((whole_second, shifted))[0])
-    whole_shifted, other_second = lax.optimization_barrier((whole_shifted, other_second))
-    whole_first = exchange(back_step(whole_shifted, store, other, 0, first_blocks), FIRST)
+    joined = full_step(whole_shifted, pieces, whole_second)
     leaf_sample, sample1, sample2 = leaf_backward(
-        places, rows, live_count, whole_first, whole_second, other_second, store
+        places, rows, live_count, joined, swapped(joined), store
     )
     return (leaf_sample[None, None], sample1[None, None], sample2[None, None])
 

time: 93.8 us -> 112 us (1.19)
  blocking collectives: 67.9 us -> 51.5 us
  between operations: 1.36 us -> 14.8 us
  Pallas kernels: 6.48 us -> 17 us
  waiting for transfers between devices: 0.01 us -> 6.13 us
  starting transfers between devices: 17.6 us -> 22.1 us
    all_to_all x8 -> x6, blocking collectives: 67.9 us -> 51.5 us  [exchange(): return lax.all_to_all(blocks, axes, 0, 0, tiled=True)]
    all_to_all x0 -> x1, waiting for transfers between devices: none -> 4.76 us  [exchange(): return lax.all_to_all(blocks, axes, 0, 0, tiled=True)]
    pallas_call x3 -> x2, Pallas kernels: 0.86 us -> 4.45 us  [back_step(): pl.pallas_call(kernel, out_shape=jax.ShapeDtypeStruct((targets,) + whole....]
    all_to_all x0 -> x1, starting transfers between devices: none -> 3.45 us  [exchange(): return lax.all_to_all(blocks, axes, 0, 0, tiled=True)]
    pallas_call x2, Pallas kernels: 0.91 us -> 4.1 us  [side_partials(): pl.pallas_call(kernel, out_shape=jax.ShapeDtypeStruct((row_count // width...]
    pallas_call x0 -> x1, Pallas kernels: none -> 2.46 us  [full_step(): pl.pallas_call(kernel, out_shape=jax.ShapeDtypeStruct((line + second.shap...]
    pallas_call x1, Pallas kernels: 0.52 us -> 2.15 us  [raise_terms(): pl.pallas_call(kernel, out_shape=(jax.ShapeDtypeStruct(keep.shape, BF16),...]
    ppermute x2, waiting for transfers between devices: 0.01 us -> 1.33 us  [swapped(): return lax.ppermute(array, 'core', [(0, 1), (1, 0)])]
  transfers between devices with their start and end apart: 2 -> 4, of which waited for: 0 -> 2; matrix products, arithmetic and copies ran while one was open for 0% -> 0% of each run, Pallas kernels for 0% -> 10%
where the time goes in v7:
time: 112 us
  blocking collectives  51.5 us (46%)
  starting transfers between devices  22.1 us (20%)
  Pallas kernels  17 us (15%)
  between operations  14.8 us (13%)
  waiting for transfers between devices  6.13 us (5%)
    all_to_all x6, blocking collectives, exchange(): return lax.all_to_all(blocks, axes, 0, 0, tiled=True)  51.5 us
    ppermute x2, starting transfers between devices, swapped(): return lax.ppermute(array, 'core', [(0, 1), (1, 0)])  18.6 us
    all_to_all x1, waiting for transfers between devices, exchange(): return lax.all_to_all(blocks, axes, 0, 0, tiled=True)  4.76 us
    pallas_call x2, Pallas kernels, back_step(): pl.pallas_call(kernel, out_shape=jax.ShapeDtypeStruct((targets,) + whole....  4.45 us
    pallas_call x2, Pallas kernels, side_partials(): pl.pallas_call(kernel, out_shape=jax.ShapeDtypeStruct((row_count // width...  4.1 us
    all_to_all x1, starting transfers between devices, exchange(): return lax.all_to_all(blocks, axes, 0, 0, tiled=True)  3.45 us
    pallas_call x1, Pallas kernels, full_step(): pl.pallas_call(kernel, out_shape=jax.ShapeDtypeStruct((line + second.shap...  2.46 us
  transfers between devices with their start and end apart: 4, of which 2 were waited for; matrix products, arithmetic and copies ran while one was open for 0% of the time, Pallas kernels for 10%

profile of v7, /device:TPU:1, one launch (start us, length us, event | category | flops | bytes accessed | tf_op | source)
XLA Modules:
  0.0 111.5 jit_solution(10745762014921689385)
XLA Ops:
  7.2 0.0 all-gather.3.cloned.1.call-start
  7.9 1.9 %leaf_forward.1 = (bf16[8,128,128]{2,1,0:T(8,128)(2,1)S(1)}, bf16[8192,128]{1,0:T(8,128)(2,1)S(1)}, f32[8,128,128]{2,1,0:T(8,128)S(1)}) custom-call(s32[2,6]{1,0:T(2,128)} %bitcast.13, s32[1,1]{1,0:T(1,128)S(6)} %copy.13.count, bf16[2,128,128]{2,1,0:T(8,128)(2,1)} %bitcast.20, bf16[256,128]{1,0:T(8,128)(2,1)} %bitcast.21, bf16[1536,128]{1,0:T(8,128)(2,1)} %bitcast.19, ...), custom_call_target="tpu_custom_call" | custom-call | tf_op jit(solution)/shard_map/leaf_forward/pallas_call | solution.py:163
  9.8 8.8 %collective-permute-start = (bf16[8192,128]{1,0:T(8,128)(2,1)S(1)}, bf16[8192,128]{1,0:T(8,128)(2,1)}, u32[]{:S(2)}, u32[]{:S(2)}) collective-permute-start(bf16[8192,128]{1,0:T(8,128)(2,1)S(1)} %get-tuple-element.12.mine.store), channel_id=1, source_target_pairs={{0,4},{4,0},{1,5},{5,1},{2,6},{6,2},{3,7},{7,3},{8,12},{12,8},{9,1... | collective-permute-start | bytes 6291464 | tf_op jit(solution)/shard_map/ppermute | solution.py:404
  18.6 0.0 all-gather.3.cloned.1.call-update
  18.6 9.0 %all_to_all.35.received = bf16[8,128,128]{2,1,0:T(8,128)(2,1)S(1)} all-to-all(bf16[8,128,128]{2,1,0:T(8,128)(2,1)S(1)} %get-tuple-element.11), channel_id=1, replica_groups=mesh['group'=32,'pair'=2,'core'=2,'panel'=4] {'core','panel'}, dimensions={0} | all-to-all | bytes 524288 | tf_op jit(solution)/shard_map/all_to_all | solution.py:400
  27.6 0.0 collective-permute-done.other
  27.6 2.0 %side_partials.2 = bf16[4,128,128]{2,1,0:T(8,128)(2,1)S(1)} custom-call(bf16[8,128,128]{2,1,0:T(8,128)(2,1)S(1)} %all_to_all.35.received, bf16[8192,128]{1,0:T(8,128)(2,1)S(1)} %get-tuple-element.12.mine.store, bf16[8192,128]{1,0:T(8,128)(2,1)} %collective-permute-done.other), custom_call_target="tpu_custom_call" | custom-call | tf_op jit(solution)/shard_map/side_partials/pallas_call | solution.py:225
  29.6 8.1 %all_to_all.36.received = bf16[4,128,128]{2,1,0:T(8,128)(2,1)S(1)} all-to-all(bf16[4,128,128]{2,1,0:T(8,128)(2,1)S(1)} %side_partials.2), channel_id=1, replica_groups=mesh['group'=32,'pair'=2,'core'=2,'panel'=4] {'panel'}, dimensions={0} | all-to-all | bytes 262144 | tf_op jit(solution)/shard_map/all_to_all | solution.py:400
  37.6 2.2 %raise_terms.1 = (bf16[8,128,128]{2,1,0:T(8,128)(2,1)S(1)}, bf16[128,128]{1,0:T(8,128)(2,1)S(1)}) custom-call(bf16[4,128,128]{2,1,0:T(8,128)(2,1)S(1)} %all_to_all.36.received, f32[8,128,128]{2,1,0:T(8,128)S(1)} %get-tuple-element.13.keep, bf16[8192,128]{1,0:T(8,128)(2,1)S(1)} %get-tuple-element.12.mine.store, bf16[8192,128]{1,0:T(8,128)(2,1)} %collective-permute-done.other), custom_call_target="tpu_custom_call" | custom-call | tf_op jit(solution)/shard_map/raise_terms/pallas_call | solution.py:249
  39.8 8.5 %all_to_all.37.received = bf16[8,128,128]{2,1,0:T(8,128)(2,1)S(1)} all-to-all(bf16[8,128,128]{2,1,0:T(8,128)(2,1)S(1)} %get-tuple-element.14), channel_id=1, replica_groups=mesh['group'=32,'pair'=2,'core'=2,'panel'=4] {'pair','panel'}, dimensions={0} | all-to-all | bytes 524288 | tf_op jit(solution)/shard_map/all_to_all | solution.py:400
  48.3 2.1 %side_partials.3 = bf16[8,128,128]{2,1,0:T(8,128)(2,1)S(1)} custom-call(bf16[8,128,128]{2,1,0:T(8,128)(2,1)S(1)} %all_to_all.37.received, bf16[8192,128]{1,0:T(8,128)(2,1)S(1)} %get-tuple-element.12.mine.store, bf16[8192,128]{1,0:T(8,128)(2,1)} %collective-permute-done.other), custom_call_target="tpu_custom_call" | custom-call | tf_op jit(solution)/shard_map/side_partials/pallas_call | solution.py:225
  50.4 9.0 %all_to_all.38.received = bf16[8,128,128]{2,1,0:T(8,128)(2,1)S(1)} all-to-all(bf16[8,128,128]{2,1,0:T(8,128)(2,1)S(1)} %side_partials.3), channel_id=1, replica_groups=mesh['group'=32,'pair'=2,'core'=2,'panel'=4] {'pair','panel'}, dimensions={0} | all-to-all | bytes 524288 | tf_op jit(solution)/shard_map/all_to_all | solution.py:400
  59.4 0.1 turned_sum.1
  59.5 8.5 %all_to_all.39.whole = bf16[8,128,128]{2,1,0:T(8,128)(2,1)S(1)} all-to-all(bf16[8,128,128]{2,1,0:T(8,128)(2,1)S(1)} %turned_sum.1), channel_id=1, replica_groups=mesh['group'=32,'pair'=2,'core'=2,'panel'=4] {'pair','panel'}, dimensions={0} | all-to-all | bytes 524288 | tf_op jit(solution)/shard_map/all_to_all | solution.py:400
  68.0 1.9 %back_step.2 = bf16[8,128,128]{2,1,0:T(8,128)(2,1)S(1)} custom-call(bf16[8,128,128]{2,1,0:T(8,128)(2,1)S(1)} %all_to_all.39.whole, bf16[8192,128]{1,0:T(8,128)(2,1)S(1)} %get-tuple-element.12.mine.store, bf16[8192,128]{1,0:T(8,128)(2,1)} %collective-permute-done.other), custom_call_target="tpu_custom_call" | custom-call | tf_op jit(solution)/shard_map/back_step/pallas_call | solution.py:305
  69.9 8.5 %all_to_all.40.whole.second = bf16[8,128,128]{2,1,0:T(8,128)(2,1)S(1)} all-to-all(bf16[8,128,128]{2,1,0:T(8,128)(2,1)S(1)} %back_step.2), channel_id=1, replica_groups=mesh['group'=32,'pair'=2,'core'=2,'panel'=4] {'pair','panel'}, dimensions={0} | all-to-all | bytes 524288 | tf_op jit(solution)/shard_map/all_to_all | solution.py:400
  78.4 2.5 %back_step.3 = bf16[4,128,128]{2,1,0:T(8,128)(2,1)} custom-call(bf16[8,128,128]{2,1,0:T(8,128)(2,1)S(1)} %all_to_all.40.whole.second, bf16[8192,128]{1,0:T(8,128)(2,1)S(1)} %get-tuple-element.12.mine.store, bf16[8192,128]{1,0:T(8,128)(2,1)} %collective-permute-done.other, bf16[128,128]{1,0:T(8,128)(2,1)S(1)} %get-tuple-element.15.rest_0_), custom_call_target="tpu_custom_call" | custom-call | tf_op jit(solution)/shard_map/back_step/pallas_call | solution.py:305
  81.0 0.0 copy-start
  81.0 3.5 %all-to-all-start.6 = ((bf16[4,128,128]{2,1,0:T(8,128)(2,1)}), bf16[4,128,128]{2,1,0:T(8,128)(2,1)S(1)}, u32[]{:S(2)}, u32[]{:S(2)}) async-start(bf16[4,128,128]{2,1,0:T(8,128)(2,1)} %back_step.3), calls=%async_computation.6 | async-start | bytes 262144 | tf_op jit(solution)/shard_map/all_to_all | solution.py:400
  84.4 0.0 all-gather.3.cloned.1.call-done
  84.5 4.8 %all-to-all-done.6.whole = bf16[4,128,128]{2,1,0:T(8,128)(2,1)S(1)} async-done(((bf16[4,128,128]{2,1,0:T(8,128)(2,1)}), bf16[4,128,128]{2,1,0:T(8,128)(2,1)S(1)}, u32[]{:S(2)}, u32[]{:S(2)}) %all-to-all-start.6) | async-done | bytes 131104 | tf_op jit(solution)/shard_map/all_to_all | solution.py:400
  89.2 2.5 %full_step.1.mine = bf16[12,128,128]{2,1,0:T(8,128)(2,1)S(1)} custom-call(bf16[4,128,128]{2,1,0:T(8,128)(2,1)S(1)} %all-to-all-done.6.whole, bf16[8192,128]{1,0:T(8,128)(2,1)} %bitcast.15, bf16[8,128,128]{2,1,0:T(8,128)(2,1)S(1)} %all_to_all.40.whole.second), custom_call_target="tpu_custom_call" | custom-call | tf_op jit(solution)/shard_map/full_step/pallas_call | solution.py:337
  91.7 9.8 %collective-permute-start.1 = (bf16[12,128,128]{2,1,0:T(8,128)(2,1)S(1)}, bf16[12,128,128]{2,1,0:T(8,128)(2,1)S(1)}, u32[]{:S(2)}, u32[]{:S(2)}) collective-permute-start(bf16[12,128,128]{2,1,0:T(8,128)(2,1)S(1)} %full_step.1.mine), channel_id=1, source_target_pairs={{0,4},{4,0},{1,5},{5,1},{2,6},{6,2},{3,7},{7,3},{8,12},{12,8},{9,1... | collective-permute-start | bytes 1179656 | tf_op jit(solution)/shard_map/ppermute | solution.py:404
  101.5 1.3 %collective-permute-done.1.other = bf16[12,128,128]{2,1,0:T(8,128)(2,1)S(1)} collective-permute-done((bf16[12,128,128]{2,1,0:T(8,128)(2,1)S(1)}, bf16[12,128,128]{2,1,0:T(8,128)(2,1)S(1)}, u32[]{:S(2)}, u32[]{:S(2)}) %collective-permute-start.1) | collective-permute-done | bytes 393248 | tf_op jit(solution)/shard_map/ppermute | solution.py:404
  102.8 0.0 copy-done
  102.8 1.8 %leaf_backward.1 = (bf16[2,128,128]{2,1,0:T(8,128)(2,1)}, bf16[128,128]{1,0:T(8,128)(2,1)}, bf16[128,128]{1,0:T(8,128)(2,1)}) custom-call(s32[2,6]{1,0:T(2,128)S(1)} %bitcast.14, s32[1,1]{1,0:T(1,128)S(6)} %copy.13.count, bf16[12,128,128]{2,1,0:T(8,128)(2,1)S(1)} %full_step.1.mine, bf16[12,128,128]{2,1,0:T(8,128)(2,1)S(1)} %collective-permute-done.1.other, ...), custom_call_target="tpu_custom_call" | custom-call | tf_op jit(solution)/shard_map/leaf_backward/pallas_call | solution.py:384
Async XLA Ops:
  7.2 77.3 %all-gather.3.cloned.1.call-start = ((), (), s32[]{:S(2)}) async-start(), calls=%async_computation.7 | async-start | bytes 2359296 | tf_op jit(solution)/shard_map/all_gather | solution.py:430
  9.8 17.8 %collective-permute-start = (bf16[8192,128]{1,0:T(8,128)(2,1)S(1)}, bf16[8192,128]{1,0:T(8,128)(2,1)}, u32[]{:S(2)}, u32[]{:S(2)}) collective-permute-start(bf16[8192,128]{1,0:T(8,128)(2,1)S(1)} %get-tuple-element.12.mine.store), channel_id=1, source_target_pairs={{0,4},{4,0},{1,5},{5,1},{2,6},{6,2},{3,7},{7,3},{8,12},{12,8},{9,1... | collective-permute-start | bytes 6291464 | tf_op jit(solution)/shard_map/ppermute | solution.py:404
  81.0 21.9 %copy-start = (s32[1,1,2,6]{3,2,1,0:T(2,128)S(1)}, s32[1,1,2,6]{3,2,1,0:T(2,128)}, u32[]{:S(2)}) copy-start(s32[1,1,2,6]{3,2,1,0:T(2,128)} %param.13) | copy-start | bytes 148
  81.0 8.3 %all-to-all-start.6 = ((bf16[4,128,128]{2,1,0:T(8,128)(2,1)}), bf16[4,128,128]{2,1,0:T(8,128)(2,1)S(1)}, u32[]{:S(2)}, u32[]{:S(2)}) async-start(bf16[4,128,128]{2,1,0:T(8,128)(2,1)} %back_step.3), calls=%async_computation.6 | async-start | bytes 262144 | tf_op jit(solution)/shard_map/all_to_all | solution.py:400
  91.7 11.2 %collective-permute-start.1 = (bf16[12,128,128]{2,1,0:T(8,128)(2,1)S(1)}, bf16[12,128,128]{2,1,0:T(8,128)(2,1)S(1)}, u32[]{:S(2)}, u32[]{:S(2)}) collective-permute-start(bf16[12,128,128]{2,1,0:T(8,128)(2,1)S(1)} %full_step.1.mine), channel_id=1, source_target_pairs={{0,4},{4,0},{1,5},{5,1},{2,6},{6,2},{3,7},{7,3},{8,12},{12,8},{9,1... | collective-permute-start | bytes 1179656 | tf_op jit(solution)/shard_map/ppermute | solution.py:404
Sparse Core Ops, SparseCore 0:
  18.7 31.2 all-gather.2

commit v8 on v6

--- a/solution.py
+++ b/solution.py
@@ -105,16 +105,16 @@
             (side1, side1_v),
             (side2, side2_v),
         )
-        core = lax.axis_index("core")
-        total[...] = jnp.zeros_like(total)
-        loads[0].wait()
-        loads[1].wait()
         matrices = start_loads(
             more_sems,
             (inverse1, store.at[part("inverse1", of=inverse1)]),
             (panel1, store.at[part("panel1", of=panel1)]),
             (inverse2, store.at[part("inverse2", of=inverse2)]),
         )
+        core = lax.axis_index("core")
+        total[...] = jnp.zeros_like(total)
+        loads[0].wait()
+        loads[1].wait()
         solved = []
         for s in range(slots):
             live = jnp.where(s < count[0, 0], 1.0, 0.0)
@@ -411,7 +411,8 @@
         inverse2,
     )
     other = swapped(store)
-    partial1 = side_partials(exchange(send1, FIRST), store, other, 0, rows1)
+    summed1 = exchange(send1, FIRST).astype(F32).sum(axis=0, keepdims=True)
+    partial1 = side_partials(summed1, store, other, 0, rows1)
     raised, solved1_t = raise_terms(
         exchange(partial1, LINE), keep, store, other, panel1_at, rows2, terms_at
     )
@@ -424,8 +425,10 @@
     shifted = back_step(whole_second, store, other, panel1_at, first_blocks // 2, solved1_t)
     whole_shifted = exchange(shifted, LINE)
     other_second = swapped(lax.optimization_barrier((whole_second, shifted))[0])
-    whole_shifted, other_second = lax.optimization_barrier((whole_shifted, other_second))
-    whole_first = exchange(back_step(whole_shifted, store, other, 0, first_blocks), FIRST)
+    sample1_t, other_second = lax.optimization_barrier(
+        (back_step(whole_shifted, store, other, 0, first_blocks), other_second)
+    )
+    whole_first = exchange(sample1_t, FIRST)
     leaf_sample, sample1, sample2 = leaf_backward(
         places, rows, live_count, whole_first, whole_second, other_second, store
     )

time: 93.8 us -> 93.5 us (level)
  no operation moved by 1% of the time
where the time goes in v8:
time: 93.5 us; the launch traced here: 93 us
  blocking collectives  67.9 us (73%)
  starting transfers between devices  17.6 us (19%)
  Pallas kernels  6.12 us (7%)
  between operations  1.37 us (1%)
    all_to_all x8, blocking collectives, exchange(): return lax.all_to_all(blocks, axes, 0, 0, tiled=True)  67.9 us
    ppermute x2, starting transfers between devices, swapped(): return lax.ppermute(array, 'core', [(0, 1), (1, 0)])  17.6 us
    pallas_call x1, Pallas kernels, leaf_forward(): pl.pallas_call(kernel, out_shape=(jax.ShapeDtypeStruct((first_blocks,) +...  1.92 us
  transfers between devices with their start and end apart: 2, of which 0 were waited for; matrix products, arithmetic and copies ran while one was open for 0% of the time, Pallas kernels for 0%

profile of v8, /device:TPU:1, one launch (start us, length us, event | category | flops | bytes accessed | tf_op | source)
XLA Modules:
  0.0 93.0 jit_solution(10210410261753899899)
XLA Ops:
  1.3 1.9 %leaf_forward.1 = (bf16[8,128,128]{2,1,0:T(8,128)(2,1)S(1)}, bf16[8192,128]{1,0:T(8,128)(2,1)S(1)}, f32[8,128,128]{2,1,0:T(8,128)S(1)}) custom-call(s32[2,6]{1,0:T(2,128)} %bitcast.14, s32[1,1]{1,0:T(1,128)S(6)} %copy.13.count, bf16[2,128,128]{2,1,0:T(8,128)(2,1)} %bitcast.20, bf16[256,128]{1,0:T(8,128)(2,1)} %bitcast.21, bf16[1536,128]{1,0:T(8,128)(2,1)} %bitcast.18, ...), custom_call_target="tpu_custom_call" | custom-call | tf_op jit(solution)/shard_map/leaf_forward/pallas_call | solution.py:163
  3.2 8.8 %collective-permute-start = (bf16[8192,128]{1,0:T(8,128)(2,1)S(1)}, bf16[8192,128]{1,0:T(8,128)(2,1)S(1)}, u32[]{:S(2)}, u32[]{:S(2)}) collective-permute-start(bf16[8192,128]{1,0:T(8,128)(2,1)S(1)} %get-tuple-element.15.mine.store), channel_id=1, source_target_pairs={{0,4},{4,0},{1,5},{5,1},{2,6},{6,2},{3,7},{7,3},{8,12},{12,8},{9,1... | collective-permute-start | bytes 6291464 | tf_op jit(solution)/shard_map/ppermute | solution.py:374
  12.0 9.0 %all_to_all.40 = bf16[8,128,128]{2,1,0:T(8,128)(2,1)S(1)} all-to-all(bf16[8,128,128]{2,1,0:T(8,128)(2,1)S(1)} %get-tuple-element.14), channel_id=1, replica_groups=mesh['group'=32,'pair'=2,'core'=2,'panel'=4] {'core','panel'}, dimensions={0} | all-to-all | bytes 524288 | tf_op jit(solution)/shard_map/all_to_all | solution.py:370
  21.0 0.0 collective-permute-done.other
  21.0 0.4 side_partials.2
  21.4 7.2 %all_to_all.41.received = bf16[4,128,128]{2,1,0:T(8,128)(2,1)S(1)} all-to-all(bf16[4,128,128]{2,1,0:T(8,128)(2,1)S(1)} %side_partials.2), channel_id=1, replica_groups=mesh['group'=32,'pair'=2,'core'=2,'panel'=4] {'panel'}, dimensions={0} | all-to-all | bytes 262144 | tf_op jit(solution)/shard_map/all_to_all | solution.py:370
  28.6 0.5 raise_terms.1
  29.1 8.5 %all_to_all.42.received = bf16[8,128,128]{2,1,0:T(8,128)(2,1)S(1)} all-to-all(bf16[8,128,128]{2,1,0:T(8,128)(2,1)S(1)} %get-tuple-element.17), channel_id=1, replica_groups=mesh['group'=32,'pair'=2,'core'=2,'panel'=4] {'pair','panel'}, dimensions={0} | all-to-all | bytes 524288 | tf_op jit(solution)/shard_map/all_to_all | solution.py:370
  37.6 0.5 side_partials.3
  38.1 8.7 %all_to_all.43.received = bf16[8,128,128]{2,1,0:T(8,128)(2,1)S(1)} all-to-all(bf16[8,128,128]{2,1,0:T(8,128)(2,1)S(1)} %side_partials.3), channel_id=1, replica_groups=mesh['group'=32,'pair'=2,'core'=2,'panel'=4] {'pair','panel'}, dimensions={0} | all-to-all | bytes 524288 | tf_op jit(solution)/shard_map/all_to_all | solution.py:370
  46.8 0.1 turned_sum.1
  47.0 8.5 %all_to_all.44.whole = bf16[8,128,128]{2,1,0:T(8,128)(2,1)S(1)} all-to-all(bf16[8,128,128]{2,1,0:T(8,128)(2,1)S(1)} %turned_sum.1), channel_id=1, replica_groups=mesh['group'=32,'pair'=2,'core'=2,'panel'=4] {'pair','panel'}, dimensions={0} | all-to-all | bytes 524288 | tf_op jit(solution)/shard_map/all_to_all | solution.py:370
  55.4 0.3 back_step.3
  55.8 8.5 %all_to_all.45.whole.mine = bf16[8,128,128]{2,1,0:T(8,128)(2,1)S(1)} all-to-all(bf16[8,128,128]{2,1,0:T(8,128)(2,1)S(1)} %back_step.3), channel_id=1, replica_groups=mesh['group'=32,'pair'=2,'core'=2,'panel'=4] {'pair','panel'}, dimensions={0} | all-to-all | bytes 524288 | tf_op jit(solution)/shard_map/all_to_all | solution.py:370
  64.3 0.3 back_step.4
  64.6 8.8 %collective-permute-start.1 = (bf16[8,128,128]{2,1,0:T(8,128)(2,1)S(1)}, bf16[8,128,128]{2,1,0:T(8,128)(2,1)S(1)}, u32[]{:S(2)}, u32[]{:S(2)}) collective-permute-start(bf16[8,128,128]{2,1,0:T(8,128)(2,1)S(1)} %all_to_all.45.whole.mine), channel_id=1, source_target_pairs={{0,4},{4,0},{1,5},{5,1},{2,6},{6,2},{3,7},{7,3},{8,12},{12,8},{9,1... | collective-permute-start | bytes 786440 | tf_op jit(solution)/shard_map/ppermute | solution.py:374
  73.4 7.5 %all_to_all.46.whole = bf16[4,128,128]{2,1,0:T(8,128)(2,1)S(1)} all-to-all(bf16[4,128,128]{2,1,0:T(8,128)(2,1)S(1)} %back_step.4), channel_id=1, replica_groups=mesh['group'=32,'pair'=2,'core'=2,'panel'=4] {'panel'}, dimensions={0} | all-to-all | bytes 262144 | tf_op jit(solution)/shard_map/all_to_all | solution.py:370
  80.9 0.0 copy-start
  80.9 0.2 back_step.5
  81.1 0.0 collective-permute-done.1.other
  81.1 10.1 %all_to_all.47.whole = bf16[8,128,128]{2,1,0:T(8,128)(2,1)S(1)} all-to-all(bf16[8,128,128]{2,1,0:T(8,128)(2,1)S(1)} %back_step.5), channel_id=1, replica_groups=mesh['group'=32,'pair'=2,'core'=2,'panel'=4] {'core','panel'}, dimensions={0} | all-to-all | bytes 524288 | tf_op jit(solution)/shard_map/all_to_all | solution.py:370
  91.2 0.0 copy-done
  91.2 1.8 %leaf_backward.1 = (bf16[2,128,128]{2,1,0:T(8,128)(2,1)}, bf16[128,128]{1,0:T(8,128)(2,1)}, bf16[128,128]{1,0:T(8,128)(2,1)}) custom-call(s32[2,6]{1,0:T(2,128)S(1)} %bitcast.15, s32[1,1]{1,0:T(1,128)S(6)} %copy.13.count, bf16[8,128,128]{2,1,0:T(8,128)(2,1)S(1)} %all_to_all.47.whole, bf16[8,128,128]{2,1,0:T(8,128)(2,1)S(1)} %all_to_all.45.whole.mine, ...), custom_call_target="tpu_custom_call" | custom-call | tf_op jit(solution)/shard_map/leaf_backward/pallas_call | solution.py:354
  (1 shorter events, 0.0 us)
Async XLA Ops:
  3.2 17.8 %collective-permute-start = (bf16[8192,128]{1,0:T(8,128)(2,1)S(1)}, bf16[8192,128]{1,0:T(8,128)(2,1)S(1)}, u32[]{:S(2)}, u32[]{:S(2)}) collective-permute-start(bf16[8192,128]{1,0:T(8,128)(2,1)S(1)} %get-tuple-element.15.mine.store), channel_id=1, source_target_pairs={{0,4},{4,0},{1,5},{5,1},{2,6},{6,2},{3,7},{7,3},{8,12},{12,8},{9,1... | collective-permute-start | bytes 6291464 | tf_op jit(solution)/shard_map/ppermute | solution.py:374
  64.6 16.6 %collective-permute-start.1 = (bf16[8,128,128]{2,1,0:T(8,128)(2,1)S(1)}, bf16[8,128,128]{2,1,0:T(8,128)(2,1)S(1)}, u32[]{:S(2)}, u32[]{:S(2)}) collective-permute-start(bf16[8,128,128]{2,1,0:T(8,128)(2,1)S(1)} %all_to_all.45.whole.mine), channel_id=1, source_target_pairs={{0,4},{4,0},{1,5},{5,1},{2,6},{6,2},{3,7},{7,3},{8,12},{12,8},{9,1... | collective-permute-start | bytes 786440 | tf_op jit(solution)/shard_map/ppermute | solution.py:374
  80.9 10.3 %copy-start = (s32[1,1,2,6]{3,2,1,0:T(2,128)S(1)}, s32[1,1,2,6]{3,2,1,0:T(2,128)}, u32[]{:S(2)}) copy-start(s32[1,1,2,6]{3,2,1,0:T(2,128)} %param.13) | copy-start | bytes 148

commit v9 on v8

--- a/solution.py
+++ b/solution.py
@@ -135,10 +135,7 @@
         total[own] -= side1_v[...].astype(F32)
         own = own + (lax.axis_index("pair") + 1) * first_blocks
         total[own] -= side2_v[...].astype(F32)
-        for p in range(line):
-            zero, one = packed(total[p], total[line + p])
-            send[p] = zero.astype(BF16)
-            send[line + p] = one.astype(BF16)
+        send[...] = total[:first_blocks].astype(BF16)
         for z in range(2):
             for p in range(line):
                 at = (z + 1) * first_blocks + p
@@ -210,6 +207,30 @@
         )
         parts.append(dot(wide, weights))
     return parts
+
+
+def first_partials(received, mine, row_count):
+    width = mine.shape[1]
+    line = received.shape[0] // 2
+
+    def kernel(received, mine, partials):
+        side = -received[...].astype(F32).sum(axis=0)
+        product = dot(mine[:row_count], side.astype(BF16))
+        for p in range(line):
+            lower = product[p * width : (p + 1) * width]
+            upper = product[(line + p) * width : (line + p + 1) * width]
+            zero, one = packed(lower, upper)
+            partials[p] = zero.astype(BF16)
+            partials[line + p] = one.astype(BF16)
+
+    return pl.pallas_call(
+        kernel,
+        out_shape=jax.ShapeDtypeStruct(received.shape, BF16),
+        in_specs=[VMEM] * 2,
+        out_specs=VMEM,
+        compiler_params=PARAMS,
+        name="first_partials",
+    )(received, mine)
 
 
 def side_partials(received, mine, other, first_row, row_count):
@@ -411,10 +432,9 @@
         inverse2,
     )
     other = swapped(store)
-    summed1 = exchange(send1, FIRST).astype(F32).sum(axis=0, keepdims=True)
-    partial1 = side_partials(summed1, store, other, 0, rows1)
+    partial1 = first_partials(exchange(send1, FIRST), store, rows1)
     raised, solved1_t = raise_terms(
-        exchange(partial1, LINE), keep, store, other, panel1_at, rows2, terms_at
+        exchange(partial1, FIRST), keep, store, other, panel1_at, rows2, terms_at
     )
     partial2 = side_partials(exchange(raised, CHIPS), store, other, inverse2_at, rows2)
     whole_solved = exchange(turned_sum(exchange(partial2, CHIPS)), CHIPS)

time: 93.5 us -> 94.9 us (1.015)
  blocking collectives: 67.9 us -> 70.7 us
  starting transfers between devices: 17.6 us -> 16.3 us
    all_to_all x8, blocking collectives: 67.9 us -> 70.7 us  [exchange(): return lax.all_to_all(blocks, axes, 0, 0, tiled=True)]
    ppermute x2, starting transfers between devices: 17.6 us -> 16.3 us  [swapped(): return lax.ppermute(array, 'core', [(0, 1), (1, 0)])]
  transfers between devices with their start and end apart: 2 -> 2, of which waited for: 0 -> 0; matrix products, arithmetic and copies ran while one was open for 0% -> 0% of each run, Pallas kernels for 0% -> 1%
where the time goes in v9:
time: 94.9 us; the launch traced here: 94.4 us
  blocking collectives  70.7 us (74%)
  starting transfers between devices  16.3 us (17%)
  Pallas kernels  6.04 us (6%)
  between operations  1.36 us (1%)
    all_to_all x8, blocking collectives, exchange(): return lax.all_to_all(blocks, axes, 0, 0, tiled=True)  70.7 us
    ppermute x2, starting transfers between devices, swapped(): return lax.ppermute(array, 'core', [(0, 1), (1, 0)])  16.3 us
  transfers between devices with their start and end apart: 2, of which 0 were waited for; matrix products, arithmetic and copies ran while one was open for 0% of the time, Pallas kernels for 1%

profile of v9, /device:TPU:1, one launch (start us, length us, event | category | flops | bytes accessed | tf_op | source)
XLA Modules:
  0.0 94.4 jit_solution(4596844351852836083)
XLA Ops:
  1.3 1.9 %leaf_forward.1 = (bf16[8,128,128]{2,1,0:T(8,128)(2,1)S(1)}, bf16[8192,128]{1,0:T(8,128)(2,1)S(1)}, f32[8,128,128]{2,1,0:T(8,128)S(1)}) custom-call(s32[2,6]{1,0:T(2,128)} %bitcast.12, s32[1,1]{1,0:T(1,128)S(6)} %copy.13.count, bf16[2,128,128]{2,1,0:T(8,128)(2,1)} %bitcast.18, bf16[256,128]{1,0:T(8,128)(2,1)} %bitcast.19, bf16[1536,128]{1,0:T(8,128)(2,1)} %bitcast.16, ...), custom_call_target="tpu_custom_call" | custom-call | tf_op jit(solution)/shard_map/leaf_forward/pallas_call | solution.py:160
  3.2 8.8 %collective-permute-start = (bf16[8192,128]{1,0:T(8,128)(2,1)S(1)}, bf16[8192,128]{1,0:T(8,128)(2,1)S(1)}, u32[]{:S(2)}, u32[]{:S(2)}) collective-permute-start(bf16[8192,128]{1,0:T(8,128)(2,1)S(1)} %get-tuple-element.15.mine.store), channel_id=1, source_target_pairs={{0,4},{4,0},{1,5},{5,1},{2,6},{6,2},{3,7},{7,3},{8,12},{12,8},{9,1... | collective-permute-start | bytes 6291464 | tf_op jit(solution)/shard_map/ppermute | solution.py:395
  12.0 9.0 %all_to_all.40.received = bf16[8,128,128]{2,1,0:T(8,128)(2,1)S(1)} all-to-all(bf16[8,128,128]{2,1,0:T(8,128)(2,1)S(1)} %get-tuple-element.14), channel_id=1, replica_groups=mesh['group'=32,'pair'=2,'core'=2,'panel'=4] {'core','panel'}, dimensions={0} | all-to-all | bytes 524288 | tf_op jit(solution)/shard_map/all_to_all | solution.py:391
  20.9 0.3 first_partials.1
  21.2 9.8 %all_to_all.41.received = bf16[8,128,128]{2,1,0:T(8,128)(2,1)S(1)} all-to-all(bf16[8,128,128]{2,1,0:T(8,128)(2,1)S(1)} %first_partials.1), channel_id=1, replica_groups=mesh['group'=32,'pair'=2,'core'=2,'panel'=4] {'core','panel'}, dimensions={0} | all-to-all | bytes 524288 | tf_op jit(solution)/shard_map/all_to_all | solution.py:391
  31.0 0.0 collective-permute-done.other
  31.0 0.5 raise_terms.1
  31.6 8.5 %all_to_all.42.received = bf16[8,128,128]{2,1,0:T(8,128)(2,1)S(1)} all-to-all(bf16[8,128,128]{2,1,0:T(8,128)(2,1)S(1)} %get-tuple-element.17), channel_id=1, replica_groups=mesh['group'=32,'pair'=2,'core'=2,'panel'=4] {'pair','panel'}, dimensions={0} | all-to-all | bytes 524288 | tf_op jit(solution)/shard_map/all_to_all | solution.py:391
  40.1 0.5 side_partials.1
  40.6 8.7 %all_to_all.43.received = bf16[8,128,128]{2,1,0:T(8,128)(2,1)S(1)} all-to-all(bf16[8,128,128]{2,1,0:T(8,128)(2,1)S(1)} %side_partials.1), channel_id=1, replica_groups=mesh['group'=32,'pair'=2,'core'=2,'panel'=4] {'pair','panel'}, dimensions={0} | all-to-all | bytes 524288 | tf_op jit(solution)/shard_map/all_to_all | solution.py:391
  49.3 0.1 turned_sum.1
  49.4 8.7 %all_to_all.44.whole = bf16[8,128,128]{2,1,0:T(8,128)(2,1)S(1)} all-to-all(bf16[8,128,128]{2,1,0:T(8,128)(2,1)S(1)} %turned_sum.1), channel_id=1, replica_groups=mesh['group'=32,'pair'=2,'core'=2,'panel'=4] {'pair','panel'}, dimensions={0} | all-to-all | bytes 524288 | tf_op jit(solution)/shard_map/all_to_all | solution.py:391
  58.1 0.3 back_step.3
  58.5 8.5 %all_to_all.45.whole.mine = bf16[8,128,128]{2,1,0:T(8,128)(2,1)S(1)} all-to-all(bf16[8,128,128]{2,1,0:T(8,128)(2,1)S(1)} %back_step.3), channel_id=1, replica_groups=mesh['group'=32,'pair'=2,'core'=2,'panel'=4] {'pair','panel'}, dimensions={0} | all-to-all | bytes 524288 | tf_op jit(solution)/shard_map/all_to_all | solution.py:391
  66.9 0.3 back_step.4
  67.3 7.5 %collective-permute-start.1 = (bf16[8,128,128]{2,1,0:T(8,128)(2,1)S(1)}, bf16[8,128,128]{2,1,0:T(8,128)(2,1)S(1)}, u32[]{:S(2)}, u32[]{:S(2)}) collective-permute-start(bf16[8,128,128]{2,1,0:T(8,128)(2,1)S(1)} %all_to_all.45.whole.mine), channel_id=1, source_target_pairs={{0,4},{4,0},{1,5},{5,1},{2,6},{6,2},{3,7},{7,3},{8,12},{12,8},{9,1... | collective-permute-start | bytes 786440 | tf_op jit(solution)/shard_map/ppermute | solution.py:395
  74.8 7.5 %all_to_all.46.whole = bf16[4,128,128]{2,1,0:T(8,128)(2,1)S(1)} all-to-all(bf16[4,128,128]{2,1,0:T(8,128)(2,1)S(1)} %back_step.4), channel_id=1, replica_groups=mesh['group'=32,'pair'=2,'core'=2,'panel'=4] {'panel'}, dimensions={0} | all-to-all | bytes 262144 | tf_op jit(solution)/shard_map/all_to_all | solution.py:391
  82.3 0.0 copy-start
  82.3 0.2 back_step.5
  82.5 0.0 collective-permute-done.1.other
  82.5 10.1 %all_to_all.47.whole = bf16[8,128,128]{2,1,0:T(8,128)(2,1)S(1)} all-to-all(bf16[8,128,128]{2,1,0:T(8,128)(2,1)S(1)} %back_step.5), channel_id=1, replica_groups=mesh['group'=32,'pair'=2,'core'=2,'panel'=4] {'core','panel'}, dimensions={0} | all-to-all | bytes 524288 | tf_op jit(solution)/shard_map/all_to_all | solution.py:391
  92.6 0.0 copy-done
  92.6 1.8 %leaf_backward.1 = (bf16[2,128,128]{2,1,0:T(8,128)(2,1)}, bf16[128,128]{1,0:T(8,128)(2,1)}, bf16[128,128]{1,0:T(8,128)(2,1)}) custom-call(s32[2,6]{1,0:T(2,128)S(1)} %bitcast.13, s32[1,1]{1,0:T(1,128)S(6)} %copy.13.count, bf16[8,128,128]{2,1,0:T(8,128)(2,1)S(1)} %all_to_all.47.whole, bf16[8,128,128]{2,1,0:T(8,128)(2,1)S(1)} %all_to_all.45.whole.mine, ...), custom_call_target="tpu_custom_call" | custom-call | tf_op jit(solution)/shard_map/leaf_backward/pallas_call | solution.py:375
Async XLA Ops:
  3.2 27.9 %collective-permute-start = (bf16[8192,128]{1,0:T(8,128)(2,1)S(1)}, bf16[8192,128]{1,0:T(8,128)(2,1)S(1)}, u32[]{:S(2)}, u32[]{:S(2)}) collective-permute-start(bf16[8192,128]{1,0:T(8,128)(2,1)S(1)} %get-tuple-element.15.mine.store), channel_id=1, source_target_pairs={{0,4},{4,0},{1,5},{5,1},{2,6},{6,2},{3,7},{7,3},{8,12},{12,8},{9,1... | collective-permute-start | bytes 6291464 | tf_op jit(solution)/shard_map/ppermute | solution.py:395
  67.3 15.3 %collective-permute-start.1 = (bf16[8,128,128]{2,1,0:T(8,128)(2,1)S(1)}, bf16[8,128,128]{2,1,0:T(8,128)(2,1)S(1)}, u32[]{:S(2)}, u32[]{:S(2)}) collective-permute-start(bf16[8,128,128]{2,1,0:T(8,128)(2,1)S(1)} %all_to_all.45.whole.mine), channel_id=1, source_target_pairs={{0,4},{4,0},{1,5},{5,1},{2,6},{6,2},{3,7},{7,3},{8,12},{12,8},{9,1... | collective-permute-start | bytes 786440 | tf_op jit(solution)/shard_map/ppermute | solution.py:395
  82.3 10.3 %copy-start = (s32[1,1,2,6]{3,2,1,0:T(2,128)S(1)}, s32[1,1,2,6]{3,2,1,0:T(2,128)}, u32[]{:S(2)}) copy-start(s32[1,1,2,6]{3,2,1,0:T(2,128)} %param.13) | copy-start | bytes 148

commit v10 on v6

--- a/solution.py
+++ b/solution.py
@@ -105,16 +105,16 @@
             (side1, side1_v),
             (side2, side2_v),
         )
-        core = lax.axis_index("core")
-        total[...] = jnp.zeros_like(total)
-        loads[0].wait()
-        loads[1].wait()
         matrices = start_loads(
             more_sems,
             (inverse1, store.at[part("inverse1", of=inverse1)]),
             (panel1, store.at[part("panel1", of=panel1)]),
             (inverse2, store.at[part("inverse2", of=inverse2)]),
         )
+        core = lax.axis_index("core")
+        total[...] = jnp.zeros_like(total)
+        loads[0].wait()
+        loads[1].wait()
         solved = []
         for s in range(slots):
             live = jnp.where(s < count[0, 0], 1.0, 0.0)

time: 93.8 us -> 93.5 us (level)
  no operation moved by 1% of the time
where the time goes in v10:
time: 93.5 us; the launch traced here: 93 us
  blocking collectives  67.9 us (73%)
  starting transfers between devices  17.6 us (19%)
  Pallas kernels  6.15 us (7%)
  between operations  1.36 us (1%)
    all_to_all x8, blocking collectives, exchange(): return lax.all_to_all(blocks, axes, 0, 0, tiled=True)  67.9 us
    ppermute x2, starting transfers between devices, swapped(): return lax.ppermute(array, 'core', [(0, 1), (1, 0)])  17.6 us
    pallas_call x1, Pallas kernels, leaf_forward(): pl.pallas_call(kernel, out_shape=(jax.ShapeDtypeStruct((first_blocks,) +...  1.92 us
  transfers between devices with their start and end apart: 2, of which 0 were waited for; matrix products, arithmetic and copies ran while one was open for 0% of the time, Pallas kernels for 0%

profile of v10, /device:TPU:1, one launch (start us, length us, event | category | flops | bytes accessed | tf_op | source)
XLA Modules:
  0.0 93.0 jit_solution(10595887242362299206)
XLA Ops:
  1.3 1.9 %leaf_forward.1 = (bf16[8,128,128]{2,1,0:T(8,128)(2,1)S(1)}, bf16[8192,128]{1,0:T(8,128)(2,1)S(1)}, f32[8,128,128]{2,1,0:T(8,128)S(1)}) custom-call(s32[2,6]{1,0:T(2,128)} %bitcast.12, s32[1,1]{1,0:T(1,128)S(6)} %copy.13.count, bf16[2,128,128]{2,1,0:T(8,128)(2,1)} %bitcast.18, bf16[256,128]{1,0:T(8,128)(2,1)} %bitcast.19, bf16[1536,128]{1,0:T(8,128)(2,1)} %bitcast.16, ...), custom_call_target="tpu_custom_call" | custom-call | tf_op jit(solution)/shard_map/leaf_forward/pallas_call | solution.py:163
  3.2 8.8 %collective-permute-start = (bf16[8192,128]{1,0:T(8,128)(2,1)S(1)}, bf16[8192,128]{1,0:T(8,128)(2,1)S(1)}, u32[]{:S(2)}, u32[]{:S(2)}) collective-permute-start(bf16[8192,128]{1,0:T(8,128)(2,1)S(1)} %get-tuple-element.15.mine.store), channel_id=1, source_target_pairs={{0,4},{4,0},{1,5},{5,1},{2,6},{6,2},{3,7},{7,3},{8,12},{12,8},{9,1... | collective-permute-start | bytes 6291464 | tf_op jit(solution)/shard_map/ppermute | solution.py:374
  12.0 9.0 %all_to_all.40.received = bf16[8,128,128]{2,1,0:T(8,128)(2,1)S(1)} all-to-all(bf16[8,128,128]{2,1,0:T(8,128)(2,1)S(1)} %get-tuple-element.14), channel_id=1, replica_groups=mesh['group'=32,'pair'=2,'core'=2,'panel'=4] {'core','panel'}, dimensions={0} | all-to-all | bytes 524288 | tf_op jit(solution)/shard_map/all_to_all | solution.py:370
  21.0 0.0 collective-permute-done.other
  21.0 0.4 side_partials.2
  21.4 7.2 %all_to_all.41.received = bf16[4,128,128]{2,1,0:T(8,128)(2,1)S(1)} all-to-all(bf16[4,128,128]{2,1,0:T(8,128)(2,1)S(1)} %side_partials.2), channel_id=1, replica_groups=mesh['group'=32,'pair'=2,'core'=2,'panel'=4] {'panel'}, dimensions={0} | all-to-all | bytes 262144 | tf_op jit(solution)/shard_map/all_to_all | solution.py:370
  28.6 0.5 raise_terms.1
  29.1 8.5 %all_to_all.42.received = bf16[8,128,128]{2,1,0:T(8,128)(2,1)S(1)} all-to-all(bf16[8,128,128]{2,1,0:T(8,128)(2,1)S(1)} %get-tuple-element.17), channel_id=1, replica_groups=mesh['group'=32,'pair'=2,'core'=2,'panel'=4] {'pair','panel'}, dimensions={0} | all-to-all | bytes 524288 | tf_op jit(solution)/shard_map/all_to_all | solution.py:370
  37.6 0.5 side_partials.3
  38.1 8.7 %all_to_all.43.received = bf16[8,128,128]{2,1,0:T(8,128)(2,1)S(1)} all-to-all(bf16[8,128,128]{2,1,0:T(8,128)(2,1)S(1)} %side_partials.3), channel_id=1, replica_groups=mesh['group'=32,'pair'=2,'core'=2,'panel'=4] {'pair','panel'}, dimensions={0} | all-to-all | bytes 524288 | tf_op jit(solution)/shard_map/all_to_all | solution.py:370
  46.8 0.1 turned_sum.1
  46.9 8.5 %all_to_all.44.whole = bf16[8,128,128]{2,1,0:T(8,128)(2,1)S(1)} all-to-all(bf16[8,128,128]{2,1,0:T(8,128)(2,1)S(1)} %turned_sum.1), channel_id=1, replica_groups=mesh['group'=32,'pair'=2,'core'=2,'panel'=4] {'pair','panel'}, dimensions={0} | all-to-all | bytes 524288 | tf_op jit(solution)/shard_map/all_to_all | solution.py:370
  55.4 0.3 back_step.3
  55.7 8.5 %all_to_all.45.whole.mine = bf16[8,128,128]{2,1,0:T(8,128)(2,1)S(1)} all-to-all(bf16[8,128,128]{2,1,0:T(8,128)(2,1)S(1)} %back_step.3), channel_id=1, replica_groups=mesh['group'=32,'pair'=2,'core'=2,'panel'=4] {'pair','panel'}, dimensions={0} | all-to-all | bytes 524288 | tf_op jit(solution)/shard_map/all_to_all | solution.py:370
  64.2 0.3 back_step.4
  64.6 8.8 %collective-permute-start.1 = (bf16[8,128,128]{2,1,0:T(8,128)(2,1)S(1)}, bf16[8,128,128]{2,1,0:T(8,128)(2,1)S(1)}, u32[]{:S(2)}, u32[]{:S(2)}) collective-permute-start(bf16[8,128,128]{2,1,0:T(8,128)(2,1)S(1)} %all_to_all.45.whole.mine), channel_id=1, source_target_pairs={{0,4},{4,0},{1,5},{5,1},{2,6},{6,2},{3,7},{7,3},{8,12},{12,8},{9,1... | collective-permute-start | bytes 786440 | tf_op jit(solution)/shard_map/ppermute | solution.py:374
  73.4 7.5 %all_to_all.46.whole = bf16[4,128,128]{2,1,0:T(8,128)(2,1)S(1)} all-to-all(bf16[4,128,128]{2,1,0:T(8,128)(2,1)S(1)} %back_step.4), channel_id=1, replica_groups=mesh['group'=32,'pair'=2,'core'=2,'panel'=4] {'panel'}, dimensions={0} | all-to-all | bytes 262144 | tf_op jit(solution)/shard_map/all_to_all | solution.py:370
  80.9 0.0 copy-start
  80.9 0.0 collective-permute-done.1.other
  80.9 0.2 back_step.5
  81.1 10.1 %all_to_all.47.whole = bf16[8,128,128]{2,1,0:T(8,128)(2,1)S(1)} all-to-all(bf16[8,128,128]{2,1,0:T(8,128)(2,1)S(1)} %back_step.5), channel_id=1, replica_groups=mesh['group'=32,'pair'=2,'core'=2,'panel'=4] {'core','panel'}, dimensions={0} | all-to-all | bytes 524288 | tf_op jit(solution)/shard_map/all_to_all | solution.py:370
  91.2 0.0 copy-done
  91.2 1.8 %leaf_backward.1 = (bf16[2,128,128]{2,1,0:T(8,128)(2,1)}, bf16[128,128]{1,0:T(8,128)(2,1)}, bf16[128,128]{1,0:T(8,128)(2,1)}) custom-call(s32[2,6]{1,0:T(2,128)S(1)} %bitcast.13, s32[1,1]{1,0:T(1,128)S(6)} %copy.13.count, bf16[8,128,128]{2,1,0:T(8,128)(2,1)S(1)} %all_to_all.47.whole, bf16[8,128,128]{2,1,0:T(8,128)(2,1)S(1)} %all_to_all.45.whole.mine, ...), custom_call_target="tpu_custom_call" | custom-call | tf_op jit(solution)/shard_map/leaf_backward/pallas_call | solution.py:354
Async XLA Ops:
  3.2 17.8 %collective-permute-start = (bf16[8192,128]{1,0:T(8,128)(2,1)S(1)}, bf16[8192,128]{1,0:T(8,128)(2,1)S(1)}, u32[]{:S(2)}, u32[]{:S(2)}) collective-permute-start(bf16[8192,128]{1,0:T(8,128)(2,1)S(1)} %get-tuple-element.15.mine.store), channel_id=1, source_target_pairs={{0,4},{4,0},{1,5},{5,1},{2,6},{6,2},{3,7},{7,3},{8,12},{12,8},{9,1... | collective-permute-start | bytes 6291464 | tf_op jit(solution)/shard_map/ppermute | solution.py:374
  64.6 16.3 %collective-permute-start.1 = (bf16[8,128,128]{2,1,0:T(8,128)(2,1)S(1)}, bf16[8,128,128]{2,1,0:T(8,128)(2,1)S(1)}, u32[]{:S(2)}, u32[]{:S(2)}) collective-permute-start(bf16[8,128,128]{2,1,0:T(8,128)(2,1)S(1)} %all_to_all.45.whole.mine), channel_id=1, source_target_pairs={{0,4},{4,0},{1,5},{5,1},{2,6},{6,2},{3,7},{7,3},{8,12},{12,8},{9,1... | collective-permute-start | bytes 786440 | tf_op jit(solution)/shard_map/ppermute | solution.py:374
  80.9 10.3 %copy-start = (s32[1,1,2,6]{3,2,1,0:T(2,128)S(1)}, s32[1,1,2,6]{3,2,1,0:T(2,128)}, u32[]{:S(2)}) copy-start(s32[1,1,2,6]{3,2,1,0:T(2,128)} %param.13) | copy-start | bytes 148
